TPU v7x, 32 devices: a whole 2x2x4 slice. The times are simulated.
32 devices in a mesh: section: 2 (over x), dp: 16 (over z, y, core).
Axes of the slice: x: 2, y: 2, z: 4, core: 2. Of those that a mesh axis runs over, the one named last changes fastest.
Arguments:
- tokens: bfloat16 [16384, 768], P('dp'), may hold values from -6 to 6
- segments: int32 [32, 512], P('dp'), may hold values from 0 to 7, never falling along the last dimension, each value on 1 to 256 neighbouring positions
- lengths: int32 [32], P('dp'), may hold values from 256 to 512
- cotangent: bfloat16 [16384, 768], P('dp'), may hold values from -6 to 6
- qkv_weight: bfloat16 [2, 768, 2304], P('section'), may hold values from -0.21875 to 0.21875
- qv_bias: float32 [2, 2, 768], P('section'), may hold values from -2 to 2
- out_weight: bfloat16 [2, 768, 768], P('section'), may hold values from -0.875 to 0.875
- out_biases: float32 [2, 2, 768], P('section'), may hold values from -2 to 2
- norm_gains: float32 [2, 2, 768], P('section'), may hold values from 0.5 to 1.5
- norm_shifts: float32 [2, 2, 768], P('section'), may hold values from -2 to 2
- up_weight: bfloat16 [2, 768, 3072], P('section'), may hold values from -0.21875 to 0.21875
- up_bias: float32 [2, 3072], P('section'), may hold values from -2 to 2
- down_weight: bfloat16 [2, 3072, 768], P('section'), may hold values from -0.109375 to 0.109375
Outputs:
- activations: bfloat16 [2, 16384, 768], P('section', 'dp')
- input_grads: bfloat16 [2, 16384, 768], P('section', 'dp')
- grad_qkv_weight: float32 [2, 768, 2304], P('section')
- grad_qv_bias: float32 [2, 2, 768], P('section')
- grad_out_weight: float32 [2, 768, 768], P('section')
- grad_out_biases: float32 [2, 2, 768], P('section')
- grad_norm_gains: float32 [2, 2, 768], P('section')
- grad_norm_shifts: float32 [2, 2, 768], P('section')
- grad_up_weight: float32 [2, 768, 3072], P('section')
- grad_up_bias: float32 [2, 3072], P('section')
- grad_down_weight: float32 [2, 3072, 768], P('section')
Inputs may be any that keep to these rules, and one draw needn't show every extreme that they name: `segments`: segment numbers never fall along a sequence. Positions at or beyond a sequence's lengths entry are padding, seen as keys only by themselves.
All inputs are finite; a program needn't handle non-finite values.
Results may differ from a plain program's by a relative error of at most 0.018.
Values may be sent and summed in bfloat16 or wider, within the bound.
A program may use at most 256 MiB of HBM per device.

v0:
```python
import math

import jax
import jax.numpy as jnp
from jax import lax
from jax.sharding import PartitionSpec as P

D = 768
H = 12
HD = 64
SEQ = 512
MICRO = 2
SEQ_MB = 1


EPSILON = 1e-05
SCORE_SCALE = 0.125
NEG_FILL = -1e30


def passed_along(value, axis, steps):
    count = lax.axis_size(axis)
    initial, last = (max(0, -steps), min(count, count - steps))
    return lax.ppermute(value, axis, [(source, source + steps) for source in range(initial, last)])


def contract_rows(left, right):
    return lax.dot_general(
        left, right, (((0,), (0,)), ((), ())), preferred_element_type=jnp.float32
    )


def times_weight(left, weight):
    return lax.dot_general(
        left, weight, (((1,), (1,)), ((), ())), preferred_element_type=jnp.float32
    )


def gelu_slope(up_pre):
    normal_cdf = 0.5 * (1.0 + lax.erf(up_pre * (1.0 / math.sqrt(2.0))))
    density = jnp.exp(-0.5 * up_pre * up_pre) * (1.0 / math.sqrt(2.0 * math.pi))
    return normal_cdf + up_pre * density


def norm_forward(resid, gain, shift):
    average = jnp.mean(resid, axis=-1, keepdims=True)
    centred = resid - average
    variance = jnp.mean(centred * centred, axis=-1, keepdims=True)
    inverse = lax.rsqrt(variance + EPSILON)
    scaled = centred * inverse
    return (scaled * gain + shift, scaled, inverse)


def norm_backward(grad_out, scaled, inverse, gain):
    weighted = grad_out * gain
    first_mean = jnp.mean(weighted, axis=-1, keepdims=True)
    second_mean = jnp.mean(weighted * scaled, axis=-1, keepdims=True)
    grad_in = inverse * (weighted - first_mean - scaled * second_mean)
    return (grad_in, jnp.sum(grad_out * scaled, axis=0), jnp.sum(grad_out, axis=0))


def allowed_mask(seg_row, seq_length):
    position = jnp.arange(seg_row.shape[0])
    key_valid = position[None, :] < seq_length
    same_doc = seg_row[:, None] == seg_row[None, :]
    return same_doc & (key_valid | (position[:, None] == position[None, :]))


def split_heads(qkv_seq):
    heads_all = qkv_seq.reshape(qkv_seq.shape[0], 3, H, HD)
    return (heads_all[:, 0], heads_all[:, 1], heads_all[:, 2])


def raw_scores(queries, keys_head, allowed):
    scores = (
        jnp.einsum("qhd,khd->hqk", queries, keys_head, preferred_element_type=jnp.float32)
        * SCORE_SCALE
    )
    return jnp.where(allowed[None], scores, NEG_FILL)


def attend_one(pieces):
    qkv_seq, seg_row, seq_length = pieces
    queries, keys_head, values = split_heads(qkv_seq)
    allowed = allowed_mask(seg_row, seq_length)
    scores = raw_scores(queries, keys_head, allowed)
    row_peak = jnp.max(scores, axis=-1, keepdims=True)
    exp_vals = jnp.exp(scores - row_peak)
    row_total = jnp.sum(exp_vals, axis=-1, keepdims=True)
    prob_low = (exp_vals / row_total).astype(jnp.bfloat16)
    context = jnp.einsum("hqk,khd->qhd", prob_low, values, preferred_element_type=jnp.float32)
    return (context.reshape(qkv_seq.shape[0], D), (row_peak + jnp.log(row_total))[..., 0])


def attend_back(pieces):
    qkv_seq, seg_row, seq_length, log_total, grad_context = pieces
    queries, keys_head, values = split_heads(qkv_seq)
    allowed = allowed_mask(seg_row, seq_length)
    scores = raw_scores(queries, keys_head, allowed)
    prob_full = jnp.where(allowed[None], jnp.exp(scores - log_total[..., None]), 0.0)
    prob_low = prob_full.astype(jnp.bfloat16)
    grad_heads = grad_context.reshape(qkv_seq.shape[0], H, HD)
    grad_prob = jnp.einsum("qhd,khd->hqk", grad_heads, values, preferred_element_type=jnp.float32)
    grad_values = jnp.einsum(
        "hqk,qhd->khd", prob_low, grad_heads, preferred_element_type=jnp.float32
    )
    row_inner = jnp.sum(prob_full * grad_prob, axis=-1, keepdims=True)
    grad_scores = (prob_full * (grad_prob - row_inner)).astype(jnp.bfloat16)
    grad_queries = (
        jnp.einsum("hqk,khd->qhd", grad_scores, keys_head, preferred_element_type=jnp.float32)
        * SCORE_SCALE
    )
    grad_keys = (
        jnp.einsum("hqk,qhd->khd", grad_scores, queries, preferred_element_type=jnp.float32)
        * SCORE_SCALE
    )
    return jnp.stack([grad_queries, grad_keys, grad_values], axis=1).reshape(
        qkv_seq.shape[0], 3 * D
    )


def layer_forward(hidden, seg_rows, len_rows, weights):
    (
        qkv_weight,
        qv_bias,
        out_weight,
        out_biases,
        gain_rows,
        shift_rows,
        up_weight,
        up_bias,
        down_weight,
    ) = weights
    bias_full = jnp.concatenate([qv_bias[0], jnp.zeros((D,), jnp.float32), qv_bias[1]])
    qkv_proj = (jnp.dot(hidden, qkv_weight, preferred_element_type=jnp.float32) + bias_full).astype(
        jnp.bfloat16
    )
    context, log_total = lax.map(attend_one, (qkv_proj.reshape(-1, SEQ, 3 * D), seg_rows, len_rows))
    context = context.reshape(-1, D).astype(jnp.bfloat16)
    attn_out = jnp.dot(context, out_weight, preferred_element_type=jnp.float32) + out_biases[0]
    normed, scaled_one, inverse_one = norm_forward(
        hidden.astype(jnp.float32) + attn_out, gain_rows[0], shift_rows[0]
    )
    normed_low = normed.astype(jnp.bfloat16)
    up_pre = jnp.dot(normed_low, up_weight, preferred_element_type=jnp.float32) + up_bias
    gelu_low = jax.nn.gelu(up_pre, approximate=False).astype(jnp.bfloat16)
    down_out = jnp.dot(gelu_low, down_weight, preferred_element_type=jnp.float32) + out_biases[1]
    result, scaled_two, inverse_two = norm_forward(normed + down_out, gain_rows[1], shift_rows[1])
    saved = (
        qkv_proj,
        context,
        log_total,
        scaled_one,
        inverse_one,
        normed_low,
        up_pre,
        gelu_low,
        scaled_two,
        inverse_two,
    )
    return (result, saved)


def layer_backward(hidden, seg_rows, len_rows, weights, grad_out):
    (
        qkv_weight,
        qv_bias,
        out_weight,
        out_biases,
        gain_rows,
        shift_rows,
        up_weight,
        up_bias,
        down_weight,
    ) = weights
    unused_out, saved = layer_forward(hidden, seg_rows, len_rows, weights)
    (
        qkv_proj,
        context,
        log_total,
        scaled_one,
        inverse_one,
        normed_low,
        up_pre,
        gelu_low,
        scaled_two,
        inverse_two,
    ) = saved
    grad_resid_two, grad_gain_two, grad_shift_two = norm_backward(
        grad_out, scaled_two, inverse_two, gain_rows[1]
    )
    grad_down = grad_resid_two.astype(jnp.bfloat16)
    grad_down_weight = contract_rows(gelu_low, grad_down)
    grad_up = (times_weight(grad_down, down_weight) * gelu_slope(up_pre)).astype(jnp.bfloat16)
    grad_up_weight = contract_rows(normed_low, grad_up)
    grad_normed = grad_resid_two + times_weight(grad_up, up_weight)
    grad_resid_one, grad_gain_one, grad_shift_one = norm_backward(
        grad_normed, scaled_one, inverse_one, gain_rows[0]
    )
    grad_attn = grad_resid_one.astype(jnp.bfloat16)
    grad_out_weight = contract_rows(context, grad_attn)
    grad_context = times_weight(grad_attn, out_weight).astype(jnp.bfloat16)
    grad_qkv = lax.map(
        attend_back,
        (
            qkv_proj.reshape(-1, SEQ, 3 * D),
            seg_rows,
            len_rows,
            log_total,
            grad_context.reshape(-1, SEQ, D),
        ),
    )
    grad_qkv = grad_qkv.reshape(-1, 3 * D).astype(jnp.bfloat16)
    grad_qkv_weight = contract_rows(hidden, grad_qkv)
    grad_hidden = grad_resid_one + times_weight(grad_qkv, qkv_weight)
    bias_sums = jnp.sum(grad_qkv, axis=0, dtype=jnp.float32)
    grad_qv_bias = jnp.stack([bias_sums[:D], bias_sums[2 * D :]])
    grad_out_biases = jnp.stack(
        [
            jnp.sum(grad_attn, axis=0, dtype=jnp.float32),
            jnp.sum(grad_down, axis=0, dtype=jnp.float32),
        ]
    )
    grad_gain_rows = jnp.stack([grad_gain_one, grad_gain_two])
    grad_shift_rows = jnp.stack([grad_shift_one, grad_shift_two])
    grad_up_bias = jnp.sum(grad_up, axis=0, dtype=jnp.float32)
    return (
        grad_hidden,
        (
            grad_qkv_weight,
            grad_qv_bias,
            grad_out_weight,
            grad_out_biases,
            grad_gain_rows,
            grad_shift_rows,
            grad_up_weight,
            grad_up_bias,
            grad_down_weight,
        ),
    )


def shards(
    tokens,
    segments,
    lengths,
    cotangent,
    qkv_weight,
    qv_bias,
    out_weight,
    out_biases,
    norm_gains,
    norm_shifts,
    up_weight,
    up_bias,
    down_weight,
):
    weights = tuple(
        (
            weight[0]
            for weight in (
                qkv_weight,
                qv_bias,
                out_weight,
                out_biases,
                norm_gains,
                norm_shifts,
                up_weight,
                up_bias,
                down_weight,
            )
        )
    )
    is_first = lax.axis_index("section") == 0
    row_count = SEQ_MB * SEQ
    input_blocks = tokens.reshape(MICRO, row_count, D)
    upstream_blocks = cotangent.reshape(MICRO, row_count, D)
    seg_blocks = segments.reshape(MICRO, SEQ_MB, SEQ)
    len_blocks = lengths.reshape(MICRO, SEQ_MB)
    received = jnp.zeros((row_count, D), jnp.bfloat16)
    stored = []
    produced = []
    for moment in range(MICRO + 1):
        early_index = min(moment, MICRO - 1)
        late_index = max(moment - 1, 0)
        hidden = jnp.where(is_first, input_blocks[early_index], received)
        seg_rows = jnp.where(is_first, seg_blocks[early_index], seg_blocks[late_index])
        len_rows = jnp.where(is_first, len_blocks[early_index], len_blocks[late_index])
        result, unused_saved = layer_forward(hidden, seg_rows, len_rows, weights)
        result_low = result.astype(jnp.bfloat16)
        stored.append(hidden)
        produced.append(result_low)
        if moment < MICRO:
            received = passed_along(result_low, "section", 1)
    block_inputs = [
        jnp.where(is_first, stored[index_mb], stored[index_mb + 1]) for index_mb in range(MICRO)
    ]
    outputs_mb = [
        jnp.where(is_first, produced[index_mb], produced[index_mb + 1]) for index_mb in range(MICRO)
    ]
    returning = jnp.zeros((row_count, D), jnp.bfloat16)
    grad_rows = []
    totals = None
    for moment in range(MICRO + 1):
        late_index = min(moment, MICRO - 1)
        early_index = max(moment - 1, 0)
        hidden = jnp.where(is_first, block_inputs[early_index], block_inputs[late_index])
        seg_rows = jnp.where(is_first, seg_blocks[early_index], seg_blocks[late_index])
        len_rows = jnp.where(is_first, len_blocks[early_index], len_blocks[late_index])
        if moment < MICRO:
            upstream_rows = upstream_blocks[late_index].astype(jnp.float32)
        else:
            upstream_rows = jnp.zeros((row_count, D), jnp.float32)
        grad_out = jnp.where(is_first, returning.astype(jnp.float32), upstream_rows)
        grad_hidden, step_grads = layer_backward(hidden, seg_rows, len_rows, weights, grad_out)
        grad_low = grad_hidden.astype(jnp.bfloat16)
        grad_rows.append(grad_low)
        if moment < MICRO:
            returning = passed_along(grad_low, "section", -1)
        totals = (
            step_grads
            if totals is None
            else tuple((older + newer for older, newer in zip(totals, step_grads)))
        )
    shares = (
        lax.psum_scatter(totals[0], "dp", scatter_dimension=0, tiled=True),
        lax.psum_scatter(totals[1], "dp", scatter_dimension=1, tiled=True),
        lax.psum_scatter(totals[2], "dp", scatter_dimension=0, tiled=True),
        lax.psum_scatter(totals[3], "dp", scatter_dimension=1, tiled=True),
        lax.psum_scatter(totals[4], "dp", scatter_dimension=1, tiled=True),
        lax.psum_scatter(totals[5], "dp", scatter_dimension=1, tiled=True),
        lax.psum_scatter(totals[6], "dp", scatter_dimension=0, tiled=True),
        lax.psum_scatter(totals[7], "dp", scatter_dimension=0, tiled=True),
        lax.psum_scatter(totals[8], "dp", scatter_dimension=0, tiled=True),
    )
    copies = (
        lax.all_gather(shares[0].astype(jnp.bfloat16), "dp", axis=0, tiled=True).astype(
            jnp.float32
        ),
        lax.all_gather(shares[1].astype(jnp.bfloat16), "dp", axis=1, tiled=True).astype(
            jnp.float32
        ),
        lax.all_gather(shares[2].astype(jnp.bfloat16), "dp", axis=0, tiled=True).astype(
            jnp.float32
        ),
        lax.all_gather(shares[3].astype(jnp.bfloat16), "dp", axis=1, tiled=True).astype(
            jnp.float32
        ),
        lax.all_gather(shares[4].astype(jnp.bfloat16), "dp", axis=1, tiled=True).astype(
            jnp.float32
        ),
        lax.all_gather(shares[5].astype(jnp.bfloat16), "dp", axis=1, tiled=True).astype(
            jnp.float32
        ),
        lax.all_gather(shares[6].astype(jnp.bfloat16), "dp", axis=0, tiled=True).astype(
            jnp.float32
        ),
        lax.all_gather(shares[7].astype(jnp.bfloat16), "dp", axis=0, tiled=True).astype(
            jnp.float32
        ),
        lax.all_gather(shares[8].astype(jnp.bfloat16), "dp", axis=0, tiled=True).astype(
            jnp.float32
        ),
    )
    input_mb = [
        jnp.where(is_first, grad_rows[index_mb + 1], grad_rows[index_mb])
        for index_mb in range(MICRO)
    ]
    activations = jnp.stack(outputs_mb).reshape(1, MICRO * row_count, D)
    input_grads = jnp.stack(input_mb).reshape(1, MICRO * row_count, D)
    return (
        activations,
        input_grads,
        copies[0][None],
        copies[1][None],
        copies[2][None],
        copies[3][None],
        copies[4][None],
        copies[5][None],
        copies[6][None],
        copies[7][None],
        copies[8][None],
    )


def solution(mesh):
    return jax.shard_map(
        shards,
        mesh=mesh,
        in_specs=(
            P("dp", None),
            P("dp", None),
            P("dp"),
            P("dp", None),
            P("section", None, None),
            P("section", None, None),
            P("section", None, None),
            P("section", None, None),
            P("section", None, None),
            P("section", None, None),
            P("section", None, None),
            P("section", None),
            P("section", None, None),
        ),
        out_specs=(
            P("section", "dp", None),
            P("section", "dp", None),
            P("section", None, None),
            P("section", None, None),
            P("section", None, None),
            P("section", None, None),
            P("section", None, None),
            P("section", None, None),
            P("section", None, None),
            P("section", None),
            P("section", None, None),
        ),
        check_vma=False,
    )
```

profile of v0, /device:TPU:0, one launch (start us, length us, event | category | flops | bytes accessed | tf_op | source)
XLA Modules:
  0.0 1316.1 jit_solution(18395667929329744668)
XLA Ops:
  14.0 4.5 fusion.144
  23.8 11.2 fusion.552
  34.9 6.1 fusion.323
  44.1 23.7 %fusion.554 = (f32[512]{0:T(512)}, f32[512,768]{1,0:T(8,128)}) fusion(f32[768]{0:T(1024)} %get-tuple-element.181, bf16[1,3072,768]{2,1,0:T(8,128)(2,1)} %param.25, bf16[1,768,3072]{2,1,0:T(8,128)(2,1)} %param.23, f32[3072]{0:T(1024)} %bitcast.573, f32[512,768]{1,0:T(8,128)} %copy-done.60, f32[768]{0:T(1024)S(1)} %get-tuple-element.180, ...), kind=kOutput, calls=%fused_computation.751 | convolution fusion | flops 4940365312 | bytes 12610560 | tf_op jit(solution)/shard_map/dot_general | solution.py:147
  70.3 12.0 add_convert_fusion.5
  82.4 4.9 collective-permute-start
  90.3 13.7 %collective-permute-done = bf16[512,768]{1,0:T(8,128)(2,1)S(1)} collective-permute-done((bf16[512,768]{1,0:T(8,128)(2,1)S(1)}, bf16[512,768]{1,0:T(8,128)(2,1)S(1)}, u32[]{:S(2)}, u32[]{:S(2)}) %collective-permute-start) | collective-permute-done | bytes 786464 | tf_op jit(solution)/shard_map/ppermute | solution.py:24
  112.7 11.2 fusion.559
  123.9 6.1 fusion.322
  133.0 23.8 %fusion.561 = (f32[512]{0:T(512)}, f32[512,768]{1,0:T(8,128)}) fusion(f32[768]{0:T(1024)} %get-tuple-element.181, bf16[1,3072,768]{2,1,0:T(8,128)(2,1)} %param.25, bf16[1,768,3072]{2,1,0:T(8,128)(2,1)} %param.23, f32[3072]{0:T(1024)} %bitcast.574, f32[512,768]{1,0:T(8,128)} %copy-done.61, f32[512]{0:T(512)} %add_rsqrt_fusion.9, f32[512]{0:T(512)} %copy-done.127, ...), kind=kOutput, calls=%fused_computation.754 | convolution fusion | flops 4940365312 | bytes 12610560 | tf_op jit(solution)/shard_map/dot_general | solution.py:147
  162.9 4.4 collective-permute-start.1
  171.3 11.9 collective-permute-done.1
  201.5 5.6 fusion.325
  211.2 4.5 copy.125
  223.7 4.9 fusion.326
  231.6 7.3 fusion.136
  238.9 5.2 fusion.134
  259.9 4.9 fusion.324
  266.2 47.6 %fusion.41 = (bf16[512,3072]{1,0:T(8,128)(2,1)}, bf16[512,3072]{1,0:T(8,128)(2,1)}, bf16[512,3072]{1,0:T(8,128)(2,1)S(1)}, f32[512,3072]{1,0:T(8,128)}) fusion(f32[3072]{0:T(1024)S(1)} %bitcast.576, f32[512,3072]{1,0:T(8,128)} %fusion.136, f32[512,3072]{1,0:T(8,128)} %fusion.134, bf16[1,768,3072]{2,1,0:T(8,128)(2,1)} %param.23, ...), kind=kOutput, calls=%fused_computation.80 | convolution fusion | flops 2729312256 | bytes 34625536 | tf_op jit(solution)/shard_map/dot_general | solution.py:145
  319.6 5.3 convert_reduce_fusion.2
  334.9 9.2 fusion.273
  344.1 9.8 multiply_reduce_fusion.2
  353.9 7.2 multiply_convert_fusion.2
  380.3 5.0 fusion.579
  390.9 5.7 convert_reduce_fusion.1
  406.6 9.2 fusion.276
  415.8 9.8 multiply_reduce_fusion.1
  425.6 7.2 multiply_convert_fusion.1
  443.3 5.0 fusion.580
  448.3 10.0 collective-permute-done.3
  461.0 5.4 convert_reduce_fusion
  476.3 5.3 add_add_fusion.3
  481.7 12.2 multiply_reduce_fusion
  495.1 7.4 multiply_convert_fusion
  507.5 5.2 fusion.279
  516.4 8.0 add_add_fusion.2
  525.2 5.5 fusion.541
  530.8 5.8 fusion.544
  536.6 8.3 add_add_fusion.1
  545.0 5.2 fusion.424
  553.0 9.9 add_add_fusion
  603.2 36.0 %reduce-scatter.17.cloned.1.call-done = f32[48,2304]{1,0:T(8,128)} async-done(((f32[768,2304]{1,0:T(8,128)}), f32[48,2304]{1,0:T(8,128)}) %reduce-scatter.17.cloned.1.call-update) | async-done | bytes 442384 | tf_op jit(solution)/shard_map/reduce_scatter | solution.py:326
  641.0 113.8 %reduce-scatter.21.cloned.1.call-done = f32[48,3072]{1,0:T(8,128)} async-done(((f32[768,3072]{1,0:T(8,128)}), f32[48,3072]{1,0:T(8,128)}) %reduce-scatter.21.cloned.1.call-update) | async-done | bytes 589840 | tf_op jit(solution)/shard_map/reduce_scatter | solution.py:332
  759.3 4.5 fusion.146
  763.9 4.7 copy.123
  768.5 12.5 fusion.566
  781.1 6.4 fusion.321
  790.5 80.6 %reduce-scatter.23.cloned.1.call-done = f32[192,768]{1,0:T(8,128)} async-done(((f32[3072,768]{1,0:T(8,128)}), f32[192,768]{1,0:T(8,128)}) %reduce-scatter.23.cloned.1.call-update) | async-done | bytes 589840 | tf_op jit(solution)/shard_map/reduce_scatter | solution.py:334
  872.9 23.6 %fusion.568 = (f32[512]{0:T(512)}, f32[512,768]{1,0:T(8,128)}) fusion(f32[768]{0:T(1024)} %get-tuple-element.181, bf16[1,3072,768]{2,1,0:T(8,128)(2,1)} %param.25, bf16[1,768,3072]{2,1,0:T(8,128)(2,1)} %param.23, f32[3072]{0:T(1024)} %bitcast.575, f32[512,768]{1,0:T(8,128)} %copy-done.59, f32[512]{0:T(512)} %add_rsqrt_fusion.7, f32[512]{0:T(512)} %copy-done.125, ...), kind=kOutput, calls=%fused_computation.757 | convolution fusion | flops 4940365312 | bytes 12610560 | tf_op jit(solution)/shard_map/dot_general | solution.py:147
  903.7 60.3 %all-reduce.1 = bf16[3072]{0:T(1024)(128)(2,1)} all-reduce(f32[3072]{0:T(1024)S(1)} %add_add_fusion.16), channel_id=9, replica_groups=mesh['section'=2,'dp'=16] {'dp'}, use_global_device_ids=true, to_apply=%region_82.83.clone | all-reduce | flops 3072 | bytes 18432
  964.9 30.0 %all-reduce = bf16[3072]{0:T(1024)(128)(2,1)S(1)} all-reduce(bf16[3072]{0:T(1024)(128)(2,1)S(1)} %dynamic-update-slice), channel_id=1, replica_groups=mesh['section'=2,'dp'=16] {'dp'}, use_global_device_ids=true, to_apply=%add | all-reduce | flops 3072 | bytes 12288
  1001.9 17.0 %all-gather = bf16[16,48,2]{1,2,0:T(2,128)(2,1)S(1)} all-gather(bf16[1,48,2]{1,2,0:T(2,128)(2,1)S(1)} %bitcast.557), channel_id=1, replica_groups=mesh['section'=2,'dp'=16] {'dp'}, dimensions={0}, use_global_device_ids=true | all-gather | bytes 3264 | tf_op jit(solution)/shard_map/all_gather | solution.py:340
  1020.4 19.0 %all-gather.1 = bf16[16,48,2]{1,2,0:T(2,128)(2,1)S(1)} all-gather(bf16[1,48,2]{1,2,0:T(2,128)(2,1)S(1)} %bitcast.558), channel_id=1, replica_groups=mesh['section'=2,'dp'=16] {'dp'}, dimensions={0}, use_global_device_ids=true | all-gather | bytes 3264 | tf_op jit(solution)/shard_map/all_gather | solution.py:346
  1040.1 6.1 reduce-scatter.29.cloned.1.call-done
  1047.0 19.3 %all-gather.2 = bf16[16,48,2]{1,2,0:T(2,128)(2,1)S(1)} all-gather(bf16[1,48,2]{1,2,0:T(2,128)(2,1)S(1)} %bitcast.559), channel_id=1, replica_groups=mesh['section'=2,'dp'=16] {'dp'}, dimensions={0}, use_global_device_ids=true | all-gather | bytes 3264 | tf_op jit(solution)/shard_map/all_gather | solution.py:349
  1067.1 37.7 %reduce-scatter.31.cloned.1.call-done = f32[48,2]{1,0:T(8,128)} async-done(((f32[768,2]{1,0:T(8,128)}), f32[48,2]{1,0:T(8,128)}) %reduce-scatter.31.cloned.1.call-update) | async-done | bytes 400
  1105.6 19.3 %all-gather.3 = bf16[16,48,2]{1,2,0:T(2,128)(2,1)S(1)} all-gather(bf16[1,48,2]{1,2,0:T(2,128)(2,1)S(1)} %bitcast.560), channel_id=1, replica_groups=mesh['section'=2,'dp'=16] {'dp'}, dimensions={0}, use_global_device_ids=true | all-gather | bytes 3264 | tf_op jit(solution)/shard_map/all_gather | solution.py:352
  1125.6 18.9 %all-gather.11.cloned.1.call-done = bf16[768,768]{1,0:T(8,128)(2,1)} async-done(((bf16[48,768]{1,0:T(8,128)(2,1)}), bf16[768,768]{1,0:T(8,128)(2,1)}) %all-gather.11.cloned.1.call-update) | async-done | bytes 1179664 | tf_op jit(solution)/shard_map/all_gather | solution.py:343
  1147.3 45.5 %all-gather.9.cloned.1.call-done = bf16[768,2304]{1,0:T(8,128)(2,1)} async-done(((bf16[48,2304]{1,0:T(8,128)(2,1)}), bf16[768,2304]{1,0:T(8,128)(2,1)}) %all-gather.9.cloned.1.call-update) | async-done | bytes 3538960 | tf_op jit(solution)/shard_map/all_gather | solution.py:337
  1192.8 5.5 bitcast_convert_fusion.2
  1198.3 49.8 %all-gather.13.cloned.1.call-done = bf16[768,3072]{1,0:T(8,128)(2,1)} async-done(((bf16[48,3072]{1,0:T(8,128)(2,1)}), bf16[768,3072]{1,0:T(8,128)(2,1)}) %all-gather.13.cloned.1.call-update) | async-done | bytes 4718608 | tf_op jit(solution)/shard_map/all_gather | solution.py:355
  1248.1 7.4 bitcast_convert_fusion.1
  1255.5 46.7 %all-gather.15.cloned.1.call-done = bf16[3072,768]{1,0:T(8,128)(2,1)} async-done(((bf16[192,768]{1,0:T(8,128)(2,1)}), bf16[3072,768]{1,0:T(8,128)(2,1)}) %all-gather.15.cloned.1.call-update) | async-done | bytes 4718608 | tf_op jit(solution)/shard_map/all_gather | solution.py:361
  1302.2 6.8 bitcast_convert_fusion
  (592 shorter events, 249.4 us)
Async XLA Ops:
  7.2 594.4 %reduce-scatter.19.cloned.1.call-start = ((), (), s32[]{:S(2)}) async-start(), calls=%async_computation.10 | async-start | bytes 2506752 | tf_op jit(solution)/shard_map/reduce_scatter | solution.py:328
  8.7 32.3 %copy-start.132 = (f32[768]{0:T(1024)}, f32[768]{0:T(1024)S(1)}, u32[]{:S(2)}) copy-start(f32[768]{0:T(1024)S(1)} %get-tuple-element.188) | copy-start | bytes 9220
  44.1 23.7 %copy-start.105 = (f32[768]{0:T(1024)}, f32[768]{0:T(1024)S(1)}, u32[]{:S(2)}) copy-start(f32[768]{0:T(1024)S(1)} %get-tuple-element.180) | copy-start | bytes 9220
  44.1 115.2 %copy-start.76 = (f32[768]{0:T(1024)}, f32[768]{0:T(1024)S(1)}, u32[]{:S(2)}) copy-start(f32[768]{0:T(1024)S(1)} %get-tuple-element.299) | copy-start | bytes 9220
  44.1 115.2 %copy-start.90 = (f32[768]{0:T(1024)}, f32[768]{0:T(1024)S(1)}, u32[]{:S(2)}) copy-start(f32[768]{0:T(1024)S(1)} %get-tuple-element.179) | copy-start | bytes 9220
  67.8 36.2 %copy-start.35 = (bf16[1024,768]{1,0:T(8,128)(2,1)S(1)}, bf16[1024,768]{1,0:T(8,128)(2,1)}, u32[]{:S(2)}) copy-start(bf16[1024,768]{1,0:T(8,128)(2,1)} %param.13) | copy-start | bytes 4718596
  67.8 37.2 %copy-start.113 = (f32[2304]{0:T(1024)S(1)}, f32[2304]{0:T(1024)}, u32[]{:S(2)}) copy-start(f32[2304]{0:T(1024)} %copy-done.112) | copy-start | bytes 27652
  70.3 33.7 %copy-start.92 = (f32[512]{0:T(512)}, f32[512]{0:T(512)S(1)}, u32[]{:S(2)}) copy-start(f32[512]{0:T(512)S(1)} %add_rsqrt_fusion.10) | copy-start | bytes 6148
  82.4 21.6 %collective-permute-start = (bf16[512,768]{1,0:T(8,128)(2,1)S(1)}, bf16[512,768]{1,0:T(8,128)(2,1)S(1)}, u32[]{:S(2)}, u32[]{:S(2)}) collective-permute-start(bf16[512,768]{1,0:T(8,128)(2,1)S(1)} %add_convert_fusion.5), channel_id=1, source_target_pairs={{0,16},{1,17},{2,18},{3,19},{4,20},{5,21},{6,22},{7,23},{8,24},{9,... | collective-permute-start | bytes 2359304 | tf_op jit(solution)/shard_map/ppermute | solution.py:24
  156.8 12.5 copy-start.94
  156.8 13.5 %copy-start.93 = (s32[1,512]{1,0:T(1,128)S(1)}, s32[1,512]{1,0:T(1,128)}, u32[]{:S(2)}) copy-start(s32[1,512]{1,0:T(1,128)} %get-tuple-element.238) | copy-start | bytes 6148
  156.8 26.4 %copy-start.36 = (bf16[1024,768]{1,0:T(8,128)(2,1)S(1)}, bf16[1024,768]{1,0:T(8,128)(2,1)}, u32[]{:S(2)}) copy-start(bf16[1024,768]{1,0:T(8,128)(2,1)} %param.13) | copy-start | bytes 4718596
  156.8 26.4 %copy-start.53 = (bf16[512,768]{1,0:T(8,128)(2,1)S(1)}, bf16[512,768]{1,0:T(8,128)(2,1)}, u32[]{:S(2)}) copy-start(bf16[512,768]{1,0:T(8,128)(2,1)} %copy-done.51) | copy-start | bytes 2359300
  159.3 26.4 %copy-start.114 = (f32[2304]{0:T(1024)S(1)}, f32[2304]{0:T(1024)}, u32[]{:S(2)}) copy-start(f32[2304]{0:T(1024)} %copy-done.112) | copy-start | bytes 27652
  162.9 20.3 %collective-permute-start.1 = (bf16[512,768]{1,0:T(8,128)(2,1)S(1)}, bf16[512,768]{1,0:T(8,128)(2,1)S(1)}, u32[]{:S(2)}, u32[]{:S(2)}) collective-permute-start(bf16[512,768]{1,0:T(8,128)(2,1)S(1)} %get-tuple-element.228), channel_id=1, source_target_pairs={{0,16},{1,17},{2,18},{3,19},{4,20},{5,21},{6,22},{7,23},{8,24},{9,... | collective-permute-start | bytes 2359304 | tf_op jit(solution)/shard_map/ppermute | solution.py:24
  264.8 49.0 %copy-start.67 = (bf16[12,64,512]{2,1,0:T(8,128)(2,1)}, bf16[12,64,512]{2,1,0:T(8,128)(2,1)S(1)}, u32[]{:S(2)}) copy-start(bf16[12,64,512]{2,1,0:T(8,128)(2,1)S(1)} %fusion.324) | copy-start | bytes 2359300
  265.8 48.0 %copy-start.7 = (f32[512,768]{1,0:T(8,128)}, f32[512,768]{1,0:T(8,128)S(1)}, u32[]{:S(2)}) copy-start(f32[512,768]{1,0:T(8,128)S(1)} %get-tuple-element.267) | copy-start | bytes 4718596
  266.2 107.1 %copy-start.101 = (f32[512]{0:T(512)}, f32[512]{0:T(512)S(1)}, u32[]{:S(2)}) copy-start(f32[512]{0:T(512)S(1)} %add_rsqrt_fusion.1) | copy-start | bytes 6148
  266.2 47.7 %copy-start.25 = (f32[512,768]{1,0:T(8,128)S(1)}, f32[512,768]{1,0:T(8,128)}, u32[]{:S(2)}) copy-start(f32[512,768]{1,0:T(8,128)} %copy-done.24) | copy-start | bytes 4718596
  266.2 47.7 %copy-start.99 = (f32[512]{0:T(512)S(1)}, f32[512]{0:T(512)}, u32[]{:S(2)}) copy-start(f32[512]{0:T(512)} %copy-done.98) | copy-start | bytes 6148
  266.2 47.7 %copy-start.107 = (f32[768]{0:T(1024)S(1)}, f32[768]{0:T(1024)}, u32[]{:S(2)}) copy-start(f32[768]{0:T(1024)} %copy-done.105) | copy-start | bytes 9220
  266.2 47.7 %copy-start.124 = (f32[512]{0:T(512)S(1)}, f32[512]{0:T(512)}, u32[]{:S(2)}) copy-start(f32[512]{0:T(512)} %copy-done.123) | copy-start | bytes 6148
  266.2 47.7 %copy-start.130 = (f32[768]{0:T(1024)S(1)}, f32[768]{0:T(1024)}, u32[]{:S(2)}) copy-start(f32[768]{0:T(1024)} %get-tuple-element.181) | copy-start | bytes 9220
  266.2 47.7 %copy-start.137 = (bf16[1,3072,768]{2,1,0:T(8,128)(2,1)S(1)}, bf16[1,3072,768]{2,1,0:T(8,128)(2,1)}, u32[]{:S(2)}) copy-start(bf16[1,3072,768]{2,1,0:T(8,128)(2,1)} %param.25) | copy-start | bytes 14155780
  334.9 19.0 %slice-start.6 = ((s8[12582912]{0:T(1024)(128)(4,1)}), s8[4194304]{0:T(1024)(128)(4,1)S(1)}, s32[]{:S(2)}) async-start(s8[12582912]{0:T(1024)(128)(4,1)} %bitcast.495), calls=%async_computation.26 | async-start | bytes 8388608
  334.9 19.0 %slice-start.7 = ((s8[12582912]{0:T(1024)(128)(4,1)}), s8[4194304]{0:T(1024)(128)(4,1)S(1)}, s32[]{:S(2)}) async-start(s8[12582912]{0:T(1024)(128)(4,1)} %bitcast.495), calls=%async_computation.27 | async-start | bytes 8388608
  344.1 9.8 slice-start.8
  368.7 19.5 %collective-permute-start.2 = (bf16[512,768]{1,0:T(8,128)(2,1)S(1)}, bf16[512,768]{1,0:T(8,128)(2,1)S(1)}, u32[]{:S(2)}, u32[]{:S(2)}) collective-permute-start(bf16[512,768]{1,0:T(8,128)(2,1)S(1)} %add_convert_fusion.2), channel_id=1, source_target_pairs={{16,0},{17,1},{18,2},{19,3},{20,4},{21,5},{22,6},{23,7},{24,8},{25... | collective-permute-start | bytes 2359304 | tf_op jit(solution)/shard_map/ppermute | solution.py:24
  378.1 12.7 slice-start.23
  380.3 10.5 slice-start.24
  406.5 9.3 copy-start.75
  406.5 9.3 copy-start.89
  406.5 19.1 %slice-start.3 = ((s8[12582912]{0:T(1024)(128)(4,1)}), s8[4194304]{0:T(1024)(128)(4,1)S(1)}, s32[]{:S(2)}) async-start(s8[12582912]{0:T(1024)(128)(4,1)} %bitcast.493), calls=%async_computation.23 | async-start | bytes 8388608
  406.5 19.1 %slice-start.4 = ((s8[12582912]{0:T(1024)(128)(4,1)}), s8[4194304]{0:T(1024)(128)(4,1)S(1)}, s32[]{:S(2)}) async-start(s8[12582912]{0:T(1024)(128)(4,1)} %bitcast.493), calls=%async_computation.24 | async-start | bytes 8388608
  415.8 9.8 slice-start.5
  437.4 23.5 %slice-start.13 = ((s8[4718592]{0:T(1024)(128)(4,1)}), s8[4194304]{0:T(1024)(128)(4,1)S(1)}, s32[]{:S(2)}) async-start(s8[4718592]{0:T(1024)(128)(4,1)} %bitcast.563), calls=%async_computation.33 | async-start | bytes 8388608
  437.4 23.5 %slice-start.27 = ((s8[6291456]{0:T(1024)(128)(4,1)}), s8[4194304]{0:T(1024)(128)(4,1)S(1)}, s32[]{:S(2)}) async-start(s8[6291456]{0:T(1024)(128)(4,1)} %bitcast.587), calls=%async_computation.47 | async-start | bytes 8388608
  439.5 21.4 %slice-start.14 = ((s8[4718592]{0:T(1024)(128)(4,1)}), s8[524288]{0:T(1024)(128)(4,1)S(1)}, s32[]{:S(2)}) async-start(s8[4718592]{0:T(1024)(128)(4,1)} %bitcast.563), calls=%async_computation.34 | async-start | bytes 1048576
  439.5 21.4 %slice-start.28 = ((s8[6291456]{0:T(1024)(128)(4,1)}), s8[2097152]{0:T(1024)(128)(4,1)S(1)}, s32[]{:S(2)}) async-start(s8[6291456]{0:T(1024)(128)(4,1)} %bitcast.587), calls=%async_computation.48 | async-start | bytes 4194304
  439.5 18.8 %collective-permute-start.3 = (bf16[512,768]{1,0:T(8,128)(2,1)S(1)}, bf16[512,768]{1,0:T(8,128)(2,1)S(1)}, u32[]{:S(2)}, u32[]{:S(2)}) collective-permute-start(bf16[512,768]{1,0:T(8,128)(2,1)S(1)} %add_convert_fusion.1), channel_id=1, source_target_pairs={{16,0},{17,1},{18,2},{19,3},{20,4},{21,5},{22,6},{23,7},{24,8},{25... | collective-permute-start | bytes 2359304 | tf_op jit(solution)/shard_map/ppermute | solution.py:24
  443.3 15.0 %copy-start.12 = (f32[512,768]{1,0:T(8,128)S(1)}, f32[512,768]{1,0:T(8,128)}, u32[]{:S(2)}) copy-start(f32[512,768]{1,0:T(8,128)} %copy-done.11) | copy-start | bytes 4718596
  443.3 15.0 %copy-start.104 = (f32[512]{0:T(512)S(1)}, f32[512]{0:T(512)}, u32[]{:S(2)}) copy-start(f32[512]{0:T(512)} %add_rsqrt_fusion) | copy-start | bytes 6148
  448.3 12.6 copy-start.148
  481.6 157.6 %reduce-scatter.17.cloned.1.call-start = ((), (), s32[]{:S(2)}) async-start(), calls=%async_computation.8 | async-start | bytes 7520256 | tf_op jit(solution)/shard_map/reduce_scatter | solution.py:326
  481.7 12.2 slice-start
  481.7 12.2 slice-start.1
  481.7 13.4 %slice-start.2 = ((s8[12582912]{0:T(1024)(128)(4,1)}), s8[4194304]{0:T(1024)(128)(4,1)S(1)}, s32[]{:S(2)}) async-start(s8[12582912]{0:T(1024)(128)(4,1)} %bitcast.491), calls=%async_computation.22 | async-start | bytes 8388608
  481.7 13.4 %copy-start.31 = (pred[512,512]{0,1:T(8,128)(4,1)S(1)}, pred[512,512]{0,1:T(8,128)(4,1)}, u32[]{:S(2)}) copy-start(pred[512,512]{0,1:T(8,128)(4,1)} %fusion.369) | copy-start | bytes 786436
  481.7 13.4 %copy-start.87 = (f32[12,512]{1,0:T(8,128)S(1)}, f32[12,512]{1,0:T(8,128)}, u32[]{:S(2)}) copy-start(f32[12,512]{1,0:T(8,128)} %log_add_fusion) | copy-start | bytes 73732
  505.5 10.9 slice-start.9
  524.5 230.3 %reduce-scatter.21.cloned.1.call-start = ((), (), s32[]{:S(2)}) async-start(), calls=%async_computation.12 | async-start | bytes 10027008 | tf_op jit(solution)/shard_map/reduce_scatter | solution.py:332
  544.9 326.1 %reduce-scatter.23.cloned.1.call-start = ((), (), s32[]{:S(2)}) async-start(), calls=%async_computation.14 | async-start | bytes 10027008 | tf_op jit(solution)/shard_map/reduce_scatter | solution.py:334
  563.0 438.1 %reduce-scatter.25.cloned.1.call-start = ((), (), s32[]{:S(2)}) async-start(), calls=%async_computation.16 | async-start | bytes 417792
  591.2 428.4 %reduce-scatter.27.cloned.1.call-start = ((), (), s32[]{:S(2)}) async-start(), calls=%async_computation.17 | async-start | bytes 417792
  595.5 450.7 %reduce-scatter.29.cloned.1.call-start = ((), (), s32[]{:S(2)}) async-start(), calls=%async_computation.18 | async-start | bytes 417792
  599.8 505.0 %reduce-scatter.31.cloned.1.call-start = ((), (), s32[]{:S(2)}) async-start(), calls=%async_computation.19 | async-start | bytes 417792
  601.6 542.9 %all-gather.11.cloned.1.call-start = ((), (), s32[]{:S(2)}) async-start(), calls=%async_computation.11 | async-start | bytes 1253376 | tf_op jit(solution)/shard_map/all_gather | solution.py:343
  603.2 589.6 %all-gather.9.cloned.1.call-start = ((), (), s32[]{:S(2)}) async-start(), calls=%async_computation.9 | async-start | bytes 3760128 | tf_op jit(solution)/shard_map/all_gather | solution.py:337
  641.0 607.1 %all-gather.13.cloned.1.call-start = ((), (), s32[]{:S(2)}) async-start(), calls=%async_computation.13 | async-start | bytes 5013504 | tf_op jit(solution)/shard_map/all_gather | solution.py:355
  756.6 545.6 %all-gather.15.cloned.1.call-start = ((), (), s32[]{:S(2)}) async-start(), calls=%async_computation.15 | async-start | bytes 5013504 | tf_op jit(solution)/shard_map/all_gather | solution.py:361
  787.4 85.4 %copy-start.110 = (f32[768]{0:T(1024)S(1)}, f32[768]{0:T(1024)}, u32[]{:S(2)}) copy-start(f32[768]{0:T(1024)} %copy-done.105) | copy-start | bytes 9220
  788.4 84.4 %copy-start.125 = (f32[512]{0:T(512)}, f32[512]{0:T(512)S(1)}, u32[]{:S(2)}) copy-start(f32[512]{0:T(512)S(1)} %broadcast_multiply_fusion.19) | copy-start | bytes 6148
  872.9 26.2 %copy-start.78 = (f32[768]{0:T(1024)S(1)}, f32[768]{0:T(1024)}, u32[]{:S(2)}) copy-start(f32[768]{0:T(1024)} %copy-done.76) | copy-start | bytes 9220
  872.9 26.2 %copy-start.91 = (f32[768]{0:T(1024)S(1)}, f32[768]{0:T(1024)}, u32[]{:S(2)}) copy-start(f32[768]{0:T(1024)} %copy-done.90) | copy-start | bytes 9220
  (133 other events, 626.7 us)
Sparse Core Ops, SparseCore 0:
  481.7 63.2 reduce-scatter.18
  550.1 89.0 reduce-scatter.16
  643.9 110.8 reduce-scatter.20
  759.9 111.1 reduce-scatter.22
  874.4 55.3 reduce-scatter.24
  933.6 54.5 reduce-scatter.26
  991.7 54.5 reduce-scatter.28
  1050.1 54.6 reduce-scatter.30
  1107.1 37.3 all-gather.10
  1146.6 46.1 all-gather.8
  1195.7 52.3 all-gather.12
  1250.2 51.9 all-gather.14
where the time goes:
time: 1320 us
  waiting for transfers between devices  474 us (36%)
  matrix products  420 us (32%)
  blocking collectives  165 us (12%)
  other arithmetic  127 us (10%)
  local copies, waits for them, and re-layouts  97.7 us (7%)
  between operations  20.3 us (2%)
    reduce_scatter x1, waiting for transfers between devices, shards(): lax.psum_scatter(totals[6], 'dp', scatter_dimension=0, tiled=True)  114 us
    unnamed x2, blocking collectives  90.3 us
    reduce_scatter x1, waiting for transfers between devices, shards(): lax.psum_scatter(totals[8], 'dp', scatter_dimension=0, tiled=True)  80.6 us
    dot_general x6, matrix products, layer_forward(): jnp.dot(gelu_low, down_weight, preferred_element_type=jnp.float32)  79.5 us
    dot_general x12, matrix products, contract_rows(): lax.dot_general(left, right, (((0,), (0,)), ((), ())), preferred_element_...  65.3 us
    dot_general x3, matrix products, layer_forward(): jnp.dot(normed_low, up_weight, preferred_element_type=jnp.float32) + up_bias  60 us
    all_gather x1, waiting for transfers between devices, shards(): lax.all_gather(shares[6].astype(jnp.bfloat16), 'dp', axis=0, tiled=True)  49.8 us
    all_gather x1, waiting for transfers between devices, shards(): lax.all_gather(shares[8].astype(jnp.bfloat16), 'dp', axis=0, tiled=True)  46.7 us
  transfers between devices with their start and end apart: 16, of which 13 were waited for; matrix products, arithmetic and copies ran while one was open for 18% of the time, Pallas kernels for 0%

commit v1 on v0

v1 whole, which is shorter than its diff:
```python
import functools
import math

import jax
import jax.numpy as jnp
from jax import lax
from jax.experimental import pallas as pl
from jax.experimental.pallas import tpu as pltpu
from jax.sharding import PartitionSpec as P

D = 768
H = 12
HD = 64
FF = 3072
SEQ = 512
MICRO = 2
PAIRS = H // 2
PAIR = 2 * HD

EPSILON = 1e-05
SCORE_SCALE = 0.125
NEG_FILL = -1e30
F32 = jnp.float32
BF16 = jnp.bfloat16
VMEM_LIMIT = 60 << 20

ANY = pl.BlockSpec(memory_space=pl.ANY)
VMEM = pl.BlockSpec(memory_space=pltpu.VMEM)
SMEM = pl.BlockSpec(memory_space=pltpu.SMEM)


def dot_nn(left, right):
    return lax.dot_general(left, right, (((1,), (0,)), ((), ())), preferred_element_type=F32)


def dot_nt(left, right):
    return lax.dot_general(left, right, (((1,), (1,)), ((), ())), preferred_element_type=F32)


def dot_tn(left, right):
    return lax.dot_general(left, right, (((0,), (0,)), ((), ())), preferred_element_type=F32)


def begin(source, target, sem):
    copy = pltpu.make_async_copy(source, target, sem)
    copy.start()
    return copy


def gelu_and_slope(u):
    size = jnp.abs(u)
    bell = jnp.exp(-0.5 * (u * u))
    t = 1.0 / (1.0 + (0.3275911 / math.sqrt(2.0)) * size)
    poly = t * (
        0.5 * 0.254829592
        + t * (-0.5 * 0.284496736 + t * (0.5 * 1.421413741 + t * (-0.5 * 1.453152027 + t * (0.5 * 1.061405429))))
    )
    tail = poly * bell
    cdf = jnp.where(u < 0.0, tail, 1.0 - tail)
    return u * cdf, cdf + u * bell * (1.0 / math.sqrt(2.0 * math.pi))


def normalize(resid):
    average = jnp.mean(resid, axis=-1, keepdims=True)
    centred = resid - average
    variance = jnp.mean(centred * centred, axis=-1, keepdims=True)
    inverse = lax.rsqrt(variance + EPSILON)
    return centred * inverse, inverse


def norm_back(grad_out, scaled, inverse, gain):
    weighted = grad_out * gain
    first_mean = jnp.mean(weighted, axis=-1, keepdims=True)
    second_mean = jnp.mean(weighted * scaled, axis=-1, keepdims=True)
    return inverse * (weighted - first_mean - scaled * second_mean)


def half_mask(which):
    lane = lax.broadcasted_iota(jnp.int32, (1, PAIR), 1)
    return ((lane // HD) == which).astype(F32).astype(BF16)


SAVED = (
    ("act", D, BF16),
    ("qkv", 3 * D, BF16),
    ("ctx", D, BF16),
    ("xh1", D, BF16),
    ("inv1", 128, F32),
    ("low", D, BF16),
    ("gelu", FF, BF16),
    ("slope", FF, BF16),
    ("xh2", D, BF16),
    ("inv2", 128, F32),
)


def forward_kernel(step, n_alias, *refs):
    (tok, rec, wqkv, wo, wu, wd, segs, lens, qv_bias, out_biases, gains, shifts, up_bias) = refs[:13]
    outs = refs[13 + n_alias : 13 + n_alias + 13]
    y_hop, hid_out, prob_out = outs[:3]
    saved_out = dict(zip([name for name, _, _ in SAVED], outs[3:]))
    (
        h_v, wqkv_v, wo_v, wu_v, wd_v, bias_v, p_v, acc_v,
        act_v, qkv_v, ctx_v, xh1_v, inv1_v, low_v, gelu_v, slope_v, xh2_v, inv2_v,
        in_sem, w_sem, p_sem, out_sem,
    ) = refs[13 + n_alias + 13 :]
    section = lax.axis_index("section")
    mb = step - section

    @pl.when((mb >= 0) & (mb < MICRO))
    def _():
        rows = pl.ds(pl.multiple_of(mb * SEQ, SEQ), SEQ)

        @pl.when(section == 0)
        def _():
            begin(tok.at[rows], h_v, in_sem.at[0])

        @pl.when(section != 0)
        def _():
            begin(rec, h_v, in_sem.at[0])

        w_copies = [
            begin(wqkv.at[0], wqkv_v, w_sem.at[0]),
            begin(wo.at[0], wo_v, w_sem.at[1]),
            begin(wu.at[0], wu_v, w_sem.at[2]),
            begin(wd.at[0], wd_v, w_sem.at[3]),
        ]
        seg_row = segs[pl.ds(mb, 1), :]
        seg_col = jnp.transpose(jnp.broadcast_to(seg_row.astype(F32), (128, SEQ)))
        length = lens[mb]
        query = lax.broadcasted_iota(jnp.int32, (SEQ, 128), 0)
        for tile in range(SEQ // 128):
            key = lax.broadcasted_iota(jnp.int32, (SEQ, 128), 1) + tile * 128
            same = seg_col == seg_row[:, tile * 128 : (tile + 1) * 128].astype(F32)
            allowed = same & ((key < length) | (key == query))
            bias_v[:, tile * 128 : (tile + 1) * 128] = jnp.where(allowed, 0.0, NEG_FILL)

        pending = []

        def save(name, value_ref):
            pending.append(begin(value_ref, saved_out[name].at[rows], out_sem.at[len(pending)]))

        pltpu.make_async_copy(rec, h_v, in_sem.at[0]).wait()
        pending.append(begin(h_v, hid_out.at[rows], out_sem.at[0]))
        w_copies[0].wait()
        for block in range(3):
            cols = slice(block * D, (block + 1) * D)
            proj = dot_nn(h_v[...], wqkv_v[:, cols])
            if block != 1:
                proj = proj + qv_bias[0, block // 2 : block // 2 + 1, :]
            qkv_v[:, cols] = proj.astype(BF16)
        save("qkv", qkv_v)

        def pair_step(pair, carry):
            slot = lax.rem(pair, 2)

            @pl.when(pair >= 2)
            def _():
                pltpu.make_async_copy(p_v.at[slot], prob_out.at[mb, pl.ds(0, 2)], p_sem.at[slot]).wait()

            at = pl.multiple_of(pair * PAIR, PAIR)
            q2 = qkv_v[:, pl.ds(at, PAIR)] * SCORE_SCALE
            k2 = qkv_v[:, pl.ds(at + D, PAIR)]
            v2 = qkv_v[:, pl.ds(at + 2 * D, PAIR)]
            total = None
            for head in range(2):
                mask = half_mask(head)
                scores = dot_nt(q2, k2 * mask) + bias_v[...]
                exp_vals = jnp.exp(scores - jnp.max(scores, axis=-1, keepdims=True))
                inverse_total = 1.0 / jnp.sum(exp_vals, axis=-1, keepdims=True)
                prob = (exp_vals * inverse_total).astype(BF16)
                p_v[slot, head] = prob
                part = dot_nn(prob, v2 * mask)
                total = part if total is None else total + part
            ctx_v[:, pl.ds(at, PAIR)] = total.astype(BF16)
            begin(p_v.at[slot], prob_out.at[mb, pl.ds(pair * 2, 2)], p_sem.at[slot])
            return carry

        lax.fori_loop(0, PAIRS, pair_step, 0)
        save("ctx", ctx_v)

        w_copies[1].wait()
        resid = h_v[...].astype(F32) + (dot_nn(ctx_v[...], wo_v[...]) + out_biases[0, 0:1, :])
        scaled, inverse = normalize(resid)
        xh1_v[...] = scaled.astype(BF16)
        inv1_v[...] = jnp.broadcast_to(inverse, (SEQ, 128))
        normed = scaled * gains[0, 0:1, :] + shifts[0, 0:1, :]
        low_v[...] = normed.astype(BF16)
        acc_v[...] = normed + out_biases[0, 1:2, :]
        save("xh1", xh1_v)
        save("inv1", inv1_v)
        save("low", low_v)
        w_copies[2].wait()
        w_copies[3].wait()
        width = 512
        for chunk in range(FF // width):
            cols = slice(chunk * width, (chunk + 1) * width)
            up = dot_nn(low_v[...], wu_v[:, cols]) + up_bias[0:1, cols]
            gelu, slope = gelu_and_slope(up)
            gelu = gelu.astype(BF16)
            gelu_v[:, cols] = gelu
            slope_v[:, cols] = slope.astype(BF16)
            acc_v[...] += dot_nn(gelu, wd_v[cols, :])
        save("gelu", gelu_v)
        save("slope", slope_v)
        scaled, inverse = normalize(acc_v[...])
        xh2_v[...] = scaled.astype(BF16)
        inv2_v[...] = jnp.broadcast_to(inverse, (SEQ, 128))
        act_v[...] = (scaled * gains[0, 1:2, :] + shifts[0, 1:2, :]).astype(BF16)
        pending.append(begin(act_v, y_hop, out_sem.at[len(pending)]))
        save("act", act_v)
        save("xh2", xh2_v)
        save("inv2", inv2_v)
        for slot in range(2):
            pltpu.make_async_copy(p_v.at[slot], prob_out.at[mb, pl.ds(0, 2)], p_sem.at[slot]).wait()
        for copy in pending:
            copy.wait()


def forward(step, tokens, received, weights, segments, lengths, params, saved):
    total = MICRO * SEQ
    shapes = [
        jax.ShapeDtypeStruct((SEQ, D), BF16),
        jax.ShapeDtypeStruct((total, D), BF16),
        jax.ShapeDtypeStruct((MICRO, H, SEQ, SEQ), BF16),
    ] + [jax.ShapeDtypeStruct((total, width), dtype) for _, width, dtype in SAVED]
    n_alias = len(saved)
    ins = [tokens, received, *weights, segments, lengths, *params, *saved]
    result = pl.pallas_call(
        functools.partial(forward_kernel, step, n_alias),
        out_shape=shapes,
        in_specs=[ANY] * 6 + [VMEM, SMEM] + [VMEM] * 5 + [ANY] * n_alias,
        out_specs=[ANY] * len(shapes),
        input_output_aliases={13 + i: 1 + i for i in range(n_alias)},
        scratch_shapes=[
            pltpu.VMEM((SEQ, D), BF16),
            pltpu.VMEM((D, 3 * D), BF16),
            pltpu.VMEM((D, D), BF16),
            pltpu.VMEM((D, FF), BF16),
            pltpu.VMEM((FF, D), BF16),
            pltpu.VMEM((SEQ, SEQ), F32),
            pltpu.VMEM((2, 2, SEQ, SEQ), BF16),
            pltpu.VMEM((SEQ, D), F32),
        ]
        + [pltpu.VMEM((SEQ, width), dtype) for _, width, dtype in SAVED]
        + [
            pltpu.SemaphoreType.DMA((1,)),
            pltpu.SemaphoreType.DMA((4,)),
            pltpu.SemaphoreType.DMA((2,)),
            pltpu.SemaphoreType.DMA((16,)),
        ],
        compiler_params=pltpu.CompilerParams(vmem_limit_bytes=VMEM_LIMIT),
        name="forward",
    )(*ins)
    return result[0], list(result[1:])


GRADS = (("d_down", D, BF16), ("d_up", FF, BF16), ("d_attn", D, BF16), ("d_qkv", 3 * D, BF16), ("d_hid", D, BF16))
SMALL_ROWS = 16


def backward_kernel(step, n_alias, *refs):
    (cot, rec, wqkv, wo, wu, wd, gains, prob_in) = refs[:8]
    saved_in = dict(zip([name for name, _, _ in SAVED], refs[8:18]))
    outs = refs[18 + n_alias : 18 + n_alias + 7]
    d_hop, small_out = outs[:2]
    grads_out = dict(zip([name for name, _, _ in GRADS], outs[2:]))
    (
        g_v, wqkv_v, wo_v, wu_v, wd_v, p_v, acc_v, acc2_v, small_v,
        qkv_v, ctx_v, xh1_v, inv1_v, slope_v, xh2_v, inv2_v, d_ctx_v,
        d_down_v, d_up_v, d_attn_v, d_qkv_v, d_hid_v,
        in_sem, w_sem, p_sem, out_sem,
    ) = refs[18 + n_alias + 7 :]
    section = lax.axis_index("section")
    mb = step - (1 - section)

    @pl.when((mb >= 0) & (mb < MICRO))
    def _():
        rows = pl.ds(pl.multiple_of(mb * SEQ, SEQ), SEQ)

        @pl.when(section == 0)
        def _():
            begin(rec, g_v, in_sem.at[0])

        @pl.when(section != 0)
        def _():
            begin(cot.at[rows], g_v, in_sem.at[0])

        def fetch(name, target, index):
            return begin(saved_in[name].at[rows], target, in_sem.at[index])

        get_xh2 = fetch("xh2", xh2_v, 1)
        get_inv2 = fetch("inv2", inv2_v, 2)
        get_wd = begin(wd.at[0], wd_v, w_sem.at[3])
        get_slope = fetch("slope", slope_v, 3)
        get_wu = begin(wu.at[0], wu_v, w_sem.at[2])
        get_xh1 = fetch("xh1", xh1_v, 4)
        get_inv1 = fetch("inv1", inv1_v, 5)
        get_wo = begin(wo.at[0], wo_v, w_sem.at[1])
        get_qkv = fetch("qkv", qkv_v, 6)
        get_ctx = fetch("ctx", ctx_v, 7)
        begin(prob_in.at[mb, pl.ds(0, 2)], p_v.at[0], p_sem.at[0])
        get_wqkv = begin(wqkv.at[0], wqkv_v, w_sem.at[0])

        pending = []

        def save(name, value_ref):
            pending.append(begin(value_ref, grads_out[name].at[rows], out_sem.at[len(pending)]))

        def column_sum(value):
            return jnp.sum(value, axis=0, keepdims=True)

        small_v[...] = jnp.zeros_like(small_v)
        pltpu.make_async_copy(rec, g_v, in_sem.at[0]).wait()
        get_xh2.wait()
        get_inv2.wait()
        grad = g_v[...].astype(F32)
        scaled = xh2_v[...].astype(F32)
        small_v[5:6, :] = column_sum(grad * scaled)
        small_v[7:8, :] = column_sum(grad)
        d_r2 = norm_back(grad, scaled, inv2_v[:, 0:1], gains[0, 1:2, :])
        d_down = d_r2.astype(BF16)
        d_down_v[...] = d_down
        small_v[3:4, :] = column_sum(d_down.astype(F32))
        acc_v[...] = d_r2
        save("d_down", d_down_v)
        get_wd.wait()
        get_slope.wait()
        get_wu.wait()
        width = 512
        for chunk in range(FF // width):
            cols = slice(chunk * width, (chunk + 1) * width)
            d_up = (dot_nt(d_down_v[...], wd_v[cols, :]) * slope_v[:, cols].astype(F32)).astype(BF16)
            d_up_v[:, cols] = d_up
            at = chunk * width
            sums = column_sum(d_up.astype(F32))
            while at < (chunk + 1) * width:
                row = at // D
                stop = min((row + 1) * D, (chunk + 1) * width)
                small_v[8 + row : 9 + row, at - row * D : stop - row * D] = sums[
                    :, at - chunk * width : stop - chunk * width
                ]
                at = stop
            acc_v[...] += dot_nt(d_up, wu_v[:, cols])
        save("d_up", d_up_v)
        get_xh1.wait()
        get_inv1.wait()
        d_normed = acc_v[...]
        scaled = xh1_v[...].astype(F32)
        small_v[4:5, :] = column_sum(d_normed * scaled)
        small_v[6:7, :] = column_sum(d_normed)
        d_r1 = norm_back(d_normed, scaled, inv1_v[:, 0:1], gains[0, 0:1, :])
        d_attn = d_r1.astype(BF16)
        d_attn_v[...] = d_attn
        small_v[2:3, :] = column_sum(d_attn.astype(F32))
        acc_v[...] = d_r1
        save("d_attn", d_attn_v)
        get_wo.wait()
        d_ctx_v[...] = dot_nt(d_attn, wo_v[...]).astype(BF16)
        get_qkv.wait()
        get_ctx.wait()

        def pair_step(pair, carry):
            slot = lax.rem(pair, 2)

            @pl.when(pair + 1 < PAIRS)
            def _():
                begin(prob_in.at[mb, pl.ds((pair + 1) * 2, 2)], p_v.at[1 - slot], p_sem.at[1 - slot])

            pltpu.make_async_copy(prob_in.at[mb, pl.ds(0, 2)], p_v.at[slot], p_sem.at[slot]).wait()
            at = pl.multiple_of(pair * PAIR, PAIR)
            q2 = qkv_v[:, pl.ds(at, PAIR)] * SCORE_SCALE
            k2 = qkv_v[:, pl.ds(at + D, PAIR)]
            v2 = qkv_v[:, pl.ds(at + 2 * D, PAIR)]
            dc2 = d_ctx_v[:, pl.ds(at, PAIR)]
            inner = dc2.astype(F32) * ctx_v[:, pl.ds(at, PAIR)].astype(F32)
            d_q, d_k, d_v = None, None, None
            for head in range(2):
                mask = half_mask(head)
                k_own, q_own, dc_own = k2 * mask, q2 * mask, dc2 * mask
                prob = p_v[slot, head]
                row_inner = jnp.sum(inner * mask.astype(F32), axis=-1, keepdims=True)
                d_prob = dot_nt(dc_own, v2)
                d_score = (prob.astype(F32) * (d_prob - row_inner)).astype(BF16)
                part_v = dot_tn(dc_own, prob)
                part_q = dot_nn(d_score, k_own)
                part_k = dot_tn(q_own, d_score)
                d_v = part_v if d_v is None else d_v + part_v
                d_q = part_q if d_q is None else d_q + part_q
                d_k = part_k if d_k is None else d_k + part_k
            d_qkv_v[:, pl.ds(at, PAIR)] = (d_q * SCORE_SCALE).astype(BF16)
            d_qkv_v[:, pl.ds(at + D, PAIR)] = jnp.transpose(d_k).astype(BF16)
            d_qkv_v[:, pl.ds(at + 2 * D, PAIR)] = jnp.transpose(d_v).astype(BF16)
            return carry

        lax.fori_loop(0, PAIRS, pair_step, 0)
        save("d_qkv", d_qkv_v)
        get_wqkv.wait()
        small_v[0:1, :] = column_sum(d_qkv_v[:, 0:D].astype(F32))
        small_v[1:2, :] = column_sum(d_qkv_v[:, 2 * D : 3 * D].astype(F32))
        d_hid_v[...] = (acc_v[...] + dot_nt(d_qkv_v[...], wqkv_v[...])).astype(BF16)
        pending.append(begin(d_hid_v, d_hop, out_sem.at[len(pending)]))
        save("d_hid", d_hid_v)
        pending.append(begin(small_v, small_out.at[mb], out_sem.at[len(pending)]))
        for copy in pending:
            copy.wait()


def backward(step, cotangent, received, weights, gains, prob, saved, grads):
    total = MICRO * SEQ
    shapes = [
        jax.ShapeDtypeStruct((SEQ, D), BF16),
        jax.ShapeDtypeStruct((MICRO, SMALL_ROWS, D), F32),
    ] + [jax.ShapeDtypeStruct((total, width), dtype) for _, width, dtype in GRADS]
    n_alias = len(grads)
    ins = [cotangent, received, *weights, gains, prob, *saved, *grads]
    widths = {name: (width, dtype) for name, width, dtype in SAVED}
    kept = ("qkv", "ctx", "xh1", "inv1", "slope", "xh2", "inv2")
    result = pl.pallas_call(
        functools.partial(backward_kernel, step, n_alias),
        out_shape=shapes,
        in_specs=[ANY] * 6 + [VMEM] + [ANY] * (11 + n_alias),
        out_specs=[ANY] * len(shapes),
        input_output_aliases={18 + i: 1 + i for i in range(n_alias)},
        scratch_shapes=[
            pltpu.VMEM((SEQ, D), BF16),
            pltpu.VMEM((D, 3 * D), BF16),
            pltpu.VMEM((D, D), BF16),
            pltpu.VMEM((D, FF), BF16),
            pltpu.VMEM((FF, D), BF16),
            pltpu.VMEM((2, 2, SEQ, SEQ), BF16),
            pltpu.VMEM((SEQ, D), F32),
            pltpu.VMEM((8, 128), F32),
            pltpu.VMEM((SMALL_ROWS, D), F32),
        ]
        + [pltpu.VMEM((SEQ, widths[name][0]), widths[name][1]) for name in kept]
        + [pltpu.VMEM((SEQ, D), BF16)]
        + [pltpu.VMEM((SEQ, width), dtype) for _, width, dtype in GRADS]
        + [
            pltpu.SemaphoreType.DMA((8,)),
            pltpu.SemaphoreType.DMA((4,)),
            pltpu.SemaphoreType.DMA((2,)),
            pltpu.SemaphoreType.DMA((8,)),
        ],
        compiler_params=pltpu.CompilerParams(vmem_limit_bytes=VMEM_LIMIT),
        name="backward",
    )(*ins)
    return result[0], list(result[1:])


def reduced(value, dim):
    share = lax.psum_scatter(value.astype(BF16), "dp", scatter_dimension=dim, tiled=True)
    return lax.all_gather(share, "dp", axis=dim, tiled=True).astype(F32)[None]


def shards(
    tokens, segments, lengths, cotangent, qkv_weight, qv_bias, out_weight, out_biases,
    norm_gains, norm_shifts, up_weight, up_bias, down_weight,
):
    weights = (qkv_weight, out_weight, up_weight, down_weight)
    params = (qv_bias, out_biases, norm_gains, norm_shifts, up_bias)
    onward = [(0, 1)]
    back = [(1, 0)]
    received = tokens[:SEQ]
    state = []
    for step in range(MICRO + 1):
        hop, state = forward(step, tokens, received, weights, segments, lengths, params, state)
        if step < MICRO:
            received = lax.ppermute(hop, "section", onward)
    hid, prob = state[:2]
    saved = state[2:]
    act = saved[0]
    received = cotangent[:SEQ]
    grads = []
    for step in range(MICRO + 1):
        hop, grads = backward(step, cotangent, received, weights, norm_gains, prob, saved, grads)
        if step < MICRO:
            received = lax.ppermute(hop, "section", back)
    small = jnp.sum(grads[0], axis=0)
    d_down, d_up, d_attn, d_qkv, d_hid = grads[1:]
    names = {name: index for index, (name, _, _) in enumerate(SAVED)}
    g_down = reduced(dot_tn(saved[names["gelu"]], d_down), 0)
    g_up = reduced(dot_tn(saved[names["low"]], d_up), 0)
    g_out = reduced(dot_tn(saved[names["ctx"]], d_attn), 0)
    g_qkv = reduced(dot_tn(hid, d_qkv), 0)
    small = lax.psum(small, "dp")[None]
    return (
        act[None], d_hid[None], g_qkv, small[:, 0:2], g_out, small[:, 2:4], small[:, 4:6], small[:, 6:8],
        g_up, small[:, 8:12].reshape(1, FF), g_down,
    )


def solution(mesh):
    return jax.shard_map(
        shards,
        mesh=mesh,
        in_specs=(
            P("dp", None), P("dp", None), P("dp"), P("dp", None),
            P("section", None, None), P("section", None, None), P("section", None, None), P("section", None, None),
            P("section", None, None), P("section", None, None), P("section", None, None), P("section", None),
            P("section", None, None),
        ),
        out_specs=(
            P("section", "dp", None), P("section", "dp", None),
            P("section", None, None), P("section", None, None), P("section", None, None), P("section", None, None),
            P("section", None, None), P("section", None, None), P("section", None, None), P("section", None),
            P("section", None, None),
        ),
        check_vma=False,
    )
```

time: 1320 us -> 777 us (0.59)
  matrix products: 420 us -> 30.9 us
  Pallas kernels: 0 us -> 121 us
  blocking collectives: 165 us -> 58.5 us
  other arithmetic: 127 us -> 22.5 us
  local copies, waits for them, and re-layouts: 97.7 us -> 10.5 us
  waiting for transfers between devices: 474 us -> 504 us
    dot_general x66 -> x4, matrix products: 385 us -> 30.9 us  [dot_tn(): lax.dot_general(left, right, (((0,), (0,)), ((), ())), preferred_element_...]
    pallas_call x0 -> x6, Pallas kernels: none -> 121 us  [the longest x3 69.9 us: forward(): pl.pallas_call(functools.partial(forward_kernel, step, n_alias), out_shap...]
    unnamed x2 -> x0, blocking collectives: 90.3 us -> none
    ppermute x4, waiting for transfers between devices: 38.5 us -> 125 us  [the longest x2 91.3 us: shards(): received = lax.ppermute(hop, 'section', back)]
    all_gather x4 -> x0, blocking collectives: 74.6 us -> none  [the longest x1 19.3 us: shards(): lax.all_gather(shares[4].astype(jnp.bfloat16), 'dp', axis=1, tiled=True)]
    psum x0 -> x1, blocking collectives: none -> 58.5 us  [shards(): small = lax.psum(small, 'dp')[None]]
    unnamed x16 -> x8, waiting for transfers between devices: 44.1 us -> 0.13 us
    convert_element_type x8 -> x0, other arithmetic: 40.7 us -> none  [the longest x3 21.8 us: attend_back(): grad_scores = (prob_full * (grad_prob - row_inner)).astype(jnp.bfloat16)]
  transfers between devices with their start and end apart: 16 -> 12, of which waited for: 13 -> 11; matrix products, arithmetic and copies ran while one was open for 18% -> 6% of each run, Pallas kernels for 0% -> 0%
where the time goes in v1:
time: 777 us; the launch traced here: 772 us
  waiting for transfers between devices  504 us (65%)
  Pallas kernels  121 us (16%)
  blocking collectives  58.5 us (8%)
  matrix products  30.9 us (4%)
  other arithmetic  22.5 us (3%)
  between operations  14.5 us (2%)
  local copies, waits for them, and re-layouts  10.5 us (1%)
  starting transfers between devices  10.1 us (1%)
    reduce_scatter x4, waiting for transfers between devices, reduced(): lax.psum_scatter(value.astype(BF16), 'dp', scatter_dimension=dim, tiled=T...  256 us
    all_gather x4, waiting for transfers between devices, reduced(): return lax.all_gather(share, 'dp', axis=dim, tiled=True).astype(F32)[None]  122 us
    ppermute x2, waiting for transfers between devices, shards(): received = lax.ppermute(hop, 'section', back)  91.3 us
    pallas_call x3, Pallas kernels, forward(): pl.pallas_call(functools.partial(forward_kernel, step, n_alias), out_shap...  69.9 us
    psum x1, blocking collectives, shards(): small = lax.psum(small, 'dp')[None]  58.5 us
    pallas_call x3, Pallas kernels, backward(): pl.pallas_call(functools.partial(backward_kernel, step, n_alias), out_sha...  50.8 us
    ppermute x2, waiting for transfers between devices, shards(): received = lax.ppermute(hop, 'section', onward)  34.1 us
    dot_general x4, matrix products, dot_tn(): lax.dot_general(left, right, (((0,), (0,)), ((), ())), preferred_element_...  30.9 us
  transfers between devices with their start and end apart: 12, of which 11 were waited for; matrix products, arithmetic and copies ran while one was open for 6% of the time, Pallas kernels for 0%

profile of v1, /device:TPU:0, one launch (start us, length us, event | category | flops | bytes accessed | tf_op | source)
XLA Modules:
  0.0 771.6 jit_solution(6718022558291492894)
XLA Ops:
  7.2 0.0 reduce-scatter.7.cloned.1.call-start
  7.2 2.1 slice.21.refs_1_
  9.3 38.9 %forward.3 = (bf16[512,768]{1,0:T(8,128)(2,1)}, bf16[1024,768]{1,0:T(8,128)(2,1)}, bf16[2,12,512,512]{3,2,1,0:T(8,128)(2,1)}, bf16[1024,768]{1,0:T(8,128)(2,1)},...) custom-call(bf16[1024,768]{1,0:T(8,128)(2,1)} %refs_0_.8, ...), custom_call_target="tpu_custom_call" | custom-call | tf_op jit(solution)/shard_map/forward/pallas_call | solution.py:229
  48.2 1.3 collective-permute-start
  49.5 17.9 %collective-permute-done.refs_1_ = bf16[512,768]{1,0:T(8,128)(2,1)S(1)} collective-permute-done((bf16[512,768]{1,0:T(8,128)(2,1)}, bf16[512,768]{1,0:T(8,128)(2,1)S(1)}, u32[]{:S(2)}, u32[]{:S(2)}) %collective-permute-start) | collective-permute-done | bytes 786464 | tf_op jit(solution)/shard_map/ppermute | solution.py:469
  67.5 0.0 copy-start.7
  67.5 0.9 copy-done.7
  68.4 0.0 copy-start.2
  68.4 29.8 %forward.4 = (bf16[512,768]{1,0:T(8,128)(2,1)}, bf16[1024,768]{1,0:T(8,128)(2,1)}, bf16[2,12,512,512]{3,2,1,0:T(8,128)(2,1)}, bf16[1024,768]{1,0:T(8,128)(2,1)},...) custom-call(bf16[1024,768]{1,0:T(8,128)(2,1)} %refs_0_.8, ...), custom_call_target="tpu_custom_call", output_to_operand_aliasing={{1}: (13, {}), {2}: (14, {}), {3}: (15, {}), {4}: (16, {}),... | custom-call | tf_op jit(solution)/shard_map/forward/pallas_call | solution.py:229
  98.2 5.7 collective-permute-start.1
  103.9 0.0 copy-done.2
  103.9 0.9 slice.22.refs_1_
  104.8 16.1 %collective-permute-done.1.refs_1_ = bf16[512,768]{1,0:T(8,128)(2,1)S(1)} collective-permute-done((bf16[512,768]{1,0:T(8,128)(2,1)}, bf16[512,768]{1,0:T(8,128)(2,1)S(1)}, u32[]{:S(2)}, u32[]{:S(2)}) %collective-permute-start.1) | collective-permute-done | bytes 786464 | tf_op jit(solution)/shard_map/ppermute | solution.py:469
  120.9 0.0 copy-start.6
  120.9 0.9 copy-done.6
  121.8 1.2 forward.5
  123.0 0.9 backward.3
  123.9 1.3 collective-permute-start.2
  125.2 72.7 %collective-permute-done.2.refs_1_ = bf16[512,768]{1,0:T(8,128)(2,1)S(1)} collective-permute-done((bf16[512,768]{1,0:T(8,128)(2,1)}, bf16[512,768]{1,0:T(8,128)(2,1)S(1)}, u32[]{:S(2)}, u32[]{:S(2)}) %collective-permute-start.2) | collective-permute-done | bytes 786464 | tf_op jit(solution)/shard_map/ppermute | solution.py:478
  197.9 0.9 copy-done.9
  198.8 24.8 %backward.4 = (bf16[512,768]{1,0:T(8,128)(2,1)}, f32[2,16,768]{2,1,0:T(8,128)}, bf16[1024,768]{1,0:T(8,128)(2,1)}, bf16[1024,3072]{1,0:T(8,128)(2,1)}, bf16[1024...) custom-call(bf16[1024,768]{1,0:T(8,128)(2,1)} %refs_0_.11, ...), custom_call_target="tpu_custom_call", output_to_operand_aliasing={{1}: (18, {}), {2}: (19, {}), {3}: (20, {}), {4}: (21, {}),... | custom-call | tf_op jit(solution)/shard_map/backward/pallas_call | solution.py:419
  223.6 1.3 collective-permute-start.3
  224.9 18.6 %collective-permute-done.3.refs_1_ = bf16[512,768]{1,0:T(8,128)(2,1)S(1)} collective-permute-done((bf16[512,768]{1,0:T(8,128)(2,1)}, bf16[512,768]{1,0:T(8,128)(2,1)S(1)}, u32[]{:S(2)}, u32[]{:S(2)}) %collective-permute-start.3) | collective-permute-done | bytes 786464 | tf_op jit(solution)/shard_map/ppermute | solution.py:478
  243.5 0.9 copy-done.8
  244.4 25.1 %backward.5 = (bf16[512,768]{1,0:T(8,128)(2,1)}, f32[2,16,768]{2,1,0:T(8,128)}, bf16[1024,768]{1,0:T(8,128)(2,1)}, bf16[1024,3072]{1,0:T(8,128)(2,1)}, bf16[1024...) custom-call(bf16[1024,768]{1,0:T(8,128)(2,1)} %refs_0_.11, ...), custom_call_target="tpu_custom_call", output_to_operand_aliasing={{1}: (18, {}), {2}: (19, {}), {3}: (20, {}), {4}: (21, {}),... | custom-call | tf_op jit(solution)/shard_map/backward/pallas_call | solution.py:419
  269.5 0.0 copy-done
  269.5 0.0 copy-start.3
  269.5 4.0 convolution_convert_fusion.3
  273.5 0.0 reduce-scatter.7.cloned.1.call-update
  273.5 0.2 reduce-scatter.5.cloned.1.call-start
  273.7 0.0 copy-done.3
  273.7 7.6 convolution_convert_fusion.2
  281.4 0.0 reduce-scatter.5.cloned.1.call-update
  281.4 0.0 reduce-scatter.11.cloned.1.call-start
  281.5 1.4 copy-done.4
  282.8 9.7 %convolution_convert_fusion = bf16[3072,768]{1,0:T(8,128)(2,1)} fusion(bf16[1024,3072]{1,0:T(8,128)(2,1)} %get-tuple-element.102.refs_14_, bf16[1024,768]{1,0:T(8,128)(2,1)S(1)} %copy-done.4), kind=kOutput, calls=%fused_computation | convolution fusion | flops 4834197504 | bytes 12582912 | tf_op jit(solution)/shard_map/dot_general | solution.py:41
  292.6 0.0 reduce-scatter.11.cloned.1.call-update
  292.6 0.0 reduce-scatter.9.cloned.1.call-start
  292.6 1.3 copy-done.1
  294.0 9.5 %convolution_convert_fusion.1 = bf16[768,3072]{1,0:T(8,128)(2,1)} fusion(bf16[1024,768]{1,0:T(8,128)(2,1)S(1)} %copy-done.1, bf16[1024,3072]{1,0:T(8,128)(2,1)} %get-tuple-element.125), kind=kOutput, calls=%fused_computation.1 | convolution fusion | flops 4834197504 | bytes 12582912 | tf_op jit(solution)/shard_map/dot_general | solution.py:41
  303.5 0.0 reduce-scatter.9.cloned.1.call-update
  303.5 0.0 all-gather.7.cloned.1.call-start
  303.6 27.4 %reduce-scatter.7.cloned.1.call-done = bf16[48,768]{1,0:T(8,128)(2,1)} async-done(((bf16[768,768]{1,0:T(8,128)(2,1)}), bf16[48,768]{1,0:T(8,128)(2,1)}) %reduce-scatter.7.cloned.1.call-update) | async-done | bytes 73744 | tf_op jit(solution)/shard_map/reduce_scatter | solution.py:452
  331.0 0.0 all-gather.7.cloned.1.call-update
  331.0 0.0 all-gather.5.cloned.1.call-start
  331.1 70.9 %reduce-scatter.5.cloned.1.call-done = bf16[48,2304]{1,0:T(8,128)(2,1)} async-done(((bf16[768,2304]{1,0:T(8,128)(2,1)}), bf16[48,2304]{1,0:T(8,128)(2,1)}) %reduce-scatter.5.cloned.1.call-update) | async-done | bytes 221200 | tf_op jit(solution)/shard_map/reduce_scatter | solution.py:452
  402.0 0.0 all-gather.5.cloned.1.call-update
  402.0 0.0 all-gather.11.cloned.1.call-start
  402.0 78.8 %reduce-scatter.11.cloned.1.call-done = bf16[192,768]{1,0:T(8,128)(2,1)} async-done(((bf16[3072,768]{1,0:T(8,128)(2,1)}), bf16[192,768]{1,0:T(8,128)(2,1)}) %reduce-scatter.11.cloned.1.call-update) | async-done | bytes 294928 | tf_op jit(solution)/shard_map/reduce_scatter | solution.py:452
  480.9 0.0 all-gather.11.cloned.1.call-update
  480.9 0.0 all-gather.9.cloned.1.call-start
  480.9 79.3 %reduce-scatter.9.cloned.1.call-done = bf16[48,3072]{1,0:T(8,128)(2,1)} async-done(((bf16[768,3072]{1,0:T(8,128)(2,1)}), bf16[48,3072]{1,0:T(8,128)(2,1)}) %reduce-scatter.9.cloned.1.call-update) | async-done | bytes 294928 | tf_op jit(solution)/shard_map/reduce_scatter | solution.py:452
  560.3 0.0 all-gather.9.cloned.1.call-update
  560.3 0.0 copy-done.5
  560.3 58.5 %psum.7 = f32[1,16,768]{2,1,0:T(8,128)S(1)} all-reduce(f32[1,16,768]{2,1,0:T(8,128)S(1)} %bitcast.28), channel_id=1, replica_groups=mesh['section'=2,'dp'=16] {'dp'}, use_global_device_ids=true, to_apply=%region_2.0 | all-reduce | flops 12288 | bytes 98304 | tf_op jit(solution)/shard_map/psum | solution.py:486
  618.9 0.6 copy.60
  619.5 0.6 fusion
  620.1 2.8 bitcast_convert_fusion.3
  622.9 25.4 %all-gather.5.cloned.1.call-done = bf16[768,2304]{1,0:T(8,128)(2,1)} async-done(((bf16[48,2304]{1,0:T(8,128)(2,1)}), bf16[768,2304]{1,0:T(8,128)(2,1)}) %all-gather.5.cloned.1.call-update) | async-done | bytes 3538960 | tf_op jit(solution)/shard_map/all_gather | solution.py:453
  648.3 5.5 bitcast_convert_fusion.2
  653.8 49.2 %all-gather.11.cloned.1.call-done = bf16[3072,768]{1,0:T(8,128)(2,1)} async-done(((bf16[192,768]{1,0:T(8,128)(2,1)}), bf16[3072,768]{1,0:T(8,128)(2,1)}) %all-gather.11.cloned.1.call-update) | async-done | bytes 4718608 | tf_op jit(solution)/shard_map/all_gather | solution.py:453
  703.0 6.8 bitcast_convert_fusion
  709.8 47.4 %all-gather.9.cloned.1.call-done = bf16[768,3072]{1,0:T(8,128)(2,1)} async-done(((bf16[48,3072]{1,0:T(8,128)(2,1)}), bf16[768,3072]{1,0:T(8,128)(2,1)}) %all-gather.9.cloned.1.call-update) | async-done | bytes 4718608 | tf_op jit(solution)/shard_map/all_gather | solution.py:453
  757.3 7.4 bitcast_convert_fusion.1
  (9 shorter events, 0.0 us)
Async XLA Ops:
  7.2 323.8 %reduce-scatter.7.cloned.1.call-start = ((), (), s32[]{:S(2)}) async-start(), calls=%async_computation.6 | async-start | bytes 1253376 | tf_op jit(solution)/shard_map/reduce_scatter | solution.py:452
  48.2 19.3 %collective-permute-start = (bf16[512,768]{1,0:T(8,128)(2,1)}, bf16[512,768]{1,0:T(8,128)(2,1)S(1)}, u32[]{:S(2)}, u32[]{:S(2)}) collective-permute-start(bf16[512,768]{1,0:T(8,128)(2,1)} %get-tuple-element.69), channel_id=1, source_target_pairs={{0,16},{1,17},{2,18},{3,19},{4,20},{5,21},{6,22},{7,23},{8,24},{9,... | collective-permute-start | bytes 2359304 | tf_op jit(solution)/shard_map/ppermute | solution.py:469
  67.5 0.9 copy-start.7
  68.4 35.5 %copy-start.2 = (bf16[1024,768]{1,0:T(8,128)(2,1)S(1)}, bf16[1024,768]{1,0:T(8,128)(2,1)}, u32[]{:S(2)}) copy-start(bf16[1024,768]{1,0:T(8,128)(2,1)} %refs_0_.11) | copy-start | bytes 4718596
  98.2 22.8 %collective-permute-start.1 = (bf16[512,768]{1,0:T(8,128)(2,1)}, bf16[512,768]{1,0:T(8,128)(2,1)S(1)}, u32[]{:S(2)}, u32[]{:S(2)}) collective-permute-start(bf16[512,768]{1,0:T(8,128)(2,1)} %get-tuple-element.82), channel_id=1, source_target_pairs={{0,16},{1,17},{2,18},{3,19},{4,20},{5,21},{6,22},{7,23},{8,24},{9,... | collective-permute-start | bytes 2359304 | tf_op jit(solution)/shard_map/ppermute | solution.py:469
  120.9 0.9 copy-start.6
  123.9 74.0 %collective-permute-start.2 = (bf16[512,768]{1,0:T(8,128)(2,1)}, bf16[512,768]{1,0:T(8,128)(2,1)S(1)}, u32[]{:S(2)}, u32[]{:S(2)}) collective-permute-start(bf16[512,768]{1,0:T(8,128)(2,1)} %get-tuple-element.106), channel_id=1, source_target_pairs={{16,0},{17,1},{18,2},{19,3},{20,4},{21,5},{22,6},{23,7},{24,8},{25... | collective-permute-start | bytes 2359304 | tf_op jit(solution)/shard_map/ppermute | solution.py:478
  197.9 0.9 copy-start.9
  223.6 19.9 %collective-permute-start.3 = (bf16[512,768]{1,0:T(8,128)(2,1)}, bf16[512,768]{1,0:T(8,128)(2,1)S(1)}, u32[]{:S(2)}, u32[]{:S(2)}) collective-permute-start(bf16[512,768]{1,0:T(8,128)(2,1)} %get-tuple-element.113), channel_id=1, source_target_pairs={{16,0},{17,1},{18,2},{19,3},{20,4},{21,5},{22,6},{23,7},{24,8},{25... | collective-permute-start | bytes 2359304 | tf_op jit(solution)/shard_map/ppermute | solution.py:478
  243.5 0.9 copy-start.8
  244.4 25.1 %copy-start = (bf16[1024,768]{1,0:T(8,128)(2,1)S(1)}, bf16[1024,768]{1,0:T(8,128)(2,1)}, u32[]{:S(2)}) copy-start(bf16[1024,768]{1,0:T(8,128)(2,1)} %get-tuple-element.98.refs_10_) | copy-start | bytes 4718596
  269.5 4.2 copy-start.3
  273.5 128.5 %reduce-scatter.5.cloned.1.call-start = ((), (), s32[]{:S(2)}) async-start(), calls=%async_computation.4 | async-start | bytes 3760128 | tf_op jit(solution)/shard_map/reduce_scatter | solution.py:452
  281.4 1.4 copy-start.4
  281.4 199.5 %reduce-scatter.11.cloned.1.call-start = ((), (), s32[]{:S(2)}) async-start(), calls=%async_computation.10 | async-start | bytes 5013504 | tf_op jit(solution)/shard_map/reduce_scatter | solution.py:452
  292.6 1.4 copy-start.1
  292.6 267.7 %reduce-scatter.9.cloned.1.call-start = ((), (), s32[]{:S(2)}) async-start(), calls=%async_computation.8 | async-start | bytes 5013504 | tf_op jit(solution)/shard_map/reduce_scatter | solution.py:452
  303.5 256.8 %copy-start.5 = (f32[2,16,768]{2,1,0:T(8,128)S(1)}, f32[2,16,768]{2,1,0:T(8,128)}, u32[]{:S(2)}) copy-start(f32[2,16,768]{2,1,0:T(8,128)} %get-tuple-element.123) | copy-start | bytes 294916
  303.5 316.6 %all-gather.7.cloned.1.call-start = ((), (), s32[]{:S(2)}) async-start(), calls=%async_computation.7 | async-start | bytes 1253376 | tf_op jit(solution)/shard_map/all_gather | solution.py:453
  331.0 317.3 %all-gather.5.cloned.1.call-start = ((), (), s32[]{:S(2)}) async-start(), calls=%async_computation.5 | async-start | bytes 3760128 | tf_op jit(solution)/shard_map/all_gather | solution.py:453
  402.0 301.0 %all-gather.11.cloned.1.call-start = ((), (), s32[]{:S(2)}) async-start(), calls=%async_computation.11 | async-start | bytes 5013504 | tf_op jit(solution)/shard_map/all_gather | solution.py:453
  480.9 276.4 %all-gather.9.cloned.1.call-start = ((), (), s32[]{:S(2)}) async-start(), calls=%async_computation.9 | async-start | bytes 5013504 | tf_op jit(solution)/shard_map/all_gather | solution.py:453
Sparse Core Ops, SparseCore 0:
  273.6 57.3 reduce-scatter.6
  334.9 67.0 reduce-scatter.4
  406.4 74.4 reduce-scatter.10
  485.6 74.5 reduce-scatter.8
  562.4 37.6 all-gather.6
  602.2 46.0 all-gather.4
  650.6 52.3 all-gather.10
  705.3 51.9 all-gather.8

commit v2 on v1

--- a/solution.py
+++ b/solution.py
@@ -448,9 +448,459 @@
     return result[0], list(result[1:])
 
 
-def reduced(value, dim):
-    share = lax.psum_scatter(value.astype(BF16), "dp", scatter_dimension=dim, tiled=True)
-    return lax.all_gather(share, "dp", axis=dim, tiled=True).astype(F32)[None]
+UNIT = 16
+RAIL = 4 * UNIT
+ROOTS = 4
+HALF = 2 * RAIL + ROOTS * UNIT
+SLAB = 2 * HALF
+MESH = pl.DeviceIdType.MESH
+
+
+def reduce_kernel(depth, *refs):
+    (gelu, d_down, low, d_up, ctx, d_attn, hid, d_qkv, small) = refs[:9]
+    (o_down, o_up, o_out, o_qkv, o_small) = refs[9:14]
+    (
+        left_v, right_v, p_v, s_v, y_v, rl_v, rr_v, o_v, sm_v, sm_in_v, sm_o_v,
+        load_sem, send_sem, recv_sem, out_sem, sm_send, sm_recv,
+    ) = refs[14:]
+    columns = d_down.shape[1]
+    plan = (
+        ("down", FF // SLAB, gelu, d_down, o_down),
+        ("up", 2 * (FF // D), low, d_up, o_up),
+        ("out", 2, ctx, d_attn, o_out),
+        ("qkv", 6, hid, d_qkv, o_qkv),
+    )
+    count = sum(entry[1] for entry in plan)
+    section = lax.axis_index("section")
+    me = lax.axis_index("dp")
+    core = lax.rem(me, 2)
+    y = lax.rem(lax.div(me, 2), 2)
+    z = lax.div(me, 4)
+    sibling = (section, me + 1 - 2 * core)
+    partner = (section, me + 2 - 4 * y)
+    left = (section, me - 4)
+    right = (section, me + 4)
+
+    barrier = pltpu.get_barrier_semaphore()
+    pl.semaphore_signal(barrier, inc=1, device_id=sibling, device_id_type=MESH)
+    pl.semaphore_signal(barrier, inc=1, device_id=partner, device_id_type=MESH)
+
+    @pl.when(z > 0)
+    def _():
+        pl.semaphore_signal(barrier, inc=1, device_id=left, device_id_type=MESH)
+
+    @pl.when(z < depth - 1)
+    def _():
+        pl.semaphore_signal(barrier, inc=1, device_id=right, device_id_type=MESH)
+
+    def at(value, size):
+        return pl.ds(pl.multiple_of(value, UNIT), size)
+
+    def load(step, start):
+        slot = lax.rem(step, 2)
+        if not start:
+            pltpu.make_async_copy(gelu.at[:, pl.ds(0, SLAB)], left_v.at[slot], load_sem.at[0, slot]).wait()
+            pltpu.make_async_copy(d_down, right_v.at[slot], load_sem.at[1, slot]).wait()
+            return
+        first = 0
+        for name, steps, factor, grad, _ in plan:
+
+            def issue(first=first, name=name, factor=factor, grad=grad):
+                index = step - first
+                if name == "down":
+                    row, column = index, 0
+                else:
+                    row, column = lax.rem(index, 2), lax.div(index, 2)
+                rows = pl.ds(pl.multiple_of(row * SLAB, 128), SLAB)
+                cols = pl.ds(pl.multiple_of(column * columns, 128), columns)
+                pltpu.make_async_copy(factor.at[:, rows], left_v.at[slot], load_sem.at[0, slot]).start()
+                pltpu.make_async_copy(grad.at[:, cols], right_v.at[slot], load_sem.at[1, slot]).start()
+
+            pl.when((step >= first) & (step < first + steps))(issue)
+            first += steps
+
+    def out_copy(step, start):
+        slot = lax.rem(step, 2)
+        if not start:
+            pltpu.make_async_copy(o_v.at[0], o_down.at[pl.ds(0, SLAB)], out_sem.at[slot]).wait()
+            return
+        first = 0
+        for name, steps, _, _, result in plan:
+
+            def issue(first=first, name=name, result=result):
+                index = step - first
+                if name == "down":
+                    row, column = index, 0
+                else:
+                    row, column = lax.rem(index, 2), lax.div(index, 2)
+                cols = pl.ds(pl.multiple_of(column * columns, 128), columns)
+                pltpu.make_async_copy(o_v.at[step], result.at[at(row * SLAB, SLAB), cols], out_sem.at[slot]).start()
+
+            pl.when((step >= first) & (step < first + steps))(issue)
+            first += steps
+
+    def send(kind, step, source, target, arrival, device, compute=None):
+        parity = lax.rem(step, 2)
+        copy = pltpu.make_async_remote_copy(
+            source, target, send_sem.at[kind, parity], arrival, device_id=device, device_id_type=MESH
+        )
+
+        @pl.when(step >= 2)
+        def _():
+            copy.wait_send()
+
+        if compute is not None:
+            compute()
+        copy.start()
+
+    def finish_send(kind, view):
+        for parity in range(2):
+            pltpu.make_async_remote_copy(
+                view, view, send_sem.at[kind, parity], recv_sem.at[kind, 0], device_id=sibling, device_id_type=MESH
+            ).wait_send()
+
+    def arrived(kind, step, view):
+        pltpu.make_async_remote_copy(
+            view, view, send_sem.at[kind, 0], recv_sem.at[kind, step], device_id=sibling, device_id_type=MESH
+        ).wait_recv()
+
+    own = core * HALF
+    theirs = HALF - own
+    CX, UP, DOWN, SIB_OTHER, YX = range(5)
+
+    def add_into(target, term):
+        target[...] = (target[...].astype(F32) + term[...].astype(F32)).astype(target.dtype)
+
+    class Tree:
+        def __init__(self, kinds, base, root, reach, size, offset, land, rail):
+            self.kinds, self.base, self.root, self.reach = kinds, base, root, reach
+            self.size, self.offset, self.land, self.rail = size, offset, land, rail
+            self.distance = jnp.abs(z - root)
+            self.from_left = (z > 0) & (z <= root)
+            self.from_right = (z < depth - 1) & (z >= root)
+
+        def part(self, step):
+            return s_v.at[step, at(self.offset, self.size)]
+
+        def total(self, step):
+            return o_v.at[step, at(own + self.offset, self.size)]
+
+        def landing(self, buffer, step):
+            return buffer.at[step, pl.ds(self.land, self.size)]
+
+        def towards(self, now):
+            inward, out_left, out_right, sib = self.kinds
+            step = now - self.base - self.reach + self.distance
+
+            @pl.when((step >= 0) & (step < count))
+            def _():
+                @pl.when(self.from_left)
+                def _():
+                    arrived(out_left, step, self.landing(rl_v, step))
+                    add_into(self.part(step), self.landing(rl_v, step))
+
+                @pl.when(self.from_right)
+                def _():
+                    arrived(out_right, step, self.landing(rr_v, step))
+                    add_into(self.part(step), self.landing(rr_v, step))
+
+                @pl.when(z < self.root)
+                def _():
+                    send(inward, step, self.part(step), self.landing(rl_v, step), recv_sem.at[out_left, step], right)
+
+                @pl.when(z > self.root)
+                def _():
+                    send(inward, step, self.part(step), self.landing(rr_v, step), recv_sem.at[out_right, step], left)
+
+                @pl.when(z == self.root)
+                def _():
+                    if self.rail:
+                        self.total(step)[...] = self.part(step)[...]
+                    else:
+                        view = y_v.at[step, pl.ds(RAIL, UNIT)]
+                        send(YX, step, self.part(step), view, recv_sem.at[YX, step], partner)
+
+            if not self.rail:
+                late = now - self.base - self.reach - 1
+
+                @pl.when((z == self.root) & (late >= 0) & (late < count))
+                def _():
+                    view = y_v.at[late, pl.ds(RAIL, UNIT)]
+                    arrived(YX, late, view)
+                    self.total(late)[...] = (self.part(late)[...].astype(F32) + view[...].astype(F32)).astype(BF16)
+
+        def away(self, now):
+            inward, out_left, out_right, sib = self.kinds
+            lag = self.base + self.reach + (0 if self.rail else 1)
+            step = now - lag - self.distance
+
+            @pl.when((step >= 0) & (step < count))
+            def _():
+                view = self.total(step)
+
+                @pl.when(z != self.root)
+                def _():
+                    arrived(inward, step, view)
+
+                @pl.when(self.from_left)
+                def _():
+                    send(out_left, step, view, view, recv_sem.at[inward, step], left)
+
+                @pl.when(self.from_right)
+                def _():
+                    send(out_right, step, view, view, recv_sem.at[inward, step], right)
+
+                if self.rail:
+                    send(DOWN, step, view, view, recv_sem.at[DOWN, step], partner)
+                send(sib, step, view, view, recv_sem.at[sib, step], sibling)
+
+            done = step - 1
+
+            @pl.when((done >= 0) & (done < count))
+            def _():
+                arrived(sib, done, o_v.at[done, at(theirs + self.offset, self.size)])
+
+        def finish(self):
+            inward, out_left, out_right, sib = self.kinds
+            view = self.part(0)
+
+            @pl.when(z != self.root)
+            def _():
+                finish_send(inward, view)
+
+            @pl.when(self.from_left)
+            def _():
+                finish_send(out_left, view)
+
+            @pl.when(self.from_right)
+            def _():
+                finish_send(out_right, view)
+
+            finish_send(sib, view)
+            if not self.rail:
+
+                @pl.when(z == self.root)
+                def _():
+                    finish_send(YX, view)
+
+    half_depth = depth // 2
+    rail_root = half_depth - 1 + y
+    rail = Tree((5, 6, 7, 8), 2, rail_root, half_depth, RAIL, y * RAIL, 0, True)
+    line = []
+    for index in range(ROOTS):
+        root = (2 * index + 1) * depth // (2 * ROOTS)
+        kinds = tuple(9 + 4 * index + offset for offset in range(4))
+        reach = max(root, depth - 1 - root)
+        line.append(Tree(kinds, 1, root, reach, UNIT, 2 * RAIL + index * UNIT, RAIL + index * UNIT, False))
+    other_distance = jnp.abs(z - (half_depth - y))
+    other = (1 - y) * RAIL
+
+    sm_root = half_depth
+    sm_reach = max(sm_root, depth - 1 - sm_root)
+    sm_distance = jnp.abs(z - sm_root)
+
+    def sm_copy(kind, source, target, arrival, device):
+        return pltpu.make_async_remote_copy(
+            source, target, sm_send.at[kind], sm_recv.at[arrival], device_id=device, device_id_type=MESH
+        )
+
+    def small_round(now):
+        @pl.when(now == 0)
+        def _():
+            sm_v[...] = small[0] + small[1]
+            sm_copy(0, sm_v, sm_in_v.at[0], 0, sibling).start()
+
+        @pl.when(now == 1)
+        def _():
+            sm_copy(0, sm_v, sm_in_v.at[0], 0, sibling).wait()
+            sm_v[...] = sm_v[...] + sm_in_v[0]
+
+        @pl.when(now == 1 + sm_reach - sm_distance)
+        def _():
+            @pl.when((z > 0) & (z <= sm_root))
+            def _():
+                sm_copy(1, sm_v, sm_in_v.at[1], 1, sibling).wait_recv()
+                sm_v[...] = sm_v[...] + sm_in_v[1]
+
+            @pl.when((z < depth - 1) & (z >= sm_root))
+            def _():
+                sm_copy(1, sm_v, sm_in_v.at[2], 2, sibling).wait_recv()
+                sm_v[...] = sm_v[...] + sm_in_v[2]
+
+            @pl.when(z < sm_root)
+            def _():
+                sm_copy(1, sm_v, sm_in_v.at[1], 1, right).start()
+
+            @pl.when(z > sm_root)
+            def _():
+                sm_copy(1, sm_v, sm_in_v.at[2], 2, left).start()
+
+            @pl.when(z == sm_root)
+            def _():
+                sm_copy(1, sm_v, sm_in_v.at[3], 3, partner).start()
+
+        @pl.when((now == 2 + sm_reach) & (z == sm_root))
+        def _():
+            sm_copy(1, sm_v, sm_in_v.at[3], 3, partner).wait_recv()
+            sm_o_v[...] = sm_v[...] + sm_in_v[3]
+
+        @pl.when(now == 2 + sm_reach + sm_distance)
+        def _():
+            @pl.when(z != sm_root)
+            def _():
+                sm_copy(2, sm_o_v, sm_o_v, 4, sibling).wait_recv()
+
+            @pl.when((z > 0) & (z <= sm_root))
+            def _():
+                sm_copy(2, sm_o_v, sm_o_v, 4, left).start()
+
+            @pl.when((z < depth - 1) & (z >= sm_root))
+            def _():
+                sm_copy(3, sm_o_v, sm_o_v, 4, right).start()
+
+    def small_finish():
+        sm_copy(1, sm_v, sm_in_v.at[1], 1, sibling).wait_send()
+
+        @pl.when((z > 0) & (z <= sm_root))
+        def _():
+            sm_copy(2, sm_o_v, sm_o_v, 4, left).wait_send()
+
+        @pl.when((z < depth - 1) & (z >= sm_root))
+        def _():
+            sm_copy(3, sm_o_v, sm_o_v, 4, right).wait_send()
+
+        o_small[...] = sm_o_v[...]
+
+    load(jnp.int32(0), True)
+    neighbours = 2 + (z > 0).astype(jnp.int32) + (z < depth - 1).astype(jnp.int32)
+    pl.semaphore_wait(barrier, neighbours)
+
+    out_lag = max(
+        [2 + half_depth + half_depth + 2] + [2 + tree.reach + max(tree.root, depth - 1 - tree.root) + 1 for tree in line]
+    )
+
+    def one_round(now, carry):
+        slot = lax.rem(now, 2)
+
+        @pl.when(now < count)
+        def _():
+            load(now, False)
+
+            @pl.when(now + 1 < count)
+            def _():
+                load(now + 1, True)
+
+            def form():
+                p_v[slot] = dot_tn(left_v[slot], right_v[slot]).astype(BF16)
+
+            view = p_v.at[slot, at(theirs, HALF)]
+            send(CX, now, view, s_v.at[now], recv_sem.at[CX, now], sibling, form)
+
+        step = now - 1
+
+        @pl.when((step >= 0) & (step < count))
+        def _():
+            arrived(CX, step, s_v.at[step])
+            add_into(s_v.at[step], p_v.at[1 - slot, at(own, HALF)])
+            view = s_v.at[step, at(other, RAIL)]
+            send(UP, step, view, y_v.at[step, pl.ds(0, RAIL)], recv_sem.at[UP, step], partner)
+
+        for tree in line:
+            tree.towards(now)
+
+        step_up = now - 2
+
+        @pl.when((step_up >= 0) & (step_up < count))
+        def _():
+            view = y_v.at[step_up, pl.ds(0, RAIL)]
+            arrived(UP, step_up, view)
+            add_into(rail.part(step_up), view)
+
+        rail.towards(now)
+        rail.away(now)
+        for tree in line:
+            tree.away(now)
+
+        step_down = now - 2 - half_depth - other_distance - 1
+
+        @pl.when((step_down >= 0) & (step_down < count))
+        def _():
+            view = o_v.at[step_down, at(own + other, RAIL)]
+            arrived(DOWN, step_down, view)
+            send(SIB_OTHER, step_down, view, view, recv_sem.at[SIB_OTHER, step_down], sibling)
+
+        step_sib = step_down - 1
+
+        @pl.when((step_sib >= 0) & (step_sib < count))
+        def _():
+            arrived(SIB_OTHER, step_sib, o_v.at[step_sib, at(theirs + other, RAIL)])
+
+        small_round(now)
+
+        step_out = now - out_lag
+
+        @pl.when(step_out >= 0)
+        def _():
+            @pl.when(step_out >= 2)
+            def _():
+                out_copy(step_out, False)
+
+            out_copy(step_out, True)
+
+        return carry
+
+    lax.fori_loop(0, count + out_lag, one_round, 0)
+    out_copy(jnp.int32(0), False)
+    out_copy(jnp.int32(1), False)
+    finish_send(CX, s_v.at[0])
+    finish_send(UP, rail.part(0))
+    finish_send(DOWN, rail.part(0))
+    finish_send(SIB_OTHER, rail.part(0))
+    rail.finish()
+    for tree in line:
+        tree.finish()
+    small_finish()
+
+
+def reduce_gradients(depth, gelu, d_down, low, d_up, ctx, d_attn, hid, d_qkv, small):
+    rows, columns = d_down.shape
+    count = FF // SLAB + 2 * (FF // D) + 8
+    kinds = 9 + 4 * ROOTS
+    return pl.pallas_call(
+        functools.partial(reduce_kernel, depth),
+        out_shape=[
+            jax.ShapeDtypeStruct((FF, columns), BF16),
+            jax.ShapeDtypeStruct((D, 4 * columns), BF16),
+            jax.ShapeDtypeStruct((D, columns), BF16),
+            jax.ShapeDtypeStruct((D, 3 * columns), BF16),
+            jax.ShapeDtypeStruct((SMALL_ROWS, small.shape[-1]), F32),
+        ],
+        in_specs=[ANY] * 8 + [VMEM],
+        out_specs=[ANY] * 4 + [VMEM],
+        scratch_shapes=[
+            pltpu.VMEM((2, rows, SLAB), BF16),
+            pltpu.VMEM((2, rows, columns), BF16),
+            pltpu.VMEM((2, SLAB, columns), BF16),
+            pltpu.VMEM((count, HALF, columns), BF16),
+            pltpu.VMEM((count, RAIL + UNIT, columns), BF16),
+            pltpu.VMEM((count, RAIL + ROOTS * UNIT, columns), BF16),
+            pltpu.VMEM((count, RAIL + ROOTS * UNIT, columns), BF16),
+            pltpu.VMEM((count, SLAB, columns), BF16),
+            pltpu.VMEM((SMALL_ROWS, small.shape[-1]), F32),
+            pltpu.VMEM((4, SMALL_ROWS, small.shape[-1]), F32),
+            pltpu.VMEM((SMALL_ROWS, small.shape[-1]), F32),
+            pltpu.SemaphoreType.DMA((2, 2)),
+            pltpu.SemaphoreType.DMA((kinds, 2)),
+            pltpu.SemaphoreType.DMA((kinds, count)),
+            pltpu.SemaphoreType.DMA((2,)),
+            pltpu.SemaphoreType.DMA((4,)),
+            pltpu.SemaphoreType.DMA((5,)),
+        ],
+        compiler_params=pltpu.CompilerParams(
+            collective_id=0, has_side_effects=True, vmem_limit_bytes=VMEM_LIMIT
+        ),
+        name="reduce_gradients",
+    )(gelu, d_down, low, d_up, ctx, d_attn, hid, d_qkv, small)
 
 
 def shards(
@@ -476,14 +926,13 @@
         hop, grads = backward(step, cotangent, received, weights, norm_gains, prob, saved, grads)
         if step < MICRO:
             received = lax.ppermute(hop, "section", back)
-    small = jnp.sum(grads[0], axis=0)
     d_down, d_up, d_attn, d_qkv, d_hid = grads[1:]
-    names = {name: index for index, (name, _, _) in enumerate(SAVED)}
-    g_down = reduced(dot_tn(saved[names["gelu"]], d_down), 0)
-    g_up = reduced(dot_tn(saved[names["low"]], d_up), 0)
-    g_out = reduced(dot_tn(saved[names["ctx"]], d_attn), 0)
-    g_qkv = reduced(dot_tn(hid, d_qkv), 0)
-    small = lax.psum(small, "dp")[None]
+    kept = dict(zip([name for name, _, _ in SAVED], saved))
+    *large, small = reduce_gradients(
+        lax.axis_size("dp") // 4, kept["gelu"], d_down, kept["low"], d_up, kept["ctx"], d_attn, hid, d_qkv, grads[0]
+    )
+    g_down, g_up, g_out, g_qkv = [value.astype(F32)[None] for value in large]
+    small = small[None]
     return (
         act[None], d_hid[None], g_qkv, small[:, 0:2], g_out, small[:, 2:4], small[:, 4:6], small[:, 6:8],
         g_up, small[:, 8:12].reshape(1, FF), g_down,

time: 777 us -> 436 us (0.56)
  waiting for transfers between devices: 504 us -> 126 us
  Pallas kernels: 121 us -> 267 us
  blocking collectives: 58.5 us -> 0 us
  matrix products: 30.9 us -> 0 us
  between operations: 14.5 us -> 0.98 us
    reduce_scatter x4 -> x0, waiting for transfers between devices: 256 us -> none  [reduced(): lax.psum_scatter(value.astype(BF16), 'dp', scatter_dimension=dim, tiled=T...]
    pallas_call x0 -> x1, Pallas kernels: none -> 146 us  [reduce_gradients(): pl.pallas_call(functools.partial(reduce_kernel, depth), out_shape=[jax.Sh...]
    all_gather x4 -> x0, waiting for transfers between devices: 122 us -> none  [reduced(): return lax.all_gather(share, 'dp', axis=dim, tiled=True).astype(F32)[None]]
    psum x1 -> x0, blocking collectives: 58.5 us -> none  [shards(): small = lax.psum(small, 'dp')[None]]
    dot_general x4 -> x0, matrix products: 30.9 us -> none  [dot_tn(): lax.dot_general(left, right, (((0,), (0,)), ((), ())), preferred_element_...]
  transfers between devices with their start and end apart: 12 -> 4, of which waited for: 11 -> 4; matrix products, arithmetic and copies ran while one was open for 6% -> 0% of each run, Pallas kernels for 0% -> 0%
where the time goes in v2:
time: 436 us; the launch traced here: 430 us
  Pallas kernels  267 us (61%)
  waiting for transfers between devices  126 us (29%)
  other arithmetic  17.1 us (4%)
  starting transfers between devices  9.72 us (2%)
  local copies, waits for them, and re-layouts  9.46 us (2%)
    pallas_call x1, Pallas kernels, reduce_gradients(): pl.pallas_call(functools.partial(reduce_kernel, depth), out_shape=[jax.Sh...  146 us
    ppermute x2, waiting for transfers between devices, shards(): received = lax.ppermute(hop, 'section', back)  91.5 us
    pallas_call x3, Pallas kernels, forward(): pl.pallas_call(functools.partial(forward_kernel, step, n_alias), out_shap...  69.9 us
    pallas_call x3, Pallas kernels, backward(): pl.pallas_call(functools.partial(backward_kernel, step, n_alias), out_sha...  50.6 us
    ppermute x2, waiting for transfers between devices, shards(): received = lax.ppermute(hop, 'section', onward)  34.1 us
    broadcast_in_dim x4, other arithmetic, shards(): g_down, g_up, g_out, g_qkv = [value.astype(F32)[None] for value in large]  17.1 us
  transfers between devices with their start and end apart: 4, of which 4 were waited for; matrix products, arithmetic and copies ran while one was open for 0% of the time, Pallas kernels for 0%

profile of v2, /device:TPU:0, one launch (start us, length us, event | category | flops | bytes accessed | tf_op | source)
XLA Modules:
  0.0 429.6 jit_solution(11071076496779094918)
XLA Ops:
  0.6 2.1 slice.21.refs_1_
  2.7 29.6 %forward.3 = (bf16[512,768]{1,0:T(8,128)(2,1)}, bf16[1024,768]{1,0:T(8,128)(2,1)}, bf16[2,12,512,512]{3,2,1,0:T(8,128)(2,1)}, bf16[1024,768]{1,0:T(8,128)(2,1)},...) custom-call(bf16[1024,768]{1,0:T(8,128)(2,1)} %refs_0_.8, ...), custom_call_target="tpu_custom_call" | custom-call | tf_op jit(solution)/shard_map/forward/pallas_call | solution.py:229
  32.3 1.3 collective-permute-start
  33.6 18.0 %collective-permute-done.refs_1_ = bf16[512,768]{1,0:T(8,128)(2,1)S(1)} collective-permute-done((bf16[512,768]{1,0:T(8,128)(2,1)}, bf16[512,768]{1,0:T(8,128)(2,1)S(1)}, u32[]{:S(2)}, u32[]{:S(2)}) %collective-permute-start) | collective-permute-done | bytes 786464 | tf_op jit(solution)/shard_map/ppermute | solution.py:919
  51.6 0.0 copy-start.5
  51.6 0.9 copy-done.5
  52.5 0.0 copy-start
  52.5 39.1 %forward.4 = (bf16[512,768]{1,0:T(8,128)(2,1)}, bf16[1024,768]{1,0:T(8,128)(2,1)}, bf16[2,12,512,512]{3,2,1,0:T(8,128)(2,1)}, bf16[1024,768]{1,0:T(8,128)(2,1)},...) custom-call(bf16[1024,768]{1,0:T(8,128)(2,1)} %refs_0_.8, ...), custom_call_target="tpu_custom_call", output_to_operand_aliasing={{1}: (13, {}), {2}: (14, {}), {3}: (15, {}), {4}: (16, {}),... | custom-call | tf_op jit(solution)/shard_map/forward/pallas_call | solution.py:229
  91.5 5.8 %collective-permute-start.1 = (bf16[512,768]{1,0:T(8,128)(2,1)}, bf16[512,768]{1,0:T(8,128)(2,1)S(1)}, u32[]{:S(2)}, u32[]{:S(2)}) collective-permute-start(bf16[512,768]{1,0:T(8,128)(2,1)} %get-tuple-element.87), channel_id=1, source_target_pairs={{0,16},{1,17},{2,18},{3,19},{4,20},{5,21},{6,22},{7,23},{8,24},{9,... | collective-permute-start | bytes 2359304 | tf_op jit(solution)/shard_map/ppermute | solution.py:919
  97.3 0.0 copy-done
  97.3 1.0 slice.22.refs_1_
  98.3 16.1 %collective-permute-done.1.refs_1_ = bf16[512,768]{1,0:T(8,128)(2,1)S(1)} collective-permute-done((bf16[512,768]{1,0:T(8,128)(2,1)}, bf16[512,768]{1,0:T(8,128)(2,1)S(1)}, u32[]{:S(2)}, u32[]{:S(2)}) %collective-permute-start.1) | collective-permute-done | bytes 786464 | tf_op jit(solution)/shard_map/ppermute | solution.py:919
  114.4 0.0 copy-start.4
  114.4 0.9 copy-done.4
  115.3 1.2 forward.5
  116.6 0.9 backward.3
  117.5 1.3 collective-permute-start.2
  118.8 72.8 %collective-permute-done.2.refs_1_ = bf16[512,768]{1,0:T(8,128)(2,1)S(1)} collective-permute-done((bf16[512,768]{1,0:T(8,128)(2,1)}, bf16[512,768]{1,0:T(8,128)(2,1)S(1)}, u32[]{:S(2)}, u32[]{:S(2)}) %collective-permute-start.2) | collective-permute-done | bytes 786464 | tf_op jit(solution)/shard_map/ppermute | solution.py:928
  191.6 0.0 copy-start.7
  191.6 0.9 copy-done.7
  192.5 25.0 %backward.4 = (bf16[512,768]{1,0:T(8,128)(2,1)}, f32[2,16,768]{2,1,0:T(8,128)}, bf16[1024,768]{1,0:T(8,128)(2,1)}, bf16[1024,3072]{1,0:T(8,128)(2,1)}, bf16[1024...) custom-call(bf16[1024,768]{1,0:T(8,128)(2,1)} %refs_0_.11, ...), custom_call_target="tpu_custom_call", output_to_operand_aliasing={{1}: (18, {}), {2}: (19, {}), {3}: (20, {}), {4}: (21, {}),... | custom-call | tf_op jit(solution)/shard_map/backward/pallas_call | solution.py:419
  217.5 1.3 collective-permute-start.3
  218.8 18.6 %collective-permute-done.3.refs_1_ = bf16[512,768]{1,0:T(8,128)(2,1)S(1)} collective-permute-done((bf16[512,768]{1,0:T(8,128)(2,1)}, bf16[512,768]{1,0:T(8,128)(2,1)S(1)}, u32[]{:S(2)}, u32[]{:S(2)}) %collective-permute-start.3) | collective-permute-done | bytes 786464 | tf_op jit(solution)/shard_map/ppermute | solution.py:928
  237.4 0.0 copy-start.6
  237.4 0.9 copy-done.6
  238.3 24.7 %backward.5 = (bf16[512,768]{1,0:T(8,128)(2,1)}, f32[2,16,768]{2,1,0:T(8,128)}, bf16[1024,768]{1,0:T(8,128)(2,1)}, bf16[1024,3072]{1,0:T(8,128)(2,1)}, bf16[1024...) custom-call(bf16[1024,768]{1,0:T(8,128)(2,1)} %refs_0_.11, ...), custom_call_target="tpu_custom_call", output_to_operand_aliasing={{1}: (18, {}), {2}: (19, {}), {3}: (20, {}), {4}: (21, {}),... | custom-call | tf_op jit(solution)/shard_map/backward/pallas_call | solution.py:419
  263.1 146.3 %reduce_gradients.1 = (bf16[3072,768]{1,0:T(8,128)(2,1)}, bf16[768,3072]{1,0:T(8,128)(2,1)}, bf16[768,768]{1,0:T(8,128)(2,1)}, bf16[768,2304]{1,0:T(8,128)(2,1)}, f32[16,768]{1,0:T(8,128)}) custom-call(bf16[1024,3072]{1,0:T(8,128)(2,1)} %get-tuple-element.107.refs_14_.refs_0_, bf16[1024,768]{1,0:T(8,128)(2,1)} %get-tuple-element.126.refs_1_, ...), custom_call_target="tpu_custom_call" | custom-call | tf_op jit(solution)/shard_map/reduce_gradients/pallas_call | solution.py:869
  409.4 1.5 fusion
  410.9 0.7 slice_bitcast_fusion
  411.6 0.0 copy-start.1
  411.6 7.0 %bitcast_convert_fusion = f32[1,3072,768]{2,1,0:T(8,128)} fusion(bf16[3072,768]{1,0:T(8,128)(2,1)} %get-tuple-element.136), kind=kLoop, calls=%fused_computation | loop fusion | flops 2359296 | bytes 14155776 | tf_op jit(solution)/shard_map/broadcast_in_dim | solution.py:934
  418.6 0.0 copy-done.1
  418.6 0.0 copy-start.2
  418.6 5.0 %bitcast_convert_fusion.1 = f32[1,768,3072]{2,1,0:T(8,128)} fusion(bf16[768,3072]{1,0:T(8,128)(2,1)S(1)} %copy-done.1), kind=kLoop, calls=%fused_computation.1 | loop fusion | flops 2359296 | bytes 14155776 | tf_op jit(solution)/shard_map/broadcast_in_dim | solution.py:934
  423.6 0.0 copy-done.2
  423.7 0.0 copy-start.3
  423.7 3.5 bitcast_convert_fusion.2
  427.1 0.0 copy-done.3
  427.1 1.6 bitcast_convert_fusion.3
  428.7 0.6 copy.60
Async XLA Ops:
  32.3 19.3 %collective-permute-start = (bf16[512,768]{1,0:T(8,128)(2,1)}, bf16[512,768]{1,0:T(8,128)(2,1)S(1)}, u32[]{:S(2)}, u32[]{:S(2)}) collective-permute-start(bf16[512,768]{1,0:T(8,128)(2,1)} %get-tuple-element.74), channel_id=1, source_target_pairs={{0,16},{1,17},{2,18},{3,19},{4,20},{5,21},{6,22},{7,23},{8,24},{9,... | collective-permute-start | bytes 2359304 | tf_op jit(solution)/shard_map/ppermute | solution.py:919
  51.6 0.9 copy-start.5
  52.5 44.9 %copy-start = (bf16[1024,768]{1,0:T(8,128)(2,1)S(1)}, bf16[1024,768]{1,0:T(8,128)(2,1)}, u32[]{:S(2)}) copy-start(bf16[1024,768]{1,0:T(8,128)(2,1)} %refs_0_.11) | copy-start | bytes 4718596
  91.5 22.9 %collective-permute-start.1 = (bf16[512,768]{1,0:T(8,128)(2,1)}, bf16[512,768]{1,0:T(8,128)(2,1)S(1)}, u32[]{:S(2)}, u32[]{:S(2)}) collective-permute-start(bf16[512,768]{1,0:T(8,128)(2,1)} %get-tuple-element.87), channel_id=1, source_target_pairs={{0,16},{1,17},{2,18},{3,19},{4,20},{5,21},{6,22},{7,23},{8,24},{9,... | collective-permute-start | bytes 2359304 | tf_op jit(solution)/shard_map/ppermute | solution.py:919
  114.4 0.9 copy-start.4
  117.5 74.1 %collective-permute-start.2 = (bf16[512,768]{1,0:T(8,128)(2,1)}, bf16[512,768]{1,0:T(8,128)(2,1)S(1)}, u32[]{:S(2)}, u32[]{:S(2)}) collective-permute-start(bf16[512,768]{1,0:T(8,128)(2,1)} %get-tuple-element.111), channel_id=1, source_target_pairs={{16,0},{17,1},{18,2},{19,3},{20,4},{21,5},{22,6},{23,7},{24,8},{25... | collective-permute-start | bytes 2359304 | tf_op jit(solution)/shard_map/ppermute | solution.py:928
  191.6 0.9 copy-start.7
  217.5 19.9 %collective-permute-start.3 = (bf16[512,768]{1,0:T(8,128)(2,1)}, bf16[512,768]{1,0:T(8,128)(2,1)S(1)}, u32[]{:S(2)}, u32[]{:S(2)}) collective-permute-start(bf16[512,768]{1,0:T(8,128)(2,1)} %get-tuple-element.118), channel_id=1, source_target_pairs={{16,0},{17,1},{18,2},{19,3},{20,4},{21,5},{22,6},{23,7},{24,8},{25... | collective-permute-start | bytes 2359304 | tf_op jit(solution)/shard_map/ppermute | solution.py:928
  237.4 0.9 copy-start.6
  411.6 7.0 %copy-start.1 = (bf16[768,3072]{1,0:T(8,128)(2,1)S(1)}, bf16[768,3072]{1,0:T(8,128)(2,1)}, u32[]{:S(2)}) copy-start(bf16[768,3072]{1,0:T(8,128)(2,1)} %get-tuple-element.135) | copy-start | bytes 14155780
  418.6 5.1 %copy-start.2 = (bf16[768,2304]{1,0:T(8,128)(2,1)S(1)}, bf16[768,2304]{1,0:T(8,128)(2,1)}, u32[]{:S(2)}) copy-start(bf16[768,2304]{1,0:T(8,128)(2,1)} %get-tuple-element.132) | copy-start | bytes 10616836
  423.7 3.5 copy-start.3

commit v3 on v2

--- a/solution.py
+++ b/solution.py
@@ -23,6 +23,7 @@
 F32 = jnp.float32
 BF16 = jnp.bfloat16
 VMEM_LIMIT = 60 << 20
+MESH = pl.DeviceIdType.MESH
 
 ANY = pl.BlockSpec(memory_space=pl.ANY)
 VMEM = pl.BlockSpec(memory_space=pltpu.VMEM)
@@ -48,16 +49,9 @@
 
 
 def gelu_and_slope(u):
-    size = jnp.abs(u)
-    bell = jnp.exp(-0.5 * (u * u))
-    t = 1.0 / (1.0 + (0.3275911 / math.sqrt(2.0)) * size)
-    poly = t * (
-        0.5 * 0.254829592
-        + t * (-0.5 * 0.284496736 + t * (0.5 * 1.421413741 + t * (-0.5 * 1.453152027 + t * (0.5 * 1.061405429))))
-    )
-    tail = poly * bell
-    cdf = jnp.where(u < 0.0, tail, 1.0 - tail)
-    return u * cdf, cdf + u * bell * (1.0 / math.sqrt(2.0 * math.pi))
+    normal_cdf = 0.5 + 0.5 * lax.erf(u * (1.0 / math.sqrt(2.0)))
+    bell = jnp.exp((-0.5 * u) * u)
+    return u * normal_cdf, normal_cdf + (u * (1.0 / math.sqrt(2.0 * math.pi))) * bell
 
 
 def normalize(resid):
@@ -80,9 +74,11 @@
     return ((lane // HD) == which).astype(F32).astype(BF16)
 
 
+ROWS = SEQ // 2
 SAVED = (
-    ("act", D, BF16),
-    ("qkv", 3 * D, BF16),
+    ("hid", D, BF16),
+    ("q", D, BF16),
+    ("linv", D, F32),
     ("ctx", D, BF16),
     ("xh1", D, BF16),
     ("inv1", 128, F32),
@@ -92,107 +88,234 @@
     ("xh2", D, BF16),
     ("inv2", 128, F32),
 )
-
-
-def forward_kernel(step, n_alias, *refs):
-    (tok, rec, wqkv, wo, wu, wd, segs, lens, qv_bias, out_biases, gains, shifts, up_bias) = refs[:13]
-    outs = refs[13 + n_alias : 13 + n_alias + 13]
-    y_hop, hid_out, prob_out = outs[:3]
-    saved_out = dict(zip([name for name, _, _ in SAVED], outs[3:]))
+GRADS = (("d_down", D, BF16), ("d_up", FF, BF16), ("d_attn", D, BF16), ("d_qkv", 3 * D, BF16))
+SMALL_ROWS = 16
+
+
+class Place:
+    def __init__(self):
+        self.section = lax.axis_index("section")
+        self.me = lax.axis_index("dp")
+        self.core = lax.rem(self.me, 2)
+        self.sibling = (self.section, self.me + 1 - 2 * self.core)
+        self.other_layer = (1 - self.section, self.me)
+        self.own = pl.ds(pl.multiple_of(self.core * ROWS, ROWS), ROWS)
+        self.theirs = pl.ds(pl.multiple_of(ROWS - self.core * ROWS, ROWS), ROWS)
+
+    def greet(self):
+        barrier = pltpu.get_barrier_semaphore()
+        for device in (self.sibling, self.other_layer):
+            pl.semaphore_signal(barrier, inc=1, device_id=device, device_id_type=MESH)
+        pl.semaphore_wait(barrier, 2)
+
+    def is_mine(self, step, sequences):
+        return lax.div(step, sequences) == self.core
+
+
+def remote(source, target, send_sem, recv_sem, device):
+    return pltpu.make_async_remote_copy(source, target, send_sem, recv_sem, device_id=device, device_id_type=MESH)
+
+
+class Rows:
+    def __init__(self, place, sequences, array, steps, local, sent, arrived):
+        self.place, self.sequences, self.array, self.steps = place, sequences, array, steps
+        self.local, self.sent, self.arrived = local, sent, arrived
+
+    def part(self, sequence, core):
+        return self.array.at[pl.ds(pl.multiple_of(sequence * SEQ + core * ROWS, ROWS), ROWS)]
+
+    def spread(self):
+        place = self.place
+        for sequence in range(self.sequences):
+            step = place.core * self.sequences + sequence
+            target = self.steps.at[step]
+            pltpu.make_async_copy(self.part(sequence, place.core), target, self.local.at[sequence]).start()
+            remote(
+                self.part(sequence, 1 - place.core), target, self.sent.at[sequence], self.arrived.at[step], place.sibling
+            ).start()
+
+    def spread_done(self):
+        for sequence in range(self.sequences):
+            view = self.steps.at[0]
+            remote(view, view, self.sent.at[sequence], self.arrived.at[0], self.place.sibling).wait_send()
+
+    def await_step(self, step, spread):
+        mine = spread & self.place.is_mine(step, self.sequences)
+        view = self.steps.at[step]
+
+        @pl.when(mine)
+        def _():
+            pltpu.make_async_copy(view, view, self.local.at[lax.rem(step, self.sequences)]).wait()
+
+        @pl.when(jnp.logical_not(mine))
+        def _():
+            remote(view, view, self.sent.at[0], self.arrived.at[step], self.place.sibling).wait_recv()
+
+    def collect(self, step):
+        sequence = lax.rem(step, self.sequences)
+        target = self.part(sequence, self.place.core)
+        mine = self.place.is_mine(step, self.sequences)
+
+        @pl.when(mine)
+        def _():
+            pltpu.make_async_copy(self.steps.at[step], target, self.local.at[sequence]).start()
+
+        @pl.when(jnp.logical_not(mine))
+        def _():
+            remote(
+                self.steps.at[step], target, self.sent.at[sequence], self.arrived.at[sequence], self.place.sibling
+            ).start()
+
+    def collect_done(self):
+        for sequence in range(self.sequences):
+            view = self.steps.at[0]
+            pltpu.make_async_copy(view, view, self.local.at[sequence]).wait()
+            remote(view, view, self.sent.at[sequence], self.arrived.at[sequence], self.place.sibling).wait()
+
+
+def forward_kernel(sequences, *refs):
+    (tok, wqkv, wo, wu, wd, segs, lens, qv_bias, out_biases, gains, shifts, up_bias) = refs[:12]
+    act_out, kv_out, prob_out = refs[12:15]
+    count = len(SAVED)
+    outs = dict(zip([name for name, _, _ in SAVED], refs[15 : 15 + count]))
     (
-        h_v, wqkv_v, wo_v, wu_v, wd_v, bias_v, p_v, acc_v,
-        act_v, qkv_v, ctx_v, xh1_v, inv1_v, low_v, gelu_v, slope_v, xh2_v, inv2_v,
-        in_sem, w_sem, p_sem, out_sem,
-    ) = refs[13 + n_alias + 13 :]
-    section = lax.axis_index("section")
-    mb = step - section
-
-    @pl.when((mb >= 0) & (mb < MICRO))
+        h_v, act_v, kv_v, p_v, wqkv_v, wo_v, wu_v, wd_v, bias_v, acc_v, seg_own, seg_their,
+        q_v, linv_v, ctx_v, xh1_v, inv1_v, low_v, gelu_v, slope_v, xh2_v, inv2_v,
+        w_sem, save_sem, p_sem, in_local, in_sent, in_arrived, out_local, out_sent, out_arrived,
+        kv_sent, kv_arrived, kv_save, seg_sem, hop_sent, hid_save,
+    ) = refs[15 + count :]
+    place = Place()
+    section = place.section
+    steps = 2 * sequences
+    names = [name for name, _, _ in SAVED]
+    inputs = Rows(place, sequences, tok, h_v, in_local, in_sent, in_arrived)
+    outputs = Rows(place, sequences, act_out, act_v, out_local, out_sent, out_arrived)
+
+    position = lax.broadcasted_iota(jnp.int32, (1, SEQ), 1)
+    for sequence in range(sequences):
+        seg_own[sequence, 0:1, :] = segs[sequence : sequence + 1, :].astype(F32)
+        seg_own[sequence, 1:2, :] = (position < lens[sequence]).astype(F32)
+        seg_own[sequence, 2:8, :] = jnp.zeros((6, SEQ), F32)
+    w_first = [begin(wqkv.at[0, :, pl.ds(block * D, D)], wqkv_v.at[:, pl.ds(block * D, D)], w_sem.at[block]) for block in (1, 2, 0)]
+    place.greet()
+    seg_copy = remote(seg_own, seg_their, seg_sem.at[0], seg_sem.at[1], place.sibling)
+    seg_copy.start()
+
+    @pl.when(section == 0)
     def _():
-        rows = pl.ds(pl.multiple_of(mb * SEQ, SEQ), SEQ)
-
-        @pl.when(section == 0)
-        def _():
-            begin(tok.at[rows], h_v, in_sem.at[0])
-
-        @pl.when(section != 0)
-        def _():
-            begin(rec, h_v, in_sem.at[0])
-
-        w_copies = [
-            begin(wqkv.at[0], wqkv_v, w_sem.at[0]),
-            begin(wo.at[0], wo_v, w_sem.at[1]),
-            begin(wu.at[0], wu_v, w_sem.at[2]),
-            begin(wd.at[0], wd_v, w_sem.at[3]),
-        ]
-        seg_row = segs[pl.ds(mb, 1), :]
-        seg_col = jnp.transpose(jnp.broadcast_to(seg_row.astype(F32), (128, SEQ)))
-        length = lens[mb]
-        query = lax.broadcasted_iota(jnp.int32, (SEQ, 128), 0)
+        inputs.spread()
+
+    w_rest = [begin(wo.at[0], wo_v, w_sem.at[3]), begin(wu.at[0], wu_v, w_sem.at[4]), begin(wd.at[0], wd_v, w_sem.at[5])]
+    seg_copy.wait()
+
+    def save(name, buffer, step):
+        target = outs[name].at[pl.ds(pl.multiple_of(step * ROWS, ROWS), ROWS)]
+        pltpu.make_async_copy(buffer, target, save_sem.at[names.index(name)]).start()
+
+    def free(name, buffer):
+        pltpu.make_async_copy(buffer, buffer, save_sem.at[names.index(name)]).wait()
+
+    reused = (
+        ("q", q_v), ("linv", linv_v), ("ctx", ctx_v), ("xh1", xh1_v), ("inv1", inv1_v), ("low", low_v),
+        ("gelu", gelu_v), ("slope", slope_v), ("xh2", xh2_v), ("inv2", inv2_v),
+    )
+
+    def one_step(step, carry):
+        sequence = lax.rem(step, sequences)
+        mine = jnp.where(place.is_mine(step, sequences), 1.0, 0.0)
+        key_rows = mine * seg_own[sequence] + (1.0 - mine) * seg_their[sequence]
+        query_row = mine * seg_own[sequence, 0:1, place.own] + (1.0 - mine) * seg_their[sequence, 0:1, place.own]
+        query_seg = jnp.transpose(jnp.broadcast_to(query_row, (128, ROWS)))
+        query = lax.broadcasted_iota(jnp.int32, (ROWS, 128), 0) + place.core * ROWS
+        key = lax.broadcasted_iota(jnp.int32, (ROWS, 128), 1)
         for tile in range(SEQ // 128):
-            key = lax.broadcasted_iota(jnp.int32, (SEQ, 128), 1) + tile * 128
-            same = seg_col == seg_row[:, tile * 128 : (tile + 1) * 128].astype(F32)
-            allowed = same & ((key < length) | (key == query))
-            bias_v[:, tile * 128 : (tile + 1) * 128] = jnp.where(allowed, 0.0, NEG_FILL)
-
-        pending = []
-
-        def save(name, value_ref):
-            pending.append(begin(value_ref, saved_out[name].at[rows], out_sem.at[len(pending)]))
-
-        pltpu.make_async_copy(rec, h_v, in_sem.at[0]).wait()
-        pending.append(begin(h_v, hid_out.at[rows], out_sem.at[0]))
-        w_copies[0].wait()
-        for block in range(3):
-            cols = slice(block * D, (block + 1) * D)
-            proj = dot_nn(h_v[...], wqkv_v[:, cols])
-            if block != 1:
-                proj = proj + qv_bias[0, block // 2 : block // 2 + 1, :]
-            qkv_v[:, cols] = proj.astype(BF16)
-        save("qkv", qkv_v)
+            cols = slice(tile * 128, (tile + 1) * 128)
+            visible = (key_rows[1:2, cols] > 0.5) | (key + tile * 128 == query)
+            bias_v[:, cols] = jnp.where((query_seg == key_rows[0:1, cols]) & visible, 0.0, NEG_FILL)
+
+        inputs.await_step(step, section == 0)
+        target = outs["hid"].at[pl.ds(pl.multiple_of(step * ROWS, ROWS), ROWS)]
+        pltpu.make_async_copy(h_v.at[step], target, hid_save.at[step]).start()
+        hidden = h_v[step]
+        for block in (1, 2):
+
+            @pl.when(step == 0)
+            def _():
+                w_first[block - 1].wait()
+
+            proj = dot_nn(hidden, wqkv_v[:, block * D : (block + 1) * D])
+            if block == 2:
+                proj = proj + qv_bias[0, 1:2, :]
+            cols = pl.ds((block - 1) * D, D)
+            kv_v[step, place.own, cols] = proj.astype(BF16)
+            view = kv_v.at[step, place.own, cols]
+            remote(view, view, kv_sent.at[step, block - 1], kv_arrived.at[step, block - 1], place.sibling).start()
+
+        @pl.when(step == 0)
+        def _():
+            w_first[2].wait()
+
+        @pl.when(step > 0)
+        def _():
+            for name, buffer in reused:
+                free(name, buffer)
+            for pair in range(PAIRS):
+                pltpu.make_async_copy(p_v.at[pair], p_v.at[pair], p_sem.at[pair]).wait()
+
+        q_v[...] = (dot_nn(hidden, wqkv_v[:, 0:D]) + qv_bias[0, 0:1, :]).astype(BF16)
+        save("q", q_v, step)
+        for block in range(2):
+            view = kv_v.at[step, place.theirs, pl.ds(block * D, D)]
+            remote(view, view, kv_sent.at[step, block], kv_arrived.at[step, block], place.sibling).wait_recv()
+        pltpu.make_async_copy(kv_v.at[step], kv_out.at[step], kv_save.at[step]).start()
 
         def pair_step(pair, carry):
-            slot = lax.rem(pair, 2)
-
-            @pl.when(pair >= 2)
-            def _():
-                pltpu.make_async_copy(p_v.at[slot], prob_out.at[mb, pl.ds(0, 2)], p_sem.at[slot]).wait()
-
             at = pl.multiple_of(pair * PAIR, PAIR)
-            q2 = qkv_v[:, pl.ds(at, PAIR)] * SCORE_SCALE
-            k2 = qkv_v[:, pl.ds(at + D, PAIR)]
-            v2 = qkv_v[:, pl.ds(at + 2 * D, PAIR)]
-            total = None
+            q2 = q_v[:, pl.ds(at, PAIR)] * SCORE_SCALE
+            k2 = kv_v[step, :, pl.ds(at, PAIR)]
+            v2 = kv_v[step, :, pl.ds(at + D, PAIR)]
+            total, inverses = None, []
             for head in range(2):
                 mask = half_mask(head)
                 scores = dot_nt(q2, k2 * mask) + bias_v[...]
                 exp_vals = jnp.exp(scores - jnp.max(scores, axis=-1, keepdims=True))
-                inverse_total = 1.0 / jnp.sum(exp_vals, axis=-1, keepdims=True)
-                prob = (exp_vals * inverse_total).astype(BF16)
-                p_v[slot, head] = prob
-                part = dot_nn(prob, v2 * mask)
+                inverses.append(1.0 / jnp.sum(exp_vals, axis=-1, keepdims=True))
+                weight = exp_vals.astype(BF16)
+                p_v[pair, head] = weight
+                part = dot_nn(weight, v2 * mask)
                 total = part if total is None else total + part
-            ctx_v[:, pl.ds(at, PAIR)] = total.astype(BF16)
-            begin(p_v.at[slot], prob_out.at[mb, pl.ds(pair * 2, 2)], p_sem.at[slot])
+            lane = lax.broadcasted_iota(jnp.int32, (1, PAIR), 1)
+            inverse = jnp.where(lane < HD, inverses[0], inverses[1])
+            linv_v[:, pl.ds(at, PAIR)] = inverse
+            ctx_v[:, pl.ds(at, PAIR)] = (total * inverse).astype(BF16)
+            pltpu.make_async_copy(p_v.at[pair], prob_out.at[step, pl.ds(pair * 2, 2)], p_sem.at[pair]).start()
             return carry
 
-        lax.fori_loop(0, PAIRS, pair_step, 0)
-        save("ctx", ctx_v)
-
-        w_copies[1].wait()
-        resid = h_v[...].astype(F32) + (dot_nn(ctx_v[...], wo_v[...]) + out_biases[0, 0:1, :])
+        lax.fori_loop(0, PAIRS, pair_step, 0, unroll=3)
+        save("linv", linv_v, step)
+        save("ctx", ctx_v, step)
+
+        @pl.when(step == 0)
+        def _():
+            w_rest[0].wait()
+
+        resid = hidden.astype(F32) + (dot_nn(ctx_v[...], wo_v[...]) + out_biases[0, 0:1, :])
         scaled, inverse = normalize(resid)
         xh1_v[...] = scaled.astype(BF16)
-        inv1_v[...] = jnp.broadcast_to(inverse, (SEQ, 128))
+        inv1_v[...] = jnp.broadcast_to(inverse, (ROWS, 128))
         normed = scaled * gains[0, 0:1, :] + shifts[0, 0:1, :]
         low_v[...] = normed.astype(BF16)
         acc_v[...] = normed + out_biases[0, 1:2, :]
-        save("xh1", xh1_v)
-        save("inv1", inv1_v)
-        save("low", low_v)
-        w_copies[2].wait()
-        w_copies[3].wait()
-        width = 512
+        save("xh1", xh1_v, step)
+        save("inv1", inv1_v, step)
+        save("low", low_v, step)
+
+        @pl.when(step == 0)
+        def _():
+            w_rest[1].wait()
+            w_rest[2].wait()
+
+        width = 1024
         for chunk in range(FF // width):
             cols = slice(chunk * width, (chunk + 1) * width)
             up = dot_nn(low_v[...], wu_v[:, cols]) + up_bias[0:1, cols]
@@ -201,251 +324,356 @@
             gelu_v[:, cols] = gelu
             slope_v[:, cols] = slope.astype(BF16)
             acc_v[...] += dot_nn(gelu, wd_v[cols, :])
-        save("gelu", gelu_v)
-        save("slope", slope_v)
+        save("gelu", gelu_v, step)
+        save("slope", slope_v, step)
         scaled, inverse = normalize(acc_v[...])
+        act_v[step] = (scaled * gains[0, 1:2, :] + shifts[0, 1:2, :]).astype(BF16)
+
+        @pl.when(section == 0)
+        def _():
+            remote(act_v.at[step], h_v.at[step], hop_sent.at[step], in_arrived.at[step], place.other_layer).start()
+
+        outputs.collect(step)
         xh2_v[...] = scaled.astype(BF16)
-        inv2_v[...] = jnp.broadcast_to(inverse, (SEQ, 128))
-        act_v[...] = (scaled * gains[0, 1:2, :] + shifts[0, 1:2, :]).astype(BF16)
-        pending.append(begin(act_v, y_hop, out_sem.at[len(pending)]))
-        save("act", act_v)
-        save("xh2", xh2_v)
-        save("inv2", inv2_v)
-        for slot in range(2):
-            pltpu.make_async_copy(p_v.at[slot], prob_out.at[mb, pl.ds(0, 2)], p_sem.at[slot]).wait()
-        for copy in pending:
-            copy.wait()
-
-
-def forward(step, tokens, received, weights, segments, lengths, params, saved):
-    total = MICRO * SEQ
+        inv2_v[...] = jnp.broadcast_to(inverse, (ROWS, 128))
+        save("xh2", xh2_v, step)
+        save("inv2", inv2_v, step)
+        return carry
+
+    lax.fori_loop(0, steps, one_step, 0)
+    for name, buffer in reused:
+        free(name, buffer)
+    for step in range(steps):
+        pltpu.make_async_copy(h_v.at[step], h_v.at[step], hid_save.at[step]).wait()
+        pltpu.make_async_copy(kv_v.at[step], kv_out.at[step], kv_save.at[step]).wait()
+        for block in range(2):
+            view = kv_v.at[step, place.own, pl.ds(block * D, D)]
+            remote(view, view, kv_sent.at[step, block], kv_arrived.at[step, block], place.sibling).wait_send()
+    for pair in range(PAIRS):
+        pltpu.make_async_copy(p_v.at[pair], p_v.at[pair], p_sem.at[pair]).wait()
+
+    @pl.when(section == 0)
+    def _():
+        inputs.spread_done()
+        for step in range(steps):
+            remote(act_v.at[step], h_v.at[step], hop_sent.at[step], in_arrived.at[step], place.other_layer).wait_send()
+
+    outputs.collect_done()
+
+
+def forward(tokens, weights, segments, lengths, params):
+    total = tokens.shape[0]
+    sequences = total // SEQ
+    steps = 2 * sequences
     shapes = [
-        jax.ShapeDtypeStruct((SEQ, D), BF16),
         jax.ShapeDtypeStruct((total, D), BF16),
-        jax.ShapeDtypeStruct((MICRO, H, SEQ, SEQ), BF16),
+        jax.ShapeDtypeStruct((steps, SEQ, 2 * D), BF16),
+        jax.ShapeDtypeStruct((steps, H, ROWS, SEQ), BF16),
     ] + [jax.ShapeDtypeStruct((total, width), dtype) for _, width, dtype in SAVED]
-    n_alias = len(saved)
-    ins = [tokens, received, *weights, segments, lengths, *params, *saved]
-    result = pl.pallas_call(
-        functools.partial(forward_kernel, step, n_alias),
+    dma = pltpu.SemaphoreType.DMA
+    act, kv, prob, *saved = pl.pallas_call(
+        functools.partial(forward_kernel, sequences),
         out_shape=shapes,
-        in_specs=[ANY] * 6 + [VMEM, SMEM] + [VMEM] * 5 + [ANY] * n_alias,
+        in_specs=[ANY] * 5 + [VMEM, SMEM] + [VMEM] * 5,
         out_specs=[ANY] * len(shapes),
-        input_output_aliases={13 + i: 1 + i for i in range(n_alias)},
         scratch_shapes=[
-            pltpu.VMEM((SEQ, D), BF16),
+            pltpu.VMEM((steps, ROWS, D), BF16),
+            pltpu.VMEM((steps, ROWS, D), BF16),
+            pltpu.VMEM((steps, SEQ, 2 * D), BF16),
+            pltpu.VMEM((PAIRS, 2, ROWS, SEQ), BF16),
             pltpu.VMEM((D, 3 * D), BF16),
             pltpu.VMEM((D, D), BF16),
             pltpu.VMEM((D, FF), BF16),
             pltpu.VMEM((FF, D), BF16),
-            pltpu.VMEM((SEQ, SEQ), F32),
-            pltpu.VMEM((2, 2, SEQ, SEQ), BF16),
-            pltpu.VMEM((SEQ, D), F32),
+            pltpu.VMEM((ROWS, SEQ), F32),
+            pltpu.VMEM((ROWS, D), F32),
+            pltpu.VMEM((sequences, 8, SEQ), F32),
+            pltpu.VMEM((sequences, 8, SEQ), F32),
         ]
-        + [pltpu.VMEM((SEQ, width), dtype) for _, width, dtype in SAVED]
+        + [pltpu.VMEM((ROWS, width), dtype) for name, width, dtype in SAVED if name != "hid"]
         + [
-            pltpu.SemaphoreType.DMA((1,)),
-            pltpu.SemaphoreType.DMA((4,)),
-            pltpu.SemaphoreType.DMA((2,)),
-            pltpu.SemaphoreType.DMA((16,)),
+            dma((6,)),
+            dma((len(SAVED),)),
+            dma((PAIRS,)),
+            dma((sequences,)),
+            dma((sequences,)),
+            dma((steps,)),
+            dma((sequences,)),
+            dma((sequences,)),
+            dma((sequences,)),
+            dma((steps, 2)),
+            dma((steps, 2)),
+            dma((steps,)),
+            dma((2,)),
+            dma((steps,)),
+            dma((steps,)),
         ],
-        compiler_params=pltpu.CompilerParams(vmem_limit_bytes=VMEM_LIMIT),
+        compiler_params=pltpu.CompilerParams(
+            collective_id=1, has_side_effects=True, vmem_limit_bytes=VMEM_LIMIT
+        ),
         name="forward",
-    )(*ins)
-    return result[0], list(result[1:])
-
-
-GRADS = (("d_down", D, BF16), ("d_up", FF, BF16), ("d_attn", D, BF16), ("d_qkv", 3 * D, BF16), ("d_hid", D, BF16))
-SMALL_ROWS = 16
-
-
-def backward_kernel(step, n_alias, *refs):
-    (cot, rec, wqkv, wo, wu, wd, gains, prob_in) = refs[:8]
-    saved_in = dict(zip([name for name, _, _ in SAVED], refs[8:18]))
-    outs = refs[18 + n_alias : 18 + n_alias + 7]
-    d_hop, small_out = outs[:2]
-    grads_out = dict(zip([name for name, _, _ in GRADS], outs[2:]))
+    )(tokens, *weights, segments, lengths, *params)
+    return act, kv, prob, dict(zip([name for name, _, _ in SAVED], saved))
+
+
+KEPT = ("q", "linv", "ctx", "xh1", "inv1", "slope", "xh2", "inv2")
+
+
+def backward_kernel(sequences, *refs):
+    (cot, wqkv, wo, wu, wd, gains, kv_in, prob_in) = refs[:8]
+    ins = dict(zip(KEPT, refs[8:16]))
+    d_hid_out, small_out = refs[16:18]
+    outs = dict(zip([name for name, _, _ in GRADS], refs[18:22]))
     (
-        g_v, wqkv_v, wo_v, wu_v, wd_v, p_v, acc_v, acc2_v, small_v,
-        qkv_v, ctx_v, xh1_v, inv1_v, slope_v, xh2_v, inv2_v, d_ctx_v,
-        d_down_v, d_up_v, d_attn_v, d_qkv_v, d_hid_v,
-        in_sem, w_sem, p_sem, out_sem,
-    ) = refs[18 + n_alias + 7 :]
-    section = lax.axis_index("section")
-    mb = step - (1 - section)
-
-    @pl.when((mb >= 0) & (mb < MICRO))
+        g_v, d_hid_v, kv_v, p_v, wqkv_v, wo_v, wu_v, wd_v, acc_v, d_ctx_v, part_v, their_v,
+        q_v, linv_v, ctx_v, xh1_v, inv1_v, slope_v, xh2_v, inv2_v,
+        d_down_v, d_up_v, d_attn_v, d_qkv_v,
+        w_sem, load_sem, save_sem, in_local, in_sent, in_arrived, out_local, out_sent, out_arrived,
+        part_sent, part_arrived, hop_sent,
+    ) = refs[22:]
+    place = Place()
+    section = place.section
+    steps = 2 * sequences
+    grad_names = [name for name, _, _ in GRADS]
+    inputs = Rows(place, sequences, cot, g_v, in_local, in_sent, in_arrived)
+    outputs = Rows(place, sequences, d_hid_out, d_hid_v, out_local, out_sent, out_arrived)
+    buffers = dict(zip(KEPT, (q_v, linv_v, ctx_v, xh1_v, inv1_v, slope_v, xh2_v, inv2_v)))
+
+    def at_step(array, step):
+        return array.at[pl.ds(pl.multiple_of(step * ROWS, ROWS), ROWS)]
+
+    def fetch(names, step):
+        for name in names:
+            if name == "kv":
+                pltpu.make_async_copy(kv_in.at[step], kv_v, load_sem.at[len(KEPT)]).start()
+            elif name == "prob":
+                pltpu.make_async_copy(prob_in.at[step], p_v, load_sem.at[len(KEPT) + 1]).start()
+            else:
+                source = at_step(ins[name], step)
+                pltpu.make_async_copy(source, buffers[name], load_sem.at[KEPT.index(name)]).start()
+
+    def fetched(*names):
+        for name in names:
+            if name == "kv":
+                pltpu.make_async_copy(kv_v, kv_v, load_sem.at[len(KEPT)]).wait()
+            elif name == "prob":
+                pltpu.make_async_copy(p_v, p_v, load_sem.at[len(KEPT) + 1]).wait()
+            else:
+                pltpu.make_async_copy(buffers[name], buffers[name], load_sem.at[KEPT.index(name)]).wait()
+
+    def fetch_next(names, step):
+        @pl.when(step + 1 < steps)
+        def _():
+            fetch(names, step + 1)
+
+    def save(name, buffer, step):
+        pltpu.make_async_copy(buffer, at_step(outs[name], step), save_sem.at[grad_names.index(name)]).start()
+
+    def free(name, buffer):
+        pltpu.make_async_copy(buffer, buffer, save_sem.at[grad_names.index(name)]).wait()
+
+    def free_before(name, buffer, step):
+        @pl.when(step > 0)
+        def _():
+            free(name, buffer)
+
+    def when_first(step, copies):
+        @pl.when(step == 0)
+        def _():
+            for copy in copies:
+                copy.wait()
+
+    place.greet()
+
+    @pl.when(section == 1)
     def _():
-        rows = pl.ds(pl.multiple_of(mb * SEQ, SEQ), SEQ)
-
-        @pl.when(section == 0)
-        def _():
-            begin(rec, g_v, in_sem.at[0])
-
-        @pl.when(section != 0)
-        def _():
-            begin(cot.at[rows], g_v, in_sem.at[0])
-
-        def fetch(name, target, index):
-            return begin(saved_in[name].at[rows], target, in_sem.at[index])
-
-        get_xh2 = fetch("xh2", xh2_v, 1)
-        get_inv2 = fetch("inv2", inv2_v, 2)
-        get_wd = begin(wd.at[0], wd_v, w_sem.at[3])
-        get_slope = fetch("slope", slope_v, 3)
-        get_wu = begin(wu.at[0], wu_v, w_sem.at[2])
-        get_xh1 = fetch("xh1", xh1_v, 4)
-        get_inv1 = fetch("inv1", inv1_v, 5)
-        get_wo = begin(wo.at[0], wo_v, w_sem.at[1])
-        get_qkv = fetch("qkv", qkv_v, 6)
-        get_ctx = fetch("ctx", ctx_v, 7)
-        begin(prob_in.at[mb, pl.ds(0, 2)], p_v.at[0], p_sem.at[0])
-        get_wqkv = begin(wqkv.at[0], wqkv_v, w_sem.at[0])
-
-        pending = []
-
-        def save(name, value_ref):
-            pending.append(begin(value_ref, grads_out[name].at[rows], out_sem.at[len(pending)]))
-
-        def column_sum(value):
-            return jnp.sum(value, axis=0, keepdims=True)
-
-        small_v[...] = jnp.zeros_like(small_v)
-        pltpu.make_async_copy(rec, g_v, in_sem.at[0]).wait()
-        get_xh2.wait()
-        get_inv2.wait()
-        grad = g_v[...].astype(F32)
+        inputs.spread()
+
+    first = jnp.int32(0)
+    fetch(("xh2", "inv2"), first)
+    get_wd = begin(wd.at[0], wd_v, w_sem.at[0])
+    fetch(("slope",), first)
+    get_wu = begin(wu.at[0], wu_v, w_sem.at[1])
+    fetch(("xh1", "inv1"), first)
+    get_wo = begin(wo.at[0], wo_v, w_sem.at[2])
+    fetch(("q", "linv", "ctx", "kv", "prob"), first)
+    get_wqkv = begin(wqkv.at[0], wqkv_v, w_sem.at[3])
+    small_out[...] = jnp.zeros_like(small_out)
+
+    def column_sum(value):
+        return jnp.sum(value, axis=0, keepdims=True)
+
+    def one_step(step, carry):
+        inputs.await_step(step, section == 1)
+        fetched("xh2", "inv2")
+        grad = g_v[step].astype(F32)
         scaled = xh2_v[...].astype(F32)
-        small_v[5:6, :] = column_sum(grad * scaled)
-        small_v[7:8, :] = column_sum(grad)
+        small_out[5:6, :] += column_sum(grad * scaled)
+        small_out[7:8, :] += column_sum(grad)
         d_r2 = norm_back(grad, scaled, inv2_v[:, 0:1], gains[0, 1:2, :])
         d_down = d_r2.astype(BF16)
+        free_before("d_down", d_down_v, step)
         d_down_v[...] = d_down
-        small_v[3:4, :] = column_sum(d_down.astype(F32))
+        small_out[3:4, :] += column_sum(d_down.astype(F32))
         acc_v[...] = d_r2
-        save("d_down", d_down_v)
-        get_wd.wait()
-        get_slope.wait()
-        get_wu.wait()
-        width = 512
-        for chunk in range(FF // width):
-            cols = slice(chunk * width, (chunk + 1) * width)
+        save("d_down", d_down_v, step)
+        fetch_next(("xh2", "inv2"), step)
+        fetched("slope")
+        when_first(step, (get_wd, get_wu))
+        free_before("d_up", d_up_v, step)
+        for chunk in range(FF // D):
+            cols = slice(chunk * D, (chunk + 1) * D)
             d_up = (dot_nt(d_down_v[...], wd_v[cols, :]) * slope_v[:, cols].astype(F32)).astype(BF16)
             d_up_v[:, cols] = d_up
-            at = chunk * width
-            sums = column_sum(d_up.astype(F32))
-            while at < (chunk + 1) * width:
-                row = at // D
-                stop = min((row + 1) * D, (chunk + 1) * width)
-                small_v[8 + row : 9 + row, at - row * D : stop - row * D] = sums[
-                    :, at - chunk * width : stop - chunk * width
-                ]
-                at = stop
+            small_out[8 + chunk : 9 + chunk, :] += column_sum(d_up.astype(F32))
             acc_v[...] += dot_nt(d_up, wu_v[:, cols])
-        save("d_up", d_up_v)
-        get_xh1.wait()
-        get_inv1.wait()
+        save("d_up", d_up_v, step)
+        fetch_next(("slope",), step)
+        fetched("xh1", "inv1")
         d_normed = acc_v[...]
         scaled = xh1_v[...].astype(F32)
-        small_v[4:5, :] = column_sum(d_normed * scaled)
-        small_v[6:7, :] = column_sum(d_normed)
+        small_out[4:5, :] += column_sum(d_normed * scaled)
+        small_out[6:7, :] += column_sum(d_normed)
         d_r1 = norm_back(d_normed, scaled, inv1_v[:, 0:1], gains[0, 0:1, :])
         d_attn = d_r1.astype(BF16)
+        free_before("d_attn", d_attn_v, step)
         d_attn_v[...] = d_attn
-        small_v[2:3, :] = column_sum(d_attn.astype(F32))
+        small_out[2:3, :] += column_sum(d_attn.astype(F32))
         acc_v[...] = d_r1
-        save("d_attn", d_attn_v)
-        get_wo.wait()
-        d_ctx_v[...] = dot_nt(d_attn, wo_v[...]).astype(BF16)
-        get_qkv.wait()
-        get_ctx.wait()
+        save("d_attn", d_attn_v, step)
+        fetch_next(("xh1", "inv1"), step)
+        when_first(step, (get_wo,))
+        fetched("q", "linv", "ctx", "kv", "prob")
+        d_ctx_v[...] = (dot_nt(d_attn_v[...], wo_v[...]) * linv_v[...]).astype(BF16)
+        free_before("d_qkv", d_qkv_v, step)
+
+        @pl.when(step > 0)
+        def _():
+            for pair in range(PAIRS):
+                view = part_v.at[pair, place.theirs]
+                remote(view, view, part_sent.at[pair], part_arrived.at[0, 0], place.sibling).wait_send()
 
         def pair_step(pair, carry):
-            slot = lax.rem(pair, 2)
-
-            @pl.when(pair + 1 < PAIRS)
-            def _():
-                begin(prob_in.at[mb, pl.ds((pair + 1) * 2, 2)], p_v.at[1 - slot], p_sem.at[1 - slot])
-
-            pltpu.make_async_copy(prob_in.at[mb, pl.ds(0, 2)], p_v.at[slot], p_sem.at[slot]).wait()
             at = pl.multiple_of(pair * PAIR, PAIR)
-            q2 = qkv_v[:, pl.ds(at, PAIR)] * SCORE_SCALE
-            k2 = qkv_v[:, pl.ds(at + D, PAIR)]
-            v2 = qkv_v[:, pl.ds(at + 2 * D, PAIR)]
+            q2 = q_v[:, pl.ds(at, PAIR)] * SCORE_SCALE
+            k2 = kv_v[:, pl.ds(at, PAIR)]
+            v2 = kv_v[:, pl.ds(at + D, PAIR)]
             dc2 = d_ctx_v[:, pl.ds(at, PAIR)]
             inner = dc2.astype(F32) * ctx_v[:, pl.ds(at, PAIR)].astype(F32)
             d_q, d_k, d_v = None, None, None
             for head in range(2):
                 mask = half_mask(head)
-                k_own, q_own, dc_own = k2 * mask, q2 * mask, dc2 * mask
-                prob = p_v[slot, head]
+                dc_own = dc2 * mask
+                weight = p_v[pair * 2 + head]
                 row_inner = jnp.sum(inner * mask.astype(F32), axis=-1, keepdims=True)
                 d_prob = dot_nt(dc_own, v2)
-                d_score = (prob.astype(F32) * (d_prob - row_inner)).astype(BF16)
-                part_v = dot_tn(dc_own, prob)
-                part_q = dot_nn(d_score, k_own)
-                part_k = dot_tn(q_own, d_score)
-                d_v = part_v if d_v is None else d_v + part_v
-                d_q = part_q if d_q is None else d_q + part_q
-                d_k = part_k if d_k is None else d_k + part_k
+                d_score = (weight.astype(F32) * (d_prob - row_inner)).astype(BF16)
+                one_v = dot_tn(dc_own, weight)
+                one_k = dot_tn(q2 * mask, d_score)
+                one_q = dot_nn(d_score, k2 * mask)
+                d_v = one_v if d_v is None else d_v + one_v
+                d_k = one_k if d_k is None else d_k + one_k
+                d_q = one_q if d_q is None else d_q + one_q
             d_qkv_v[:, pl.ds(at, PAIR)] = (d_q * SCORE_SCALE).astype(BF16)
-            d_qkv_v[:, pl.ds(at + D, PAIR)] = jnp.transpose(d_k).astype(BF16)
-            d_qkv_v[:, pl.ds(at + 2 * D, PAIR)] = jnp.transpose(d_v).astype(BF16)
+            part_v[pair, :, 0:PAIR] = jnp.transpose(d_k).astype(BF16)
+            part_v[pair, :, PAIR : 2 * PAIR] = jnp.transpose(d_v).astype(BF16)
+            remote(
+                part_v.at[pair, place.theirs], their_v.at[step, pair], part_sent.at[pair],
+                part_arrived.at[step, pair], place.sibling,
+            ).start()
             return carry
 
-        lax.fori_loop(0, PAIRS, pair_step, 0)
-        save("d_qkv", d_qkv_v)
-        get_wqkv.wait()
-        small_v[0:1, :] = column_sum(d_qkv_v[:, 0:D].astype(F32))
-        small_v[1:2, :] = column_sum(d_qkv_v[:, 2 * D : 3 * D].astype(F32))
-        d_hid_v[...] = (acc_v[...] + dot_nt(d_qkv_v[...], wqkv_v[...])).astype(BF16)
-        pending.append(begin(d_hid_v, d_hop, out_sem.at[len(pending)]))
-        save("d_hid", d_hid_v)
-        pending.append(begin(small_v, small_out.at[mb], out_sem.at[len(pending)]))
-        for copy in pending:
-            copy.wait()
-
-
-def backward(step, cotangent, received, weights, gains, prob, saved, grads):
-    total = MICRO * SEQ
+        lax.fori_loop(0, PAIRS, pair_step, 0, unroll=3)
+        fetch_next(("q", "linv", "ctx", "kv", "prob"), step)
+        when_first(step, (get_wqkv,))
+        d_query = d_qkv_v[:, 0:D]
+        acc_v[...] += dot_nt(d_query, wqkv_v[:, 0:D])
+        small_out[0:1, :] += column_sum(d_query.astype(F32))
+        for pair in range(PAIRS):
+            view = their_v.at[step, pair]
+            remote(view, view, part_sent.at[pair], part_arrived.at[step, pair], place.sibling).wait_recv()
+            total = part_v[pair, place.own, :].astype(F32) + their_v[step, pair].astype(F32)
+            at = pair * PAIR
+            d_qkv_v[:, D + at : D + at + PAIR] = total[:, 0:PAIR].astype(BF16)
+            d_qkv_v[:, 2 * D + at : 2 * D + at + PAIR] = total[:, PAIR : 2 * PAIR].astype(BF16)
+        d_hid_v[step] = (acc_v[...] + dot_nt(d_qkv_v[:, D : 3 * D], wqkv_v[:, D : 3 * D])).astype(BF16)
+
+        @pl.when(section == 1)
+        def _():
+            remote(d_hid_v.at[step], g_v.at[step], hop_sent.at[step], in_arrived.at[step], place.other_layer).start()
+
+        outputs.collect(step)
+        small_out[1:2, :] += column_sum(d_qkv_v[:, 2 * D : 3 * D].astype(F32))
+        save("d_qkv", d_qkv_v, step)
+        return carry
+
+    lax.fori_loop(0, steps, one_step, 0)
+    for name, buffer in zip(grad_names, (d_down_v, d_up_v, d_attn_v, d_qkv_v)):
+        free(name, buffer)
+    for pair in range(PAIRS):
+        view = part_v.at[pair, place.theirs]
+        remote(view, view, part_sent.at[pair], part_arrived.at[0, 0], place.sibling).wait_send()
+
+    @pl.when(section == 1)
+    def _():
+        inputs.spread_done()
+        for step in range(steps):
+            remote(d_hid_v.at[step], g_v.at[step], hop_sent.at[step], in_arrived.at[step], place.other_layer).wait_send()
+
+    outputs.collect_done()
+
+
+def backward(cotangent, weights, gains, kv, prob, saved):
+    total = cotangent.shape[0]
+    sequences = total // SEQ
+    steps = 2 * sequences
     shapes = [
-        jax.ShapeDtypeStruct((SEQ, D), BF16),
-        jax.ShapeDtypeStruct((MICRO, SMALL_ROWS, D), F32),
+        jax.ShapeDtypeStruct((total, D), BF16),
+        jax.ShapeDtypeStruct((SMALL_ROWS, D), F32),
     ] + [jax.ShapeDtypeStruct((total, width), dtype) for _, width, dtype in GRADS]
-    n_alias = len(grads)
-    ins = [cotangent, received, *weights, gains, prob, *saved, *grads]
     widths = {name: (width, dtype) for name, width, dtype in SAVED}
-    kept = ("qkv", "ctx", "xh1", "inv1", "slope", "xh2", "inv2")
-    result = pl.pallas_call(
-        functools.partial(backward_kernel, step, n_alias),
+    dma = pltpu.SemaphoreType.DMA
+    d_hid, small, *grads = pl.pallas_call(
+        functools.partial(backward_kernel, sequences),
         out_shape=shapes,
-        in_specs=[ANY] * 6 + [VMEM] + [ANY] * (11 + n_alias),
-        out_specs=[ANY] * len(shapes),
-        input_output_aliases={18 + i: 1 + i for i in range(n_alias)},
+        in_specs=[ANY] * 5 + [VMEM] + [ANY] * (2 + len(KEPT)),
+        out_specs=[ANY, VMEM] + [ANY] * len(GRADS),
         scratch_shapes=[
-            pltpu.VMEM((SEQ, D), BF16),
+            pltpu.VMEM((steps, ROWS, D), BF16),
+            pltpu.VMEM((steps, ROWS, D), BF16),
+            pltpu.VMEM((SEQ, 2 * D), BF16),
+            pltpu.VMEM((H, ROWS, SEQ), BF16),
             pltpu.VMEM((D, 3 * D), BF16),
             pltpu.VMEM((D, D), BF16),
             pltpu.VMEM((D, FF), BF16),
             pltpu.VMEM((FF, D), BF16),
-            pltpu.VMEM((2, 2, SEQ, SEQ), BF16),
-            pltpu.VMEM((SEQ, D), F32),
-            pltpu.VMEM((8, 128), F32),
-            pltpu.VMEM((SMALL_ROWS, D), F32),
+            pltpu.VMEM((ROWS, D), F32),
+            pltpu.VMEM((ROWS, D), BF16),
+            pltpu.VMEM((PAIRS, SEQ, 2 * PAIR), BF16),
+            pltpu.VMEM((steps, PAIRS, ROWS, 2 * PAIR), BF16),
         ]
-        + [pltpu.VMEM((SEQ, widths[name][0]), widths[name][1]) for name in kept]
-        + [pltpu.VMEM((SEQ, D), BF16)]
-        + [pltpu.VMEM((SEQ, width), dtype) for _, width, dtype in GRADS]
+        + [pltpu.VMEM((ROWS, widths[name][0]), widths[name][1]) for name in KEPT]
+        + [pltpu.VMEM((ROWS, width), dtype) for _, width, dtype in GRADS]
         + [
-            pltpu.SemaphoreType.DMA((8,)),
-            pltpu.SemaphoreType.DMA((4,)),
-            pltpu.SemaphoreType.DMA((2,)),
-            pltpu.SemaphoreType.DMA((8,)),
+            dma((4,)),
+            dma((len(KEPT) + 2,)),
+            dma((len(GRADS),)),
+            dma((sequences,)),
+            dma((sequences,)),
+            dma((steps,)),
+            dma((sequences,)),
+            dma((sequences,)),
+            dma((sequences,)),
+            dma((PAIRS,)),
+            dma((steps, PAIRS)),
+            dma((steps,)),
         ],
-        compiler_params=pltpu.CompilerParams(vmem_limit_bytes=VMEM_LIMIT),
+        compiler_params=pltpu.CompilerParams(
+            collective_id=2, has_side_effects=True, vmem_limit_bytes=VMEM_LIMIT
+        ),
         name="backward",
-    )(*ins)
-    return result[0], list(result[1:])
+    )(cotangent, *weights, gains, kv, prob, *[saved[name] for name in KEPT])
+    return d_hid, small, dict(zip([name for name, _, _ in GRADS], grads))
 
 
 UNIT = 16
@@ -453,7 +681,6 @@
 ROOTS = 4
 HALF = 2 * RAIL + ROOTS * UNIT
 SLAB = 2 * HALF
-MESH = pl.DeviceIdType.MESH
 
 
 def reduce_kernel(depth, *refs):
@@ -707,7 +934,7 @@
     def small_round(now):
         @pl.when(now == 0)
         def _():
-            sm_v[...] = small[0] + small[1]
+            sm_v[...] = small[...]
             sm_copy(0, sm_v, sm_in_v.at[0], 0, sibling).start()
 
         @pl.when(now == 1)
@@ -909,27 +1136,11 @@
 ):
     weights = (qkv_weight, out_weight, up_weight, down_weight)
     params = (qv_bias, out_biases, norm_gains, norm_shifts, up_bias)
-    onward = [(0, 1)]
-    back = [(1, 0)]
-    received = tokens[:SEQ]
-    state = []
-    for step in range(MICRO + 1):
-        hop, state = forward(step, tokens, received, weights, segments, lengths, params, state)
-        if step < MICRO:
-            received = lax.ppermute(hop, "section", onward)
-    hid, prob = state[:2]
-    saved = state[2:]
-    act = saved[0]
-    received = cotangent[:SEQ]
-    grads = []
-    for step in range(MICRO + 1):
-        hop, grads = backward(step, cotangent, received, weights, norm_gains, prob, saved, grads)
-        if step < MICRO:
-            received = lax.ppermute(hop, "section", back)
-    d_down, d_up, d_attn, d_qkv, d_hid = grads[1:]
-    kept = dict(zip([name for name, _, _ in SAVED], saved))
+    act, kv, prob, saved = forward(tokens, weights, segments, lengths, params)
+    d_hid, small, grads = backward(cotangent, weights, norm_gains, kv, prob, saved)
     *large, small = reduce_gradients(
-        lax.axis_size("dp") // 4, kept["gelu"], d_down, kept["low"], d_up, kept["ctx"], d_attn, hid, d_qkv, grads[0]
+        lax.axis_size("dp") // 4, saved["gelu"], grads["d_down"], saved["low"], grads["d_up"],
+        saved["ctx"], grads["d_attn"], saved["hid"], grads["d_qkv"], small,
     )
     g_down, g_up, g_out, g_qkv = [value.astype(F32)[None] for value in large]
     small = small[None]

time: 436 us -> 317 us (0.73); the launches traced: 430 us -> 316 us
  waiting for transfers between devices: 126 us -> 0 us
  Pallas kernels: 267 us -> 293 us
  starting transfers between devices: 9.72 us -> 0 us
    ppermute x4 -> x0, waiting for transfers between devices: 126 us -> none  [the longest x2 91.5 us: shards(): received = lax.ppermute(hop, 'section', back)]
    pallas_call x6 -> x2, Pallas kernels: 120 us -> 146 us  [the longest x1 88.6 us: backward(): pl.pallas_call(functools.partial(backward_kernel, sequences), out_shape=s...]
    ppermute x4 -> x0, starting transfers between devices: 9.72 us -> none  [the longest x2 7.13 us: shards(): received = lax.ppermute(hop, 'section', onward)]
  transfers between devices with their start and end apart: 4 -> 0, of which waited for: 4 -> 0; matrix products, arithmetic and copies ran while one was open for 0% -> 0% of each run, Pallas kernels for 0% -> 0%
where the time goes in v3:
time: 317 us; the launch traced here: 316 us
  Pallas kernels  293 us (92%)
  other arithmetic  16.5 us (5%)
  local copies, waits for them, and re-layouts  6.64 us (2%)
    pallas_call x1, Pallas kernels, reduce_gradients(): pl.pallas_call(functools.partial(reduce_kernel, depth), out_shape=[jax.Sh...  147 us
    pallas_call x1, Pallas kernels, backward(): pl.pallas_call(functools.partial(backward_kernel, sequences), out_shape=s...  88.6 us
    pallas_call x1, Pallas kernels, forward(): pl.pallas_call(functools.partial(forward_kernel, sequences), out_shape=sh...  56.9 us
    broadcast_in_dim x4, other arithmetic, shards(): g_down, g_up, g_out, g_qkv = [value.astype(F32)[None] for value in large]  16.5 us

profile of v3, /device:TPU:0, one launch (start us, length us, event | category | flops | bytes accessed | tf_op | source)
XLA Modules:
  0.0 316.4 jit_solution(6488080090622092260)
XLA Ops:
  0.6 56.9 %forward.1 = (bf16[1024,768]{1,0:T(8,128)(2,1)}, bf16[4,512,1536]{2,1,0:T(8,128)(2,1)}, bf16[4,12,256,512]{3,2,1,0:T(8,128)(2,1)}, bf16[1024,768]{1,0:T(8,128)(2...) custom-call(bf16[1024,768]{1,0:T(8,128)(2,1)} %refs_0_.2, ...), custom_call_target="tpu_custom_call" | custom-call | tf_op jit(solution)/shard_map/forward/pallas_call | solution.py:374
  57.6 88.6 %backward.1 = (bf16[1024,768]{1,0:T(8,128)(2,1)}, f32[16,768]{1,0:T(8,128)}, bf16[1024,768]{1,0:T(8,128)(2,1)}, bf16[1024,3072]{1,0:T(8,128)(2,1)}, bf16[1024,76...) custom-call(bf16[1024,768]{1,0:T(8,128)(2,1)} %refs_0_.3, bf16[1,768,2304]{2,1,0:T(8,128)(2,1)} %refs_1_.3, ...), custom_call_target="tpu_custom_call" | custom-call | tf_op jit(solution)/shard_map/backward/pallas_call | solution.py:636
  146.2 147.1 %reduce_gradients.1 = (bf16[3072,768]{1,0:T(8,128)(2,1)}, bf16[768,3072]{1,0:T(8,128)(2,1)}, bf16[768,768]{1,0:T(8,128)(2,1)}, bf16[768,2304]{1,0:T(8,128)(2,1)}, f32[16,768]{1,0:T(8,128)}) custom-call(bf16[1024,3072]{1,0:T(8,128)(2,1)} %get-tuple-element.48.refs_0_, bf16[1024,768]{1,0:T(8,128)(2,1)} %get-tuple-element.49.refs_1_, ...), custom_call_target="tpu_custom_call" | custom-call | tf_op jit(solution)/shard_map/reduce_gradients/pallas_call | solution.py:1096
  293.2 0.0 copy-start.1
  293.3 0.9 slice_bitcast_fusion
  294.1 1.6 fusion
  295.7 0.6 copy.24
  296.3 2.8 bitcast_convert_fusion.3
  299.2 0.0 copy-done.1
  299.2 0.0 copy-start
  299.2 0.0 slice-start
  299.2 4.1 %bitcast_convert_fusion.2 = f32[1,768,2304]{2,1,0:T(8,128)} fusion(bf16[768,2304]{1,0:T(8,128)(2,1)S(1)} %copy-done.1), kind=kLoop, calls=%fused_computation.2 | loop fusion | flops 1769472 | bytes 10616832 | tf_op jit(solution)/shard_map/broadcast_in_dim | solution.py:1145
  303.3 0.4 copy-done
  303.7 0.0 slice-start.1
  303.7 5.0 %bitcast_convert_fusion.1 = f32[1,768,3072]{2,1,0:T(8,128)} fusion(bf16[768,3072]{1,0:T(8,128)(2,1)S(1)} %copy-done), kind=kLoop, calls=%fused_computation.1 | loop fusion | flops 2359296 | bytes 14155776 | tf_op jit(solution)/shard_map/broadcast_in_dim | solution.py:1145
  308.8 0.0 slice-done
  308.8 0.0 slice-done.1
  308.8 0.0 copy-start.2
  308.8 4.5 %bitcast_convert_fusion = f32[1,3072,768]{2,1,0:T(8,128)} fusion(bf16[3072,768]{1,0:T(8,128)(2,1)S(1)} %bitcast.19), kind=kLoop, calls=%fused_computation | loop fusion | flops 2359296 | bytes 14155776 | tf_op jit(solution)/shard_map/broadcast_in_dim | solution.py:1145
  313.3 0.0 copy-done.2
  313.3 0.0 copy-start.3
  313.3 1.1 copy.27
  314.4 0.8 copy-done.3
  315.2 1.1 copy.28
  (1 shorter events, 0.0 us)
Async XLA Ops:
  293.2 5.9 %copy-start.1 = (bf16[768,2304]{1,0:T(8,128)(2,1)S(1)}, bf16[768,2304]{1,0:T(8,128)(2,1)}, u32[]{:S(2)}) copy-start(bf16[768,2304]{1,0:T(8,128)(2,1)} %get-tuple-element.56) | copy-start | bytes 10616836
  299.2 4.5 %copy-start = (bf16[768,3072]{1,0:T(8,128)(2,1)S(1)}, bf16[768,3072]{1,0:T(8,128)(2,1)}, u32[]{:S(2)}) copy-start(bf16[768,3072]{1,0:T(8,128)(2,1)} %get-tuple-element.59) | copy-start | bytes 14155780
  299.2 9.6 %slice-start = ((s8[4718592]{0:T(1024)(128)(4,1)}), s8[4194304]{0:T(1024)(128)(4,1)S(1)}, s32[]{:S(2)}) async-start(s8[4718592]{0:T(1024)(128)(4,1)} %bitcast.18), calls=%async_computation | async-start | bytes 8388608
  303.7 5.1 %slice-start.1 = ((s8[4718592]{0:T(1024)(128)(4,1)}), s8[524288]{0:T(1024)(128)(4,1)S(1)}, s32[]{:S(2)}) async-start(s8[4718592]{0:T(1024)(128)(4,1)} %bitcast.18), calls=%async_computation.1 | async-start | bytes 1048576
  308.8 4.5 %copy-start.2 = (bf16[1024,768]{1,0:T(8,128)(2,1)S(1)}, bf16[1024,768]{1,0:T(8,128)(2,1)}, u32[]{:S(2)}) copy-start(bf16[1024,768]{1,0:T(8,128)(2,1)} %get-tuple-element.36) | copy-start | bytes 4718596
  313.3 2.0 copy-start.3

commit v4 on v3

--- a/solution.py
+++ b/solution.py
@@ -16,6 +16,7 @@
 MICRO = 2
 PAIRS = H // 2
 PAIR = 2 * HD
+GROUP = PAIRS // 2
 
 EPSILON = 1e-05
 SCORE_SCALE = 0.125
@@ -23,6 +24,7 @@
 F32 = jnp.float32
 BF16 = jnp.bfloat16
 VMEM_LIMIT = 60 << 20
+REDUCE_LIMIT = 44 << 20
 MESH = pl.DeviceIdType.MESH
 
 ANY = pl.BlockSpec(memory_space=pl.ANY)
@@ -206,7 +208,6 @@
         inputs.spread()
 
     w_rest = [begin(wo.at[0], wo_v, w_sem.at[3]), begin(wu.at[0], wu_v, w_sem.at[4]), begin(wd.at[0], wd_v, w_sem.at[5])]
-    seg_copy.wait()
 
     def save(name, buffer, step):
         target = outs[name].at[pl.ds(pl.multiple_of(step * ROWS, ROWS), ROWS)]
@@ -214,6 +215,11 @@
 
     def free(name, buffer):
         pltpu.make_async_copy(buffer, buffer, save_sem.at[names.index(name)]).wait()
+
+    def free_prob():
+        for group in range(2):
+            view = p_v.at[pl.ds(group * 2 * GROUP, 2 * GROUP)]
+            pltpu.make_async_copy(view, view, p_sem.at[group]).wait()
 
     reused = (
         ("q", q_v), ("linv", linv_v), ("ctx", ctx_v), ("xh1", xh1_v), ("inv1", inv1_v), ("low", low_v),
@@ -221,6 +227,41 @@
     )
 
     def one_step(step, carry):
+        inputs.await_step(step, section == 0)
+        target = outs["hid"].at[pl.ds(pl.multiple_of(step * ROWS, ROWS), ROWS)]
+        pltpu.make_async_copy(h_v.at[step], target, hid_save.at[step]).start()
+        hidden = h_v[step]
+        for block in (1, 2):
+
+            @pl.when(step == 0)
+            def _():
+                w_first[block - 1].wait()
+
+            proj = dot_nn(hidden, wqkv_v[:, block * D : (block + 1) * D])
+            if block == 2:
+                proj = proj + qv_bias[0, 1:2, :]
+            cols = pl.ds((block - 1) * D, D)
+            kv_v[step, place.own, cols] = proj.astype(BF16)
+            view = kv_v.at[step, place.own, cols]
+            remote(view, view, kv_sent.at[step, block - 1], kv_arrived.at[step, block - 1], place.sibling).start()
+
+        @pl.when(step == 0)
+        def _():
+            w_first[2].wait()
+
+        @pl.when(step > 0)
+        def _():
+            for name, buffer in reused:
+                free(name, buffer)
+            free_prob()
+
+        q_v[...] = (dot_nn(hidden, wqkv_v[:, 0:D]) + qv_bias[0, 0:1, :]).astype(BF16)
+        save("q", q_v, step)
+
+        @pl.when(step == 0)
+        def _():
+            seg_copy.wait()
+
         sequence = lax.rem(step, sequences)
         mine = jnp.where(place.is_mine(step, sequences), 1.0, 0.0)
         key_rows = mine * seg_own[sequence] + (1.0 - mine) * seg_their[sequence]
@@ -233,43 +274,12 @@
             visible = (key_rows[1:2, cols] > 0.5) | (key + tile * 128 == query)
             bias_v[:, cols] = jnp.where((query_seg == key_rows[0:1, cols]) & visible, 0.0, NEG_FILL)
 
-        inputs.await_step(step, section == 0)
-        target = outs["hid"].at[pl.ds(pl.multiple_of(step * ROWS, ROWS), ROWS)]
-        pltpu.make_async_copy(h_v.at[step], target, hid_save.at[step]).start()
-        hidden = h_v[step]
-        for block in (1, 2):
-
-            @pl.when(step == 0)
-            def _():
-                w_first[block - 1].wait()
-
-            proj = dot_nn(hidden, wqkv_v[:, block * D : (block + 1) * D])
-            if block == 2:
-                proj = proj + qv_bias[0, 1:2, :]
-            cols = pl.ds((block - 1) * D, D)
-            kv_v[step, place.own, cols] = proj.astype(BF16)
-            view = kv_v.at[step, place.own, cols]
-            remote(view, view, kv_sent.at[step, block - 1], kv_arrived.at[step, block - 1], place.sibling).start()
-
-        @pl.when(step == 0)
-        def _():
-            w_first[2].wait()
-
-        @pl.when(step > 0)
-        def _():
-            for name, buffer in reused:
-                free(name, buffer)
-            for pair in range(PAIRS):
-                pltpu.make_async_copy(p_v.at[pair], p_v.at[pair], p_sem.at[pair]).wait()
-
-        q_v[...] = (dot_nn(hidden, wqkv_v[:, 0:D]) + qv_bias[0, 0:1, :]).astype(BF16)
-        save("q", q_v, step)
         for block in range(2):
             view = kv_v.at[step, place.theirs, pl.ds(block * D, D)]
             remote(view, view, kv_sent.at[step, block], kv_arrived.at[step, block], place.sibling).wait_recv()
         pltpu.make_async_copy(kv_v.at[step], kv_out.at[step], kv_save.at[step]).start()
 
-        def pair_step(pair, carry):
+        def pair_step(pair):
             at = pl.multiple_of(pair * PAIR, PAIR)
             q2 = q_v[:, pl.ds(at, PAIR)] * SCORE_SCALE
             k2 = kv_v[step, :, pl.ds(at, PAIR)]
@@ -281,17 +291,22 @@
                 exp_vals = jnp.exp(scores - jnp.max(scores, axis=-1, keepdims=True))
                 inverses.append(1.0 / jnp.sum(exp_vals, axis=-1, keepdims=True))
                 weight = exp_vals.astype(BF16)
-                p_v[pair, head] = weight
+                p_v[pair * 2 + head] = weight
                 part = dot_nn(weight, v2 * mask)
                 total = part if total is None else total + part
             lane = lax.broadcasted_iota(jnp.int32, (1, PAIR), 1)
             inverse = jnp.where(lane < HD, inverses[0], inverses[1])
             linv_v[:, pl.ds(at, PAIR)] = inverse
             ctx_v[:, pl.ds(at, PAIR)] = (total * inverse).astype(BF16)
-            pltpu.make_async_copy(p_v.at[pair], prob_out.at[step, pl.ds(pair * 2, 2)], p_sem.at[pair]).start()
+
+        def group_step(group, carry):
+            for index in range(GROUP):
+                pair_step(group * GROUP + index)
+            target = prob_out.at[step, pl.ds(group * 2 * GROUP, 2 * GROUP)]
+            pltpu.make_async_copy(p_v.at[pl.ds(group * 2 * GROUP, 2 * GROUP)], target, p_sem.at[group]).start()
             return carry
 
-        lax.fori_loop(0, PAIRS, pair_step, 0, unroll=3)
+        lax.fori_loop(0, 2, group_step, 0)
         save("linv", linv_v, step)
         save("ctx", ctx_v, step)
 
@@ -349,8 +364,7 @@
         for block in range(2):
             view = kv_v.at[step, place.own, pl.ds(block * D, D)]
             remote(view, view, kv_sent.at[step, block], kv_arrived.at[step, block], place.sibling).wait_send()
-    for pair in range(PAIRS):
-        pltpu.make_async_copy(p_v.at[pair], p_v.at[pair], p_sem.at[pair]).wait()
+    free_prob()
 
     @pl.when(section == 0)
     def _():
@@ -380,7 +394,7 @@
             pltpu.VMEM((steps, ROWS, D), BF16),
             pltpu.VMEM((steps, ROWS, D), BF16),
             pltpu.VMEM((steps, SEQ, 2 * D), BF16),
-            pltpu.VMEM((PAIRS, 2, ROWS, SEQ), BF16),
+            pltpu.VMEM((H, ROWS, SEQ), BF16),
             pltpu.VMEM((D, 3 * D), BF16),
             pltpu.VMEM((D, D), BF16),
             pltpu.VMEM((D, FF), BF16),
@@ -394,7 +408,7 @@
         + [
             dma((6,)),
             dma((len(SAVED),)),
-            dma((PAIRS,)),
+            dma((2,)),
             dma((sequences,)),
             dma((sequences,)),
             dma((steps,)),
@@ -482,6 +496,11 @@
         def _():
             for copy in copies:
                 copy.wait()
+
+    def free_parts():
+        for group in range(2):
+            view = part_v.at[pl.ds(group * GROUP, GROUP), place.theirs]
+            remote(view, view, part_sent.at[group], part_arrived.at[0, 0], place.sibling).wait_send()
 
     place.greet()
 
@@ -549,11 +568,9 @@
 
         @pl.when(step > 0)
         def _():
-            for pair in range(PAIRS):
-                view = part_v.at[pair, place.theirs]
-                remote(view, view, part_sent.at[pair], part_arrived.at[0, 0], place.sibling).wait_send()
-
-        def pair_step(pair, carry):
+            free_parts()
+
+        def pair_step(pair):
             at = pl.multiple_of(pair * PAIR, PAIR)
             q2 = q_v[:, pl.ds(at, PAIR)] * SCORE_SCALE
             k2 = kv_v[:, pl.ds(at, PAIR)]
@@ -577,26 +594,39 @@
             d_qkv_v[:, pl.ds(at, PAIR)] = (d_q * SCORE_SCALE).astype(BF16)
             part_v[pair, :, 0:PAIR] = jnp.transpose(d_k).astype(BF16)
             part_v[pair, :, PAIR : 2 * PAIR] = jnp.transpose(d_v).astype(BF16)
+
+        def group_step(group, carry):
+            for index in range(GROUP):
+                pair_step(group * GROUP + index)
+            pairs = pl.ds(group * GROUP, GROUP)
             remote(
-                part_v.at[pair, place.theirs], their_v.at[step, pair], part_sent.at[pair],
-                part_arrived.at[step, pair], place.sibling,
+                part_v.at[pairs, place.theirs], their_v.at[step, pairs], part_sent.at[group],
+                part_arrived.at[step, group], place.sibling,
             ).start()
             return carry
 
-        lax.fori_loop(0, PAIRS, pair_step, 0, unroll=3)
+        lax.fori_loop(0, 2, group_step, 0)
         fetch_next(("q", "linv", "ctx", "kv", "prob"), step)
         when_first(step, (get_wqkv,))
         d_query = d_qkv_v[:, 0:D]
         acc_v[...] += dot_nt(d_query, wqkv_v[:, 0:D])
         small_out[0:1, :] += column_sum(d_query.astype(F32))
-        for pair in range(PAIRS):
-            view = their_v.at[step, pair]
-            remote(view, view, part_sent.at[pair], part_arrived.at[step, pair], place.sibling).wait_recv()
-            total = part_v[pair, place.own, :].astype(F32) + their_v[step, pair].astype(F32)
-            at = pair * PAIR
-            d_qkv_v[:, D + at : D + at + PAIR] = total[:, 0:PAIR].astype(BF16)
-            d_qkv_v[:, 2 * D + at : 2 * D + at + PAIR] = total[:, PAIR : 2 * PAIR].astype(BF16)
-        d_hid_v[step] = (acc_v[...] + dot_nt(d_qkv_v[:, D : 3 * D], wqkv_v[:, D : 3 * D])).astype(BF16)
+        for group in range(2):
+            start = group * GROUP
+            view = their_v.at[step, pl.ds(start, GROUP)]
+            remote(view, view, part_sent.at[group], part_arrived.at[step, group], place.sibling).wait_recv()
+            for pair in range(start, start + GROUP):
+                total = part_v[pair, place.own, :].astype(F32) + their_v[step, pair].astype(F32)
+                at = pair * PAIR
+                d_qkv_v[:, D + at : D + at + PAIR] = total[:, 0:PAIR].astype(BF16)
+                d_qkv_v[:, 2 * D + at : 2 * D + at + PAIR] = total[:, PAIR : 2 * PAIR].astype(BF16)
+            keys = slice(D + start * PAIR, D + (start + GROUP) * PAIR)
+            values = slice(2 * D + start * PAIR, 2 * D + (start + GROUP) * PAIR)
+            d_hid = acc_v[...] + dot_nt(d_qkv_v[:, keys], wqkv_v[:, keys]) + dot_nt(d_qkv_v[:, values], wqkv_v[:, values])
+            if start == 0:
+                acc_v[...] = d_hid
+            else:
+                d_hid_v[step] = d_hid.astype(BF16)
 
         @pl.when(section == 1)
         def _():
@@ -610,9 +640,7 @@
     lax.fori_loop(0, steps, one_step, 0)
     for name, buffer in zip(grad_names, (d_down_v, d_up_v, d_attn_v, d_qkv_v)):
         free(name, buffer)
-    for pair in range(PAIRS):
-        view = part_v.at[pair, place.theirs]
-        remote(view, view, part_sent.at[pair], part_arrived.at[0, 0], place.sibling).wait_send()
+    free_parts()
 
     @pl.when(section == 1)
     def _():
@@ -664,8 +692,8 @@
             dma((sequences,)),
             dma((sequences,)),
             dma((sequences,)),
-            dma((PAIRS,)),
-            dma((steps, PAIRS)),
+            dma((2,)),
+            dma((steps, 2)),
             dma((steps,)),
         ],
         compiler_params=pltpu.CompilerParams(
@@ -677,27 +705,28 @@
 
 
 UNIT = 16
-RAIL = 4 * UNIT
-ROOTS = 4
-HALF = 2 * RAIL + ROOTS * UNIT
-SLAB = 2 * HALF
+SLAB = D
+WIDTH = D // 2
+HALF = SLAB // 2
+RAIL = 7 * UNIT
+LINES = (3 * UNIT, 2 * UNIT, 2 * UNIT, 3 * UNIT)
+SLABS = 2 * FF // D + FF // WIDTH + D // WIDTH + 3 * D // WIDTH
 
 
 def reduce_kernel(depth, *refs):
     (gelu, d_down, low, d_up, ctx, d_attn, hid, d_qkv, small) = refs[:9]
-    (o_down, o_up, o_out, o_qkv, o_small) = refs[9:14]
+    (o_v, o_small) = refs[9:11]
     (
-        left_v, right_v, p_v, s_v, y_v, rl_v, rr_v, o_v, sm_v, sm_in_v, sm_o_v,
-        load_sem, send_sem, recv_sem, out_sem, sm_send, sm_recv,
-    ) = refs[14:]
-    columns = d_down.shape[1]
+        left_v, right_v, p_v, s_v, y_v, rl_v, rr_v, sm_v, sm_in_v, sm_o_v,
+        load_sem, send_sem, recv_sem, sm_send, sm_recv,
+    ) = refs[11:]
     plan = (
-        ("down", FF // SLAB, gelu, d_down, o_down),
-        ("up", 2 * (FF // D), low, d_up, o_up),
-        ("out", 2, ctx, d_attn, o_out),
-        ("qkv", 6, hid, d_qkv, o_qkv),
+        (2 * FF // D, gelu, d_down),
+        (FF // WIDTH, low, d_up),
+        (D // WIDTH, ctx, d_attn),
+        (3 * D // WIDTH, hid, d_qkv),
     )
-    count = sum(entry[1] for entry in plan)
+    count = SLABS
     section = lax.axis_index("section")
     me = lax.axis_index("dp")
     core = lax.rem(me, 2)
@@ -726,42 +755,19 @@
     def load(step, start):
         slot = lax.rem(step, 2)
         if not start:
-            pltpu.make_async_copy(gelu.at[:, pl.ds(0, SLAB)], left_v.at[slot], load_sem.at[0, slot]).wait()
-            pltpu.make_async_copy(d_down, right_v.at[slot], load_sem.at[1, slot]).wait()
+            pltpu.make_async_copy(low, left_v.at[slot], load_sem.at[0, slot]).wait()
+            pltpu.make_async_copy(d_down.at[:, pl.ds(0, WIDTH)], right_v.at[slot], load_sem.at[1, slot]).wait()
             return
         first = 0
-        for name, steps, factor, grad, _ in plan:
-
-            def issue(first=first, name=name, factor=factor, grad=grad):
+        for steps, factor, grad in plan:
+
+            def issue(first=first, factor=factor, grad=grad):
                 index = step - first
-                if name == "down":
-                    row, column = index, 0
-                else:
-                    row, column = lax.rem(index, 2), lax.div(index, 2)
-                rows = pl.ds(pl.multiple_of(row * SLAB, 128), SLAB)
-                cols = pl.ds(pl.multiple_of(column * columns, 128), columns)
+                halves = grad.shape[1] // WIDTH
+                rows = pl.ds(pl.multiple_of(lax.div(index, halves) * SLAB, 128), SLAB)
+                cols = pl.ds(pl.multiple_of(lax.rem(index, halves) * WIDTH, 128), WIDTH)
                 pltpu.make_async_copy(factor.at[:, rows], left_v.at[slot], load_sem.at[0, slot]).start()
                 pltpu.make_async_copy(grad.at[:, cols], right_v.at[slot], load_sem.at[1, slot]).start()
-
-            pl.when((step >= first) & (step < first + steps))(issue)
-            first += steps
-
-    def out_copy(step, start):
-        slot = lax.rem(step, 2)
-        if not start:
-            pltpu.make_async_copy(o_v.at[0], o_down.at[pl.ds(0, SLAB)], out_sem.at[slot]).wait()
-            return
-        first = 0
-        for name, steps, _, _, result in plan:
-
-            def issue(first=first, name=name, result=result):
-                index = step - first
-                if name == "down":
-                    row, column = index, 0
-                else:
-                    row, column = lax.rem(index, 2), lax.div(index, 2)
-                cols = pl.ds(pl.multiple_of(column * columns, 128), columns)
-                pltpu.make_async_copy(o_v.at[step], result.at[at(row * SLAB, SLAB), cols], out_sem.at[slot]).start()
 
             pl.when((step >= first) & (step < first + steps))(issue)
             first += steps
@@ -844,7 +850,7 @@
                     if self.rail:
                         self.total(step)[...] = self.part(step)[...]
                     else:
-                        view = y_v.at[step, pl.ds(RAIL, UNIT)]
+                        view = y_v.at[step, pl.ds(RAIL, self.size)]
                         send(YX, step, self.part(step), view, recv_sem.at[YX, step], partner)
 
             if not self.rail:
@@ -852,7 +858,7 @@
 
                 @pl.when((z == self.root) & (late >= 0) & (late < count))
                 def _():
-                    view = y_v.at[late, pl.ds(RAIL, UNIT)]
+                    view = y_v.at[late, pl.ds(RAIL, self.size)]
                     arrived(YX, late, view)
                     self.total(late)[...] = (self.part(late)[...].astype(F32) + view[...].astype(F32)).astype(BF16)
 
@@ -914,11 +920,13 @@
     rail_root = half_depth - 1 + y
     rail = Tree((5, 6, 7, 8), 2, rail_root, half_depth, RAIL, y * RAIL, 0, True)
     line = []
-    for index in range(ROOTS):
-        root = (2 * index + 1) * depth // (2 * ROOTS)
-        kinds = tuple(9 + 4 * index + offset for offset in range(4))
+    offset = 0
+    for index, size in enumerate(LINES):
+        root = (2 * index + 1) * depth // (2 * len(LINES))
+        kinds = tuple(9 + 4 * index + kind for kind in range(4))
         reach = max(root, depth - 1 - root)
-        line.append(Tree(kinds, 1, root, reach, UNIT, 2 * RAIL + index * UNIT, RAIL + index * UNIT, False))
+        line.append(Tree(kinds, 1, root, reach, size, 2 * RAIL + offset, RAIL + offset, False))
+        offset += size
     other_distance = jnp.abs(z - (half_depth - y))
     other = (1 - y) * RAIL
 
@@ -1002,7 +1010,7 @@
     neighbours = 2 + (z > 0).astype(jnp.int32) + (z < depth - 1).astype(jnp.int32)
     pl.semaphore_wait(barrier, neighbours)
 
-    out_lag = max(
+    last = max(
         [2 + half_depth + half_depth + 2] + [2 + tree.reach + max(tree.root, depth - 1 - tree.root) + 1 for tree in line]
     )
 
@@ -1064,21 +1072,9 @@
 
         small_round(now)
 
-        step_out = now - out_lag
-
-        @pl.when(step_out >= 0)
-        def _():
-            @pl.when(step_out >= 2)
-            def _():
-                out_copy(step_out, False)
-
-            out_copy(step_out, True)
-
         return carry
 
-    lax.fori_loop(0, count + out_lag, one_round, 0)
-    out_copy(jnp.int32(0), False)
-    out_copy(jnp.int32(1), False)
+    lax.fori_loop(0, count + last, one_round, 0)
     finish_send(CX, s_v.at[0])
     finish_send(UP, rail.part(0))
     finish_send(DOWN, rail.part(0))
@@ -1090,44 +1086,98 @@
 
 
 def reduce_gradients(depth, gelu, d_down, low, d_up, ctx, d_attn, hid, d_qkv, small):
-    rows, columns = d_down.shape
-    count = FF // SLAB + 2 * (FF // D) + 8
-    kinds = 9 + 4 * ROOTS
+    rows = d_down.shape[0]
+    columns = WIDTH
+    count = SLABS
+    kinds = 9 + 4 * len(LINES)
     return pl.pallas_call(
         functools.partial(reduce_kernel, depth),
         out_shape=[
-            jax.ShapeDtypeStruct((FF, columns), BF16),
-            jax.ShapeDtypeStruct((D, 4 * columns), BF16),
-            jax.ShapeDtypeStruct((D, columns), BF16),
-            jax.ShapeDtypeStruct((D, 3 * columns), BF16),
+            pltpu.VMEM((count, SLAB, columns), BF16),
             jax.ShapeDtypeStruct((SMALL_ROWS, small.shape[-1]), F32),
         ],
         in_specs=[ANY] * 8 + [VMEM],
-        out_specs=[ANY] * 4 + [VMEM],
+        out_specs=[VMEM] * 2,
         scratch_shapes=[
             pltpu.VMEM((2, rows, SLAB), BF16),
             pltpu.VMEM((2, rows, columns), BF16),
             pltpu.VMEM((2, SLAB, columns), BF16),
             pltpu.VMEM((count, HALF, columns), BF16),
-            pltpu.VMEM((count, RAIL + UNIT, columns), BF16),
-            pltpu.VMEM((count, RAIL + ROOTS * UNIT, columns), BF16),
-            pltpu.VMEM((count, RAIL + ROOTS * UNIT, columns), BF16),
-            pltpu.VMEM((count, SLAB, columns), BF16),
+            pltpu.VMEM((count, RAIL + max(LINES), columns), BF16),
+            pltpu.VMEM((count, RAIL + sum(LINES), columns), BF16),
+            pltpu.VMEM((count, RAIL + sum(LINES), columns), BF16),
             pltpu.VMEM((SMALL_ROWS, small.shape[-1]), F32),
             pltpu.VMEM((4, SMALL_ROWS, small.shape[-1]), F32),
             pltpu.VMEM((SMALL_ROWS, small.shape[-1]), F32),
             pltpu.SemaphoreType.DMA((2, 2)),
             pltpu.SemaphoreType.DMA((kinds, 2)),
             pltpu.SemaphoreType.DMA((kinds, count)),
-            pltpu.SemaphoreType.DMA((2,)),
             pltpu.SemaphoreType.DMA((4,)),
             pltpu.SemaphoreType.DMA((5,)),
         ],
         compiler_params=pltpu.CompilerParams(
-            collective_id=0, has_side_effects=True, vmem_limit_bytes=VMEM_LIMIT
+            collective_id=0, has_side_effects=True, vmem_limit_bytes=REDUCE_LIMIT
         ),
         name="reduce_gradients",
     )(gelu, d_down, low, d_up, ctx, d_attn, hid, d_qkv, small)
+
+
+def finish_kernel(*refs):
+    (totals, small, act, d_hid) = refs[:4]
+    (o_act, o_hid, o_down, o_up, o_out, o_qkv, o_qv, o_bias, o_gain, o_shift, o_up_bias) = refs[4:15]
+    stage_v, stage_sem, move_sem = refs[15:]
+    moves = [begin(act, o_act.at[0], move_sem.at[0]), begin(d_hid, o_hid.at[0], move_sem.at[1])]
+    o_qv[0] = small[0:2, :]
+    o_bias[0] = small[2:4, :]
+    o_gain[0] = small[4:6, :]
+    o_shift[0] = small[6:8, :]
+    for part in range(FF // D):
+        o_up_bias[0:1, part * D : (part + 1) * D] = small[8 + part : 9 + part, :]
+    places = []
+    for array in (o_down, o_up, o_out, o_qkv):
+        _, rows, columns = array.shape
+        places += [(array, row, column) for row in range(rows // SLAB) for column in range(columns // WIDTH)]
+    slots = stage_v.shape[0]
+    copies = []
+    for index, (array, row, column) in enumerate(places):
+        slot = index % slots
+        if index >= slots:
+            copies[index - slots].wait()
+        stage_v[slot] = totals[index].astype(F32)
+        target = array.at[0, pl.ds(row * SLAB, SLAB), pl.ds(column * WIDTH, WIDTH)]
+        copies.append(begin(stage_v.at[slot], target, stage_sem.at[slot]))
+    for copy in copies[-slots:] + moves:
+        copy.wait()
+
+
+def finish(totals, small, act, d_hid):
+    slots = 6
+    shapes = [
+        jax.ShapeDtypeStruct((1, *act.shape), BF16),
+        jax.ShapeDtypeStruct((1, *act.shape), BF16),
+        jax.ShapeDtypeStruct((1, FF, D), F32),
+        jax.ShapeDtypeStruct((1, D, FF), F32),
+        jax.ShapeDtypeStruct((1, D, D), F32),
+        jax.ShapeDtypeStruct((1, D, 3 * D), F32),
+        jax.ShapeDtypeStruct((1, 2, D), F32),
+        jax.ShapeDtypeStruct((1, 2, D), F32),
+        jax.ShapeDtypeStruct((1, 2, D), F32),
+        jax.ShapeDtypeStruct((1, 2, D), F32),
+        jax.ShapeDtypeStruct((1, FF), F32),
+    ]
+    return pl.pallas_call(
+        finish_kernel,
+        out_shape=shapes,
+        in_specs=[VMEM, VMEM, ANY, ANY],
+        out_specs=[ANY] * 6 + [VMEM] * 5,
+        scratch_shapes=[
+            pltpu.VMEM((slots, SLAB, WIDTH), F32),
+            pltpu.SemaphoreType.DMA((slots,)),
+            pltpu.SemaphoreType.DMA((2,)),
+        ],
+        compiler_params=pltpu.CompilerParams(vmem_limit_bytes=16 << 20),
+        name="finish",
+    )(pltpu.with_memory_space_constraint(totals, pltpu.VMEM), small, act, d_hid)
 
 
 def shards(
@@ -1138,16 +1188,14 @@
     params = (qv_bias, out_biases, norm_gains, norm_shifts, up_bias)
     act, kv, prob, saved = forward(tokens, weights, segments, lengths, params)
     d_hid, small, grads = backward(cotangent, weights, norm_gains, kv, prob, saved)
-    *large, small = reduce_gradients(
+    totals, small = reduce_gradients(
         lax.axis_size("dp") // 4, saved["gelu"], grads["d_down"], saved["low"], grads["d_up"],
         saved["ctx"], grads["d_attn"], saved["hid"], grads["d_qkv"], small,
     )
-    g_down, g_up, g_out, g_qkv = [value.astype(F32)[None] for value in large]
-    small = small[None]
-    return (
-        act[None], d_hid[None], g_qkv, small[:, 0:2], g_out, small[:, 2:4], small[:, 4:6], small[:, 6:8],
-        g_up, small[:, 8:12].reshape(1, FF), g_down,
-    )
+    (
+        o_act, o_hid, g_down, g_up, g_out, g_qkv, g_qv, g_bias, g_gain, g_shift, g_up_bias
+    ) = finish(totals, small, act, d_hid)
+    return (o_act, o_hid, g_qkv, g_qv, g_out, g_bias, g_gain, g_shift, g_up, g_up_bias, g_down)
 
 
 def solution(mesh):

time: 317 us -> 301 us (0.950)
  other arithmetic: 16.5 us -> 0 us
  Pallas kernels: 293 us -> 299 us
  local copies, waits for them, and re-layouts: 6.64 us -> 0.8 us
    broadcast_in_dim x4 -> x0, other arithmetic: 16.5 us -> none  [shards(): g_down, g_up, g_out, g_qkv = [value.astype(F32)[None] for value in large]]
    pallas_call x1 -> x2, Pallas kernels: 147 us -> 156 us  [the longest x1 145 us: reduce_gradients(): pl.pallas_call(functools.partial(reduce_kernel, depth), out_shape=[pltpu....]
    unnamed x16 -> x6, local copies, waits for them, and re-layouts: 5.06 us -> 0.8 us
where the time goes in v4:
time: 301 us
  Pallas kernels  299 us (99%)
    pallas_call x1, Pallas kernels, reduce_gradients(): pl.pallas_call(functools.partial(reduce_kernel, depth), out_shape=[pltpu....  145 us
    pallas_call x1, Pallas kernels, backward(): pl.pallas_call(functools.partial(backward_kernel, sequences), out_shape=s...  86.4 us
    pallas_call x1, Pallas kernels, forward(): pl.pallas_call(functools.partial(forward_kernel, sequences), out_shape=sh...  56.9 us
    pallas_call x1, Pallas kernels, finish(): pl.pallas_call(finish_kernel, out_shape=shapes, in_specs=[VMEM, VMEM, ANY...  11 us

profile of v4, /device:TPU:0, one launch (start us, length us, event | category | flops | bytes accessed | tf_op | source)
XLA Modules:
  0.0 301.1 jit_solution(7651089089814696182)
XLA Ops:
  0.6 56.9 %forward.1 = (bf16[1024,768]{1,0:T(8,128)(2,1)}, bf16[4,512,1536]{2,1,0:T(8,128)(2,1)}, bf16[4,12,256,512]{3,2,1,0:T(8,128)(2,1)}, bf16[1024,768]{1,0:T(8,128)(2...) custom-call(bf16[1024,768]{1,0:T(8,128)(2,1)} %refs_0_.2, ...), custom_call_target="tpu_custom_call" | custom-call | tf_op jit(solution)/shard_map/forward/pallas_call | solution.py:388
  57.5 86.4 %backward.1 = (bf16[1024,768]{1,0:T(8,128)(2,1)}, f32[16,768]{1,0:T(8,128)}, bf16[1024,768]{1,0:T(8,128)(2,1)}, bf16[1024,3072]{1,0:T(8,128)(2,1)}, bf16[1024,76...) custom-call(bf16[1024,768]{1,0:T(8,128)(2,1)} %refs_0_.3, bf16[1,768,2304]{2,1,0:T(8,128)(2,1)} %refs_1_.3, ...), custom_call_target="tpu_custom_call" | custom-call | tf_op jit(solution)/shard_map/backward/pallas_call | solution.py:664
  144.0 0.0 copy-start
  144.0 0.0 copy-start.1
  144.0 145.1 %reduce_gradients.1 = (bf16[24,768,384]{2,1,0:T(8,128)(2,1)S(1)}, f32[16,768]{1,0:T(8,128)}) custom-call(bf16[1024,3072]{1,0:T(8,128)(2,1)} %get-tuple-element.44.refs_0_, bf16[1024,768]{1,0:T(8,128)(2,1)} %get-tuple-element.55.refs_1_, bf16[1024,768]{1,0:T(8,128)(2,1)} %get-tuple-element.56.refs_2_, bf16[1024,3072]{1,0:T(8,128)(2,1)} %get-tuple-element.57.refs_3_, ...), custom_call_target="tpu_custom_call" | custom-call | tf_op jit(solution)/shard_map/reduce_gradients/pallas_call | solution.py:1093
  289.1 0.0 copy-done
  289.1 0.0 copy-done.1
  289.1 0.0 copy-start.2
  289.2 0.8 copy-done.2
  289.9 11.0 %finish.1 = (bf16[1,1024,768]{2,1,0:T(8,128)(2,1)}, bf16[1,1024,768]{2,1,0:T(8,128)(2,1)}, f32[1,3072,768]{2,1,0:T(8,128)}, f32[1,768,3072]{2,1,0:T(8,128)}, f32...) custom-call(bf16[24,768,384]{2,1,0:T(8,128)(2,1)S(1)} %get-tuple-ele, ...), custom_call_target="tpu_custom_call" | custom-call | tf_op jit(solution)/shard_map/finish/pallas_call | solution.py:1168
Async XLA Ops:
  144.0 145.2 %copy-start = (bf16[1024,768]{1,0:T(8,128)(2,1)S(1)}, bf16[1024,768]{1,0:T(8,128)(2,1)}, u32[]{:S(2)}) copy-start(bf16[1024,768]{1,0:T(8,128)(2,1)} %get-tuple-element.64.refs_2_) | copy-start | bytes 4718596
  144.0 145.2 %copy-start.1 = (bf16[1024,768]{1,0:T(8,128)(2,1)S(1)}, bf16[1024,768]{1,0:T(8,128)(2,1)}, u32[]{:S(2)}) copy-start(bf16[1024,768]{1,0:T(8,128)(2,1)} %get-tuple-element.65.refs_3_) | copy-start | bytes 4718596
  289.1 0.8 copy-start.2

commit v5 on v4

--- a/solution.py
+++ b/solution.py
@@ -77,23 +77,6 @@
 
 
 ROWS = SEQ // 2
-SAVED = (
-    ("hid", D, BF16),
-    ("q", D, BF16),
-    ("linv", D, F32),
-    ("ctx", D, BF16),
-    ("xh1", D, BF16),
-    ("inv1", 128, F32),
-    ("low", D, BF16),
-    ("gelu", FF, BF16),
-    ("slope", FF, BF16),
-    ("xh2", D, BF16),
-    ("inv2", 128, F32),
-)
-GRADS = (("d_down", D, BF16), ("d_up", FF, BF16), ("d_attn", D, BF16), ("d_qkv", 3 * D, BF16))
-SMALL_ROWS = 16
-
-
 class Place:
     def __init__(self):
         self.section = lax.axis_index("section")
@@ -175,68 +158,116 @@
             remote(view, view, self.sent.at[sequence], self.arrived.at[sequence], self.place.sibling).wait()
 
 
-def forward_kernel(sequences, *refs):
-    (tok, wqkv, wo, wu, wd, segs, lens, qv_bias, out_biases, gains, shifts, up_bias) = refs[:12]
-    act_out, kv_out, prob_out = refs[12:15]
-    count = len(SAVED)
-    outs = dict(zip([name for name, _, _ in SAVED], refs[15 : 15 + count]))
+SAVED = (
+    ("hid", D, BF16),
+    ("low", D, BF16),
+    ("gelu", FF, BF16),
+    ("ctx", D, BF16),
+    ("q", D, BF16),
+    ("linv", D, F32),
+    ("xh1", D, BF16),
+    ("inv1", 128, F32),
+    ("slope", FF, BF16),
+    ("xh2", D, BF16),
+    ("inv2", 128, F32),
+)
+GRADS = (("d_down", D, BF16), ("d_up", FF, BF16), ("d_attn", D, BF16), ("d_qkv", 3 * D, BF16))
+SMALL_ROWS = 16
+
+
+def layers_kernel(sequences, *refs):
+    (tok, cot, wqkv, wo, wu, wd, segs, lens, qv_bias, out_biases, gains, shifts, up_bias) = refs[:13]
+    act_out, d_hid_out, small_out, prob_io = refs[13:17]
+    stop = 17 + len(SAVED)
+    saved = dict(zip([name for name, _, _ in SAVED], refs[17:stop]))
+    grads = dict(zip([name for name, _, _ in GRADS], refs[stop : stop + len(GRADS)]))
+    stop += len(GRADS)
     (
-        h_v, act_v, kv_v, p_v, wqkv_v, wo_v, wu_v, wd_v, bias_v, acc_v, seg_own, seg_their,
-        q_v, linv_v, ctx_v, xh1_v, inv1_v, low_v, gelu_v, slope_v, xh2_v, inv2_v,
-        w_sem, save_sem, p_sem, in_local, in_sent, in_arrived, out_local, out_sent, out_arrived,
-        kv_sent, kv_arrived, kv_save, seg_sem, hop_sent, hid_save,
-    ) = refs[15 + count :]
+        h_v, act_v, g_v, d_hid_v, kv_v, p_v, wqkv_v, wo_v, wu_v, wd_v, bias_v, acc_v, seg_own, seg_their,
+        d_ctx_v, part_v, their_v,
+    ) = refs[stop : stop + 17]
+    stop += 17
+    buffers = dict(zip([name for name, _, _ in SAVED if name != "hid"], refs[stop : stop + len(SAVED) - 1]))
+    stop += len(SAVED) - 1
+    grad_buffers = dict(zip([name for name, _, _ in GRADS], refs[stop : stop + len(GRADS)]))
+    stop += len(GRADS)
+    (
+        w_sem, save_sem, hid_sem, grad_sem, p_sem, seg_sem, kv_sent, kv_arrived, part_sent, part_arrived,
+        in_local, in_sent, in_arrived, out_local, out_sent, out_arrived, hop_sent,
+        up_local, up_sent, up_arrived, down_local, down_sent, down_arrived, back_sent,
+    ) = refs[stop:]
     place = Place()
     section = place.section
     steps = 2 * sequences
     names = [name for name, _, _ in SAVED]
+    grad_names = [name for name, _, _ in GRADS]
     inputs = Rows(place, sequences, tok, h_v, in_local, in_sent, in_arrived)
     outputs = Rows(place, sequences, act_out, act_v, out_local, out_sent, out_arrived)
-
+    upstream = Rows(place, sequences, cot, g_v, up_local, up_sent, up_arrived)
+    downstream = Rows(place, sequences, d_hid_out, d_hid_v, down_local, down_sent, down_arrived)
+
+    def at_step(array, step):
+        return array.at[pl.ds(pl.multiple_of(step * ROWS, ROWS), ROWS)]
+
+    def save(name, step):
+        pltpu.make_async_copy(buffers[name], at_step(saved[name], step), save_sem.at[names.index(name)]).start()
+
+    def fetch(name, step):
+        pltpu.make_async_copy(at_step(saved[name], step), buffers[name], save_sem.at[names.index(name)]).start()
+
+    def settle(name):
+        pltpu.make_async_copy(buffers[name], buffers[name], save_sem.at[names.index(name)]).wait()
+
+    def prob_part(group, step):
+        heads = pl.ds(group * 2 * GROUP, 2 * GROUP)
+        return p_v.at[heads], prob_io.at[step, heads], p_sem.at[group]
+
+    def settle_prob():
+        for group in range(2):
+            view, _, sem = prob_part(group, 0)
+            pltpu.make_async_copy(view, view, sem).wait()
+
+    def when_first(step, copies):
+        @pl.when(step == 0)
+        def _():
+            for copy in copies:
+                copy.wait()
+
+    def column_sum(value):
+        return jnp.sum(value, axis=0, keepdims=True)
+
+    get_qkv = [
+        begin(wqkv.at[0, :, pl.ds(block * D, D)], wqkv_v.at[:, pl.ds(block * D, D)], w_sem.at[block])
+        for block in (1, 2, 0)
+    ]
     position = lax.broadcasted_iota(jnp.int32, (1, SEQ), 1)
     for sequence in range(sequences):
         seg_own[sequence, 0:1, :] = segs[sequence : sequence + 1, :].astype(F32)
         seg_own[sequence, 1:2, :] = (position < lens[sequence]).astype(F32)
         seg_own[sequence, 2:8, :] = jnp.zeros((6, SEQ), F32)
-    w_first = [begin(wqkv.at[0, :, pl.ds(block * D, D)], wqkv_v.at[:, pl.ds(block * D, D)], w_sem.at[block]) for block in (1, 2, 0)]
     place.greet()
     seg_copy = remote(seg_own, seg_their, seg_sem.at[0], seg_sem.at[1], place.sibling)
-    seg_copy.start()
 
     @pl.when(section == 0)
     def _():
         inputs.spread()
 
-    w_rest = [begin(wo.at[0], wo_v, w_sem.at[3]), begin(wu.at[0], wu_v, w_sem.at[4]), begin(wd.at[0], wd_v, w_sem.at[5])]
-
-    def save(name, buffer, step):
-        target = outs[name].at[pl.ds(pl.multiple_of(step * ROWS, ROWS), ROWS)]
-        pltpu.make_async_copy(buffer, target, save_sem.at[names.index(name)]).start()
-
-    def free(name, buffer):
-        pltpu.make_async_copy(buffer, buffer, save_sem.at[names.index(name)]).wait()
-
-    def free_prob():
-        for group in range(2):
-            view = p_v.at[pl.ds(group * 2 * GROUP, 2 * GROUP)]
-            pltpu.make_async_copy(view, view, p_sem.at[group]).wait()
-
-    reused = (
-        ("q", q_v), ("linv", linv_v), ("ctx", ctx_v), ("xh1", xh1_v), ("inv1", inv1_v), ("low", low_v),
-        ("gelu", gelu_v), ("slope", slope_v), ("xh2", xh2_v), ("inv2", inv2_v),
-    )
-
-    def one_step(step, carry):
+    @pl.when(section == 1)
+    def _():
+        upstream.spread()
+
+    seg_copy.start()
+    get_wo = begin(wo.at[0], wo_v, w_sem.at[3])
+    get_wu = begin(wu.at[0], wu_v, w_sem.at[4])
+    get_wd = begin(wd.at[0], wd_v, w_sem.at[5])
+    small_out[...] = jnp.zeros_like(small_out)
+
+    def forward_step(step, carry):
         inputs.await_step(step, section == 0)
-        target = outs["hid"].at[pl.ds(pl.multiple_of(step * ROWS, ROWS), ROWS)]
-        pltpu.make_async_copy(h_v.at[step], target, hid_save.at[step]).start()
+        pltpu.make_async_copy(h_v.at[step], at_step(saved["hid"], step), hid_sem.at[step]).start()
         hidden = h_v[step]
         for block in (1, 2):
-
-            @pl.when(step == 0)
-            def _():
-                w_first[block - 1].wait()
-
+            when_first(step, (get_qkv[block - 1],))
             proj = dot_nn(hidden, wqkv_v[:, block * D : (block + 1) * D])
             if block == 2:
                 proj = proj + qv_bias[0, 1:2, :]
@@ -245,22 +276,21 @@
             view = kv_v.at[step, place.own, cols]
             remote(view, view, kv_sent.at[step, block - 1], kv_arrived.at[step, block - 1], place.sibling).start()
 
-        @pl.when(step == 0)
-        def _():
-            w_first[2].wait()
+        def await_keys_or_values(block):
+            view = kv_v.at[step, place.theirs, pl.ds(block * D, D)]
+            remote(view, view, kv_sent.at[step, block], kv_arrived.at[step, block], place.sibling).wait_recv()
+
+        when_first(step, (get_qkv[2],))
 
         @pl.when(step > 0)
         def _():
-            for name, buffer in reused:
-                free(name, buffer)
-            free_prob()
-
-        q_v[...] = (dot_nn(hidden, wqkv_v[:, 0:D]) + qv_bias[0, 0:1, :]).astype(BF16)
-        save("q", q_v, step)
-
-        @pl.when(step == 0)
-        def _():
-            seg_copy.wait()
+            for name in buffers:
+                settle(name)
+            settle_prob()
+
+        buffers["q"][...] = (dot_nn(hidden, wqkv_v[:, 0:D]) + qv_bias[0, 0:1, :]).astype(BF16)
+        save("q", step)
+        when_first(step, (seg_copy,))
 
         sequence = lax.rem(step, sequences)
         mine = jnp.where(place.is_mine(step, sequences), 1.0, 0.0)
@@ -274,73 +304,55 @@
             visible = (key_rows[1:2, cols] > 0.5) | (key + tile * 128 == query)
             bias_v[:, cols] = jnp.where((query_seg == key_rows[0:1, cols]) & visible, 0.0, NEG_FILL)
 
-        for block in range(2):
-            view = kv_v.at[step, place.theirs, pl.ds(block * D, D)]
-            remote(view, view, kv_sent.at[step, block], kv_arrived.at[step, block], place.sibling).wait_recv()
-        pltpu.make_async_copy(kv_v.at[step], kv_out.at[step], kv_save.at[step]).start()
-
-        def pair_step(pair):
-            at = pl.multiple_of(pair * PAIR, PAIR)
-            q2 = q_v[:, pl.ds(at, PAIR)] * SCORE_SCALE
-            k2 = kv_v[step, :, pl.ds(at, PAIR)]
-            v2 = kv_v[step, :, pl.ds(at + D, PAIR)]
-            total, inverses = None, []
-            for head in range(2):
-                mask = half_mask(head)
-                scores = dot_nt(q2, k2 * mask) + bias_v[...]
-                exp_vals = jnp.exp(scores - jnp.max(scores, axis=-1, keepdims=True))
-                inverses.append(1.0 / jnp.sum(exp_vals, axis=-1, keepdims=True))
-                weight = exp_vals.astype(BF16)
-                p_v[pair * 2 + head] = weight
-                part = dot_nn(weight, v2 * mask)
-                total = part if total is None else total + part
-            lane = lax.broadcasted_iota(jnp.int32, (1, PAIR), 1)
-            inverse = jnp.where(lane < HD, inverses[0], inverses[1])
-            linv_v[:, pl.ds(at, PAIR)] = inverse
-            ctx_v[:, pl.ds(at, PAIR)] = (total * inverse).astype(BF16)
-
-        def group_step(group, carry):
-            for index in range(GROUP):
-                pair_step(group * GROUP + index)
-            target = prob_out.at[step, pl.ds(group * 2 * GROUP, 2 * GROUP)]
-            pltpu.make_async_copy(p_v.at[pl.ds(group * 2 * GROUP, 2 * GROUP)], target, p_sem.at[group]).start()
-            return carry
-
-        lax.fori_loop(0, 2, group_step, 0)
-        save("linv", linv_v, step)
-        save("ctx", ctx_v, step)
-
-        @pl.when(step == 0)
-        def _():
-            w_rest[0].wait()
-
+        await_keys_or_values(0)
+        q_v, linv_v, ctx_v = buffers["q"], buffers["linv"], buffers["ctx"]
+        for group in range(2):
+            for pair in range(group * GROUP, (group + 1) * GROUP):
+                at = pair * PAIR
+                q2 = q_v[:, at : at + PAIR] * SCORE_SCALE
+                k2 = kv_v[step, :, at : at + PAIR]
+                weights = []
+                for head in range(2):
+                    scores = dot_nt(q2, k2 * half_mask(head)) + bias_v[...]
+                    weight = jnp.exp(scores - jnp.max(scores, axis=-1, keepdims=True)).astype(BF16)
+                    p_v[pair * 2 + head] = weight
+                    weights.append(weight)
+                if pair == 0:
+                    await_keys_or_values(1)
+                v2 = kv_v[step, :, D + at : D + at + PAIR]
+                total = None
+                for head in range(2):
+                    mask = half_mask(head)
+                    values = jnp.concatenate([v2 * mask, jnp.broadcast_to(mask, (SEQ, PAIR))], axis=1)
+                    part = dot_nn(weights[head], values)
+                    total = part if total is None else total + part
+                inverse = 1.0 / total[:, PAIR : 2 * PAIR]
+                linv_v[:, at : at + PAIR] = inverse
+                ctx_v[:, at : at + PAIR] = (total[:, 0:PAIR] * inverse).astype(BF16)
+            view, target, sem = prob_part(group, step)
+            pltpu.make_async_copy(view, target, sem).start()
+        save("linv", step)
+        save("ctx", step)
+        when_first(step, (get_wo,))
         resid = hidden.astype(F32) + (dot_nn(ctx_v[...], wo_v[...]) + out_biases[0, 0:1, :])
         scaled, inverse = normalize(resid)
-        xh1_v[...] = scaled.astype(BF16)
-        inv1_v[...] = jnp.broadcast_to(inverse, (ROWS, 128))
+        buffers["xh1"][...] = scaled.astype(BF16)
+        buffers["inv1"][...] = jnp.broadcast_to(inverse, (ROWS, 128))
         normed = scaled * gains[0, 0:1, :] + shifts[0, 0:1, :]
-        low_v[...] = normed.astype(BF16)
+        buffers["low"][...] = normed.astype(BF16)
         acc_v[...] = normed + out_biases[0, 1:2, :]
-        save("xh1", xh1_v, step)
-        save("inv1", inv1_v, step)
-        save("low", low_v, step)
-
-        @pl.when(step == 0)
-        def _():
-            w_rest[1].wait()
-            w_rest[2].wait()
-
+        for name in ("xh1", "inv1", "low"):
+            save(name, step)
+        when_first(step, (get_wu, get_wd))
         width = 1024
         for chunk in range(FF // width):
             cols = slice(chunk * width, (chunk + 1) * width)
-            up = dot_nn(low_v[...], wu_v[:, cols]) + up_bias[0:1, cols]
+            up = dot_nn(buffers["low"][...], wu_v[:, cols]) + up_bias[0:1, cols]
             gelu, slope = gelu_and_slope(up)
             gelu = gelu.astype(BF16)
-            gelu_v[:, cols] = gelu
-            slope_v[:, cols] = slope.astype(BF16)
+            buffers["gelu"][:, cols] = gelu
+            buffers["slope"][:, cols] = slope.astype(BF16)
             acc_v[...] += dot_nn(gelu, wd_v[cols, :])
-        save("gelu", gelu_v, step)
-        save("slope", slope_v, step)
         scaled, inverse = normalize(acc_v[...])
         act_v[step] = (scaled * gains[0, 1:2, :] + shifts[0, 1:2, :]).astype(BF16)
 
@@ -349,22 +361,187 @@
             remote(act_v.at[step], h_v.at[step], hop_sent.at[step], in_arrived.at[step], place.other_layer).start()
 
         outputs.collect(step)
-        xh2_v[...] = scaled.astype(BF16)
-        inv2_v[...] = jnp.broadcast_to(inverse, (ROWS, 128))
-        save("xh2", xh2_v, step)
-        save("inv2", inv2_v, step)
+        buffers["xh2"][...] = scaled.astype(BF16)
+        buffers["inv2"][...] = jnp.broadcast_to(inverse, (ROWS, 128))
+        for name in ("gelu", "slope", "xh2", "inv2"):
+            save(name, step)
         return carry
 
-    lax.fori_loop(0, steps, one_step, 0)
-    for name, buffer in reused:
-        free(name, buffer)
+    lax.fori_loop(0, steps, forward_step, 0)
+
+    def backward_step(turn, carry):
+        step = steps - 1 - turn
+
+        def fetched(*wanted):
+            @pl.when(turn > 0)
+            def _():
+                for name in wanted:
+                    settle(name)
+
+        def fetch_next(*wanted):
+            @pl.when(turn == 0)
+            def _():
+                for name in wanted:
+                    settle(name)
+
+            @pl.when(turn + 1 < steps)
+            def _():
+                for name in wanted:
+                    fetch(name, step - 1)
+
+        def keep(name):
+            pltpu.make_async_copy(
+                grad_buffers[name], at_step(grads[name], step), grad_sem.at[grad_names.index(name)]
+            ).start()
+
+        def free(name):
+            @pl.when(turn > 0)
+            def _():
+                buffer = grad_buffers[name]
+                pltpu.make_async_copy(buffer, buffer, grad_sem.at[grad_names.index(name)]).wait()
+
+        upstream.await_step(step, section == 1)
+        fetched("xh2", "inv2")
+        grad = g_v[step].astype(F32)
+        scaled = buffers["xh2"][...].astype(F32)
+        small_out[5:6, :] += column_sum(grad * scaled)
+        small_out[7:8, :] += column_sum(grad)
+        d_r2 = norm_back(grad, scaled, buffers["inv2"][:, 0:1], gains[0, 1:2, :])
+        d_down = d_r2.astype(BF16)
+        free("d_down")
+        d_down_v, d_up_v, d_attn_v, d_qkv_v = [grad_buffers[name] for name in grad_names]
+        d_down_v[...] = d_down
+        small_out[3:4, :] += column_sum(d_down.astype(F32))
+        acc_v[...] = d_r2
+        keep("d_down")
+        fetch_next("xh2", "inv2")
+        fetched("slope")
+        free("d_up")
+        for chunk in range(FF // D):
+            cols = slice(chunk * D, (chunk + 1) * D)
+            d_up = (dot_nt(d_down_v[...], wd_v[cols, :]) * buffers["slope"][:, cols].astype(F32)).astype(BF16)
+            d_up_v[:, cols] = d_up
+            small_out[8 + chunk : 9 + chunk, :] += column_sum(d_up.astype(F32))
+            acc_v[...] += dot_nt(d_up, wu_v[:, cols])
+        keep("d_up")
+        fetch_next("slope")
+        fetched("xh1", "inv1")
+        d_normed = acc_v[...]
+        scaled = buffers["xh1"][...].astype(F32)
+        small_out[4:5, :] += column_sum(d_normed * scaled)
+        small_out[6:7, :] += column_sum(d_normed)
+        d_r1 = norm_back(d_normed, scaled, buffers["inv1"][:, 0:1], gains[0, 0:1, :])
+        d_attn = d_r1.astype(BF16)
+        free("d_attn")
+        d_attn_v[...] = d_attn
+        small_out[2:3, :] += column_sum(d_attn.astype(F32))
+        acc_v[...] = d_r1
+        keep("d_attn")
+        fetch_next("xh1", "inv1")
+        fetched("q", "linv", "ctx")
+
+        @pl.when(turn > 0)
+        def _():
+            settle_prob()
+
+        d_ctx_v[...] = (dot_nt(d_attn_v[...], wo_v[...]) * buffers["linv"][...]).astype(BF16)
+        free("d_qkv")
+
+        def part_copy(group):
+            pairs = pl.ds(group * GROUP, GROUP)
+            return remote(
+                part_v.at[pairs, place.theirs], their_v.at[step, pairs], part_sent.at[group],
+                part_arrived.at[step, group], place.sibling,
+            )
+
+        @pl.when(turn > 0)
+        def _():
+            for group in range(2):
+                part_copy(group).wait_send()
+
+        q_v, ctx_v = buffers["q"], buffers["ctx"]
+        for group in range(2):
+            for pair in range(group * GROUP, (group + 1) * GROUP):
+                at = pair * PAIR
+                q2 = q_v[:, at : at + PAIR] * SCORE_SCALE
+                k2 = kv_v[step, :, at : at + PAIR]
+                v2 = kv_v[step, :, D + at : D + at + PAIR]
+                dc2 = d_ctx_v[:, at : at + PAIR]
+                inner = dc2.astype(F32) * ctx_v[:, at : at + PAIR].astype(F32)
+                d_q, d_k, d_v = None, None, None
+                for head in range(2):
+                    mask = half_mask(head)
+                    dc_own = dc2 * mask
+                    weight = p_v[pair * 2 + head]
+                    row_inner = jnp.sum(inner * mask.astype(F32), axis=-1, keepdims=True)
+                    d_prob = dot_nt(dc_own, v2)
+                    d_score = (weight.astype(F32) * (d_prob - row_inner)).astype(BF16)
+                    one_v = dot_tn(dc_own, weight)
+                    one_k = dot_tn(q2 * mask, d_score)
+                    one_q = dot_nn(d_score, k2 * mask)
+                    d_v = one_v if d_v is None else d_v + one_v
+                    d_k = one_k if d_k is None else d_k + one_k
+                    d_q = one_q if d_q is None else d_q + one_q
+                d_qkv_v[:, at : at + PAIR] = (d_q * SCORE_SCALE).astype(BF16)
+                part_v[pair, :, 0:PAIR] = jnp.transpose(d_k).astype(BF16)
+                part_v[pair, :, PAIR : 2 * PAIR] = jnp.transpose(d_v).astype(BF16)
+            part_copy(group).start()
+
+        fetch_next("q", "linv", "ctx")
+
+        @pl.when(turn == 0)
+        def _():
+            settle_prob()
+
+        @pl.when(turn + 1 < steps)
+        def _():
+            for group in range(2):
+                view, source, sem = prob_part(group, step - 1)
+                pltpu.make_async_copy(source, view, sem).start()
+
+        d_query = d_qkv_v[:, 0:D]
+        acc_v[...] += dot_nt(d_query, wqkv_v[:, 0:D])
+        small_out[0:1, :] += column_sum(d_query.astype(F32))
+        for group in range(2):
+            start = group * GROUP
+            part_copy(group).wait_recv()
+            for pair in range(start, start + GROUP):
+                total = part_v[pair, place.own, :].astype(F32) + their_v[step, pair].astype(F32)
+                at = pair * PAIR
+                d_qkv_v[:, D + at : D + at + PAIR] = total[:, 0:PAIR].astype(BF16)
+                d_qkv_v[:, 2 * D + at : 2 * D + at + PAIR] = total[:, PAIR : 2 * PAIR].astype(BF16)
+            keys = slice(D + start * PAIR, D + (start + GROUP) * PAIR)
+            values = slice(2 * D + start * PAIR, 2 * D + (start + GROUP) * PAIR)
+            d_hid = acc_v[...] + dot_nt(d_qkv_v[:, keys], wqkv_v[:, keys]) + dot_nt(d_qkv_v[:, values], wqkv_v[:, values])
+            if group == 0:
+                acc_v[...] = d_hid
+            else:
+                d_hid_v[step] = d_hid.astype(BF16)
+
+        @pl.when(section == 1)
+        def _():
+            remote(d_hid_v.at[step], g_v.at[step], back_sent.at[step], up_arrived.at[step], place.other_layer).start()
+
+        downstream.collect(step)
+        small_out[1:2, :] += column_sum(d_qkv_v[:, 2 * D : 3 * D].astype(F32))
+        keep("d_qkv")
+        return carry
+
+    lax.fori_loop(0, steps, backward_step, 0)
+
+    for name in ("low", "gelu"):
+        settle(name)
+    for name in grad_names:
+        buffer = grad_buffers[name]
+        pltpu.make_async_copy(buffer, buffer, grad_sem.at[grad_names.index(name)]).wait()
+    for group in range(2):
+        view = part_v.at[pl.ds(group * GROUP, GROUP), place.theirs]
+        remote(view, view, part_sent.at[group], part_arrived.at[0, group], place.sibling).wait_send()
     for step in range(steps):
-        pltpu.make_async_copy(h_v.at[step], h_v.at[step], hid_save.at[step]).wait()
-        pltpu.make_async_copy(kv_v.at[step], kv_out.at[step], kv_save.at[step]).wait()
+        pltpu.make_async_copy(h_v.at[step], h_v.at[step], hid_sem.at[step]).wait()
         for block in range(2):
             view = kv_v.at[step, place.own, pl.ds(block * D, D)]
             remote(view, view, kv_sent.at[step, block], kv_arrived.at[step, block], place.sibling).wait_send()
-    free_prob()
 
     @pl.when(section == 0)
     def _():
@@ -372,27 +549,34 @@
         for step in range(steps):
             remote(act_v.at[step], h_v.at[step], hop_sent.at[step], in_arrived.at[step], place.other_layer).wait_send()
 
+    @pl.when(section == 1)
+    def _():
+        upstream.spread_done()
+        for step in range(steps):
+            remote(d_hid_v.at[step], g_v.at[step], back_sent.at[step], up_arrived.at[step], place.other_layer).wait_send()
+
     outputs.collect_done()
-
-
-def forward(tokens, weights, segments, lengths, params):
+    downstream.collect_done()
+
+
+def layers(tokens, cotangent, weights, segments, lengths, params):
     total = tokens.shape[0]
     sequences = total // SEQ
     steps = 2 * sequences
     shapes = [
         jax.ShapeDtypeStruct((total, D), BF16),
-        jax.ShapeDtypeStruct((steps, SEQ, 2 * D), BF16),
+        jax.ShapeDtypeStruct((total, D), BF16),
+        jax.ShapeDtypeStruct((SMALL_ROWS, D), F32),
         jax.ShapeDtypeStruct((steps, H, ROWS, SEQ), BF16),
-    ] + [jax.ShapeDtypeStruct((total, width), dtype) for _, width, dtype in SAVED]
+    ] + [jax.ShapeDtypeStruct((total, width), dtype) for _, width, dtype in SAVED + GRADS]
     dma = pltpu.SemaphoreType.DMA
-    act, kv, prob, *saved = pl.pallas_call(
-        functools.partial(forward_kernel, sequences),
+    act, d_hid, small, _, *rest = pl.pallas_call(
+        functools.partial(layers_kernel, sequences),
         out_shape=shapes,
-        in_specs=[ANY] * 5 + [VMEM, SMEM] + [VMEM] * 5,
-        out_specs=[ANY] * len(shapes),
-        scratch_shapes=[
-            pltpu.VMEM((steps, ROWS, D), BF16),
-            pltpu.VMEM((steps, ROWS, D), BF16),
+        in_specs=[ANY] * 6 + [VMEM, SMEM] + [VMEM] * 5,
+        out_specs=[ANY, ANY, VMEM] + [ANY] * (len(shapes) - 3),
+        scratch_shapes=[pltpu.VMEM((steps, ROWS, D), BF16)] * 4
+        + [
             pltpu.VMEM((steps, SEQ, 2 * D), BF16),
             pltpu.VMEM((H, ROWS, SEQ), BF16),
             pltpu.VMEM((D, 3 * D), BF16),
@@ -403,305 +587,25 @@
             pltpu.VMEM((ROWS, D), F32),
             pltpu.VMEM((sequences, 8, SEQ), F32),
             pltpu.VMEM((sequences, 8, SEQ), F32),
-        ]
-        + [pltpu.VMEM((ROWS, width), dtype) for name, width, dtype in SAVED if name != "hid"]
-        + [
-            dma((6,)),
-            dma((len(SAVED),)),
-            dma((2,)),
-            dma((sequences,)),
-            dma((sequences,)),
-            dma((steps,)),
-            dma((sequences,)),
-            dma((sequences,)),
-            dma((sequences,)),
-            dma((steps, 2)),
-            dma((steps, 2)),
-            dma((steps,)),
-            dma((2,)),
-            dma((steps,)),
-            dma((steps,)),
-        ],
-        compiler_params=pltpu.CompilerParams(
-            collective_id=1, has_side_effects=True, vmem_limit_bytes=VMEM_LIMIT
-        ),
-        name="forward",
-    )(tokens, *weights, segments, lengths, *params)
-    return act, kv, prob, dict(zip([name for name, _, _ in SAVED], saved))
-
-
-KEPT = ("q", "linv", "ctx", "xh1", "inv1", "slope", "xh2", "inv2")
-
-
-def backward_kernel(sequences, *refs):
-    (cot, wqkv, wo, wu, wd, gains, kv_in, prob_in) = refs[:8]
-    ins = dict(zip(KEPT, refs[8:16]))
-    d_hid_out, small_out = refs[16:18]
-    outs = dict(zip([name for name, _, _ in GRADS], refs[18:22]))
-    (
-        g_v, d_hid_v, kv_v, p_v, wqkv_v, wo_v, wu_v, wd_v, acc_v, d_ctx_v, part_v, their_v,
-        q_v, linv_v, ctx_v, xh1_v, inv1_v, slope_v, xh2_v, inv2_v,
-        d_down_v, d_up_v, d_attn_v, d_qkv_v,
-        w_sem, load_sem, save_sem, in_local, in_sent, in_arrived, out_local, out_sent, out_arrived,
-        part_sent, part_arrived, hop_sent,
-    ) = refs[22:]
-    place = Place()
-    section = place.section
-    steps = 2 * sequences
-    grad_names = [name for name, _, _ in GRADS]
-    inputs = Rows(place, sequences, cot, g_v, in_local, in_sent, in_arrived)
-    outputs = Rows(place, sequences, d_hid_out, d_hid_v, out_local, out_sent, out_arrived)
-    buffers = dict(zip(KEPT, (q_v, linv_v, ctx_v, xh1_v, inv1_v, slope_v, xh2_v, inv2_v)))
-
-    def at_step(array, step):
-        return array.at[pl.ds(pl.multiple_of(step * ROWS, ROWS), ROWS)]
-
-    def fetch(names, step):
-        for name in names:
-            if name == "kv":
-                pltpu.make_async_copy(kv_in.at[step], kv_v, load_sem.at[len(KEPT)]).start()
-            elif name == "prob":
-                pltpu.make_async_copy(prob_in.at[step], p_v, load_sem.at[len(KEPT) + 1]).start()
-            else:
-                source = at_step(ins[name], step)
-                pltpu.make_async_copy(source, buffers[name], load_sem.at[KEPT.index(name)]).start()
-
-    def fetched(*names):
-        for name in names:
-            if name == "kv":
-                pltpu.make_async_copy(kv_v, kv_v, load_sem.at[len(KEPT)]).wait()
-            elif name == "prob":
-                pltpu.make_async_copy(p_v, p_v, load_sem.at[len(KEPT) + 1]).wait()
-            else:
-                pltpu.make_async_copy(buffers[name], buffers[name], load_sem.at[KEPT.index(name)]).wait()
-
-    def fetch_next(names, step):
-        @pl.when(step + 1 < steps)
-        def _():
-            fetch(names, step + 1)
-
-    def save(name, buffer, step):
-        pltpu.make_async_copy(buffer, at_step(outs[name], step), save_sem.at[grad_names.index(name)]).start()
-
-    def free(name, buffer):
-        pltpu.make_async_copy(buffer, buffer, save_sem.at[grad_names.index(name)]).wait()
-
-    def free_before(name, buffer, step):
-        @pl.when(step > 0)
-        def _():
-            free(name, buffer)
-
-    def when_first(step, copies):
-        @pl.when(step == 0)
-        def _():
-            for copy in copies:
-                copy.wait()
-
-    def free_parts():
-        for group in range(2):
-            view = part_v.at[pl.ds(group * GROUP, GROUP), place.theirs]
-            remote(view, view, part_sent.at[group], part_arrived.at[0, 0], place.sibling).wait_send()
-
-    place.greet()
-
-    @pl.when(section == 1)
-    def _():
-        inputs.spread()
-
-    first = jnp.int32(0)
-    fetch(("xh2", "inv2"), first)
-    get_wd = begin(wd.at[0], wd_v, w_sem.at[0])
-    fetch(("slope",), first)
-    get_wu = begin(wu.at[0], wu_v, w_sem.at[1])
-    fetch(("xh1", "inv1"), first)
-    get_wo = begin(wo.at[0], wo_v, w_sem.at[2])
-    fetch(("q", "linv", "ctx", "kv", "prob"), first)
-    get_wqkv = begin(wqkv.at[0], wqkv_v, w_sem.at[3])
-    small_out[...] = jnp.zeros_like(small_out)
-
-    def column_sum(value):
-        return jnp.sum(value, axis=0, keepdims=True)
-
-    def one_step(step, carry):
-        inputs.await_step(step, section == 1)
-        fetched("xh2", "inv2")
-        grad = g_v[step].astype(F32)
-        scaled = xh2_v[...].astype(F32)
-        small_out[5:6, :] += column_sum(grad * scaled)
-        small_out[7:8, :] += column_sum(grad)
-        d_r2 = norm_back(grad, scaled, inv2_v[:, 0:1], gains[0, 1:2, :])
-        d_down = d_r2.astype(BF16)
-        free_before("d_down", d_down_v, step)
-        d_down_v[...] = d_down
-        small_out[3:4, :] += column_sum(d_down.astype(F32))
-        acc_v[...] = d_r2
-        save("d_down", d_down_v, step)
-        fetch_next(("xh2", "inv2"), step)
-        fetched("slope")
-        when_first(step, (get_wd, get_wu))
-        free_before("d_up", d_up_v, step)
-        for chunk in range(FF // D):
-            cols = slice(chunk * D, (chunk + 1) * D)
-            d_up = (dot_nt(d_down_v[...], wd_v[cols, :]) * slope_v[:, cols].astype(F32)).astype(BF16)
-            d_up_v[:, cols] = d_up
-            small_out[8 + chunk : 9 + chunk, :] += column_sum(d_up.astype(F32))
-            acc_v[...] += dot_nt(d_up, wu_v[:, cols])
-        save("d_up", d_up_v, step)
-        fetch_next(("slope",), step)
-        fetched("xh1", "inv1")
-        d_normed = acc_v[...]
-        scaled = xh1_v[...].astype(F32)
-        small_out[4:5, :] += column_sum(d_normed * scaled)
-        small_out[6:7, :] += column_sum(d_normed)
-        d_r1 = norm_back(d_normed, scaled, inv1_v[:, 0:1], gains[0, 0:1, :])
-        d_attn = d_r1.astype(BF16)
-        free_before("d_attn", d_attn_v, step)
-        d_attn_v[...] = d_attn
-        small_out[2:3, :] += column_sum(d_attn.astype(F32))
-        acc_v[...] = d_r1
-        save("d_attn", d_attn_v, step)
-        fetch_next(("xh1", "inv1"), step)
-        when_first(step, (get_wo,))
-        fetched("q", "linv", "ctx", "kv", "prob")
-        d_ctx_v[...] = (dot_nt(d_attn_v[...], wo_v[...]) * linv_v[...]).astype(BF16)
-        free_before("d_qkv", d_qkv_v, step)
-
-        @pl.when(step > 0)
-        def _():
-            free_parts()
-
-        def pair_step(pair):
-            at = pl.multiple_of(pair * PAIR, PAIR)
-            q2 = q_v[:, pl.ds(at, PAIR)] * SCORE_SCALE
-            k2 = kv_v[:, pl.ds(at, PAIR)]
-            v2 = kv_v[:, pl.ds(at + D, PAIR)]
-            dc2 = d_ctx_v[:, pl.ds(at, PAIR)]
-            inner = dc2.astype(F32) * ctx_v[:, pl.ds(at, PAIR)].astype(F32)
-            d_q, d_k, d_v = None, None, None
-            for head in range(2):
-                mask = half_mask(head)
-                dc_own = dc2 * mask
-                weight = p_v[pair * 2 + head]
-                row_inner = jnp.sum(inner * mask.astype(F32), axis=-1, keepdims=True)
-                d_prob = dot_nt(dc_own, v2)
-                d_score = (weight.astype(F32) * (d_prob - row_inner)).astype(BF16)
-                one_v = dot_tn(dc_own, weight)
-                one_k = dot_tn(q2 * mask, d_score)
-                one_q = dot_nn(d_score, k2 * mask)
-                d_v = one_v if d_v is None else d_v + one_v
-                d_k = one_k if d_k is None else d_k + one_k
-                d_q = one_q if d_q is None else d_q + one_q
-            d_qkv_v[:, pl.ds(at, PAIR)] = (d_q * SCORE_SCALE).astype(BF16)
-            part_v[pair, :, 0:PAIR] = jnp.transpose(d_k).astype(BF16)
-            part_v[pair, :, PAIR : 2 * PAIR] = jnp.transpose(d_v).astype(BF16)
-
-        def group_step(group, carry):
-            for index in range(GROUP):
-                pair_step(group * GROUP + index)
-            pairs = pl.ds(group * GROUP, GROUP)
-            remote(
-                part_v.at[pairs, place.theirs], their_v.at[step, pairs], part_sent.at[group],
-                part_arrived.at[step, group], place.sibling,
-            ).start()
-            return carry
-
-        lax.fori_loop(0, 2, group_step, 0)
-        fetch_next(("q", "linv", "ctx", "kv", "prob"), step)
-        when_first(step, (get_wqkv,))
-        d_query = d_qkv_v[:, 0:D]
-        acc_v[...] += dot_nt(d_query, wqkv_v[:, 0:D])
-        small_out[0:1, :] += column_sum(d_query.astype(F32))
-        for group in range(2):
-            start = group * GROUP
-            view = their_v.at[step, pl.ds(start, GROUP)]
-            remote(view, view, part_sent.at[group], part_arrived.at[step, group], place.sibling).wait_recv()
-            for pair in range(start, start + GROUP):
-                total = part_v[pair, place.own, :].astype(F32) + their_v[step, pair].astype(F32)
-                at = pair * PAIR
-                d_qkv_v[:, D + at : D + at + PAIR] = total[:, 0:PAIR].astype(BF16)
-                d_qkv_v[:, 2 * D + at : 2 * D + at + PAIR] = total[:, PAIR : 2 * PAIR].astype(BF16)
-            keys = slice(D + start * PAIR, D + (start + GROUP) * PAIR)
-            values = slice(2 * D + start * PAIR, 2 * D + (start + GROUP) * PAIR)
-            d_hid = acc_v[...] + dot_nt(d_qkv_v[:, keys], wqkv_v[:, keys]) + dot_nt(d_qkv_v[:, values], wqkv_v[:, values])
-            if start == 0:
-                acc_v[...] = d_hid
-            else:
-                d_hid_v[step] = d_hid.astype(BF16)
-
-        @pl.when(section == 1)
-        def _():
-            remote(d_hid_v.at[step], g_v.at[step], hop_sent.at[step], in_arrived.at[step], place.other_layer).start()
-
-        outputs.collect(step)
-        small_out[1:2, :] += column_sum(d_qkv_v[:, 2 * D : 3 * D].astype(F32))
-        save("d_qkv", d_qkv_v, step)
-        return carry
-
-    lax.fori_loop(0, steps, one_step, 0)
-    for name, buffer in zip(grad_names, (d_down_v, d_up_v, d_attn_v, d_qkv_v)):
-        free(name, buffer)
-    free_parts()
-
-    @pl.when(section == 1)
-    def _():
-        inputs.spread_done()
-        for step in range(steps):
-            remote(d_hid_v.at[step], g_v.at[step], hop_sent.at[step], in_arrived.at[step], place.other_layer).wait_send()
-
-    outputs.collect_done()
-
-
-def backward(cotangent, weights, gains, kv, prob, saved):
-    total = cotangent.shape[0]
-    sequences = total // SEQ
-    steps = 2 * sequences
-    shapes = [
-        jax.ShapeDtypeStruct((total, D), BF16),
-        jax.ShapeDtypeStruct((SMALL_ROWS, D), F32),
-    ] + [jax.ShapeDtypeStruct((total, width), dtype) for _, width, dtype in GRADS]
-    widths = {name: (width, dtype) for name, width, dtype in SAVED}
-    dma = pltpu.SemaphoreType.DMA
-    d_hid, small, *grads = pl.pallas_call(
-        functools.partial(backward_kernel, sequences),
-        out_shape=shapes,
-        in_specs=[ANY] * 5 + [VMEM] + [ANY] * (2 + len(KEPT)),
-        out_specs=[ANY, VMEM] + [ANY] * len(GRADS),
-        scratch_shapes=[
-            pltpu.VMEM((steps, ROWS, D), BF16),
-            pltpu.VMEM((steps, ROWS, D), BF16),
-            pltpu.VMEM((SEQ, 2 * D), BF16),
-            pltpu.VMEM((H, ROWS, SEQ), BF16),
-            pltpu.VMEM((D, 3 * D), BF16),
-            pltpu.VMEM((D, D), BF16),
-            pltpu.VMEM((D, FF), BF16),
-            pltpu.VMEM((FF, D), BF16),
-            pltpu.VMEM((ROWS, D), F32),
             pltpu.VMEM((ROWS, D), BF16),
             pltpu.VMEM((PAIRS, SEQ, 2 * PAIR), BF16),
             pltpu.VMEM((steps, PAIRS, ROWS, 2 * PAIR), BF16),
         ]
-        + [pltpu.VMEM((ROWS, widths[name][0]), widths[name][1]) for name in KEPT]
-        + [pltpu.VMEM((ROWS, width), dtype) for _, width, dtype in GRADS]
+        + [pltpu.VMEM((ROWS, width), dtype) for name, width, dtype in SAVED + GRADS if name != "hid"]
         + [
-            dma((4,)),
-            dma((len(KEPT) + 2,)),
-            dma((len(GRADS),)),
-            dma((sequences,)),
-            dma((sequences,)),
-            dma((steps,)),
-            dma((sequences,)),
-            dma((sequences,)),
-            dma((sequences,)),
-            dma((2,)),
-            dma((steps, 2)),
-            dma((steps,)),
-        ],
+            dma((6,)), dma((len(SAVED),)), dma((steps,)), dma((len(GRADS),)), dma((2,)), dma((2,)),
+            dma((steps, 2)), dma((steps, 2)), dma((2,)), dma((steps, 2)),
+        ]
+        + [dma((sequences,)), dma((sequences,)), dma((steps,))]
+        + [dma((sequences,)), dma((sequences,)), dma((sequences,)), dma((steps,))]
+        + [dma((sequences,)), dma((sequences,)), dma((steps,))]
+        + [dma((sequences,)), dma((sequences,)), dma((sequences,)), dma((steps,))],
         compiler_params=pltpu.CompilerParams(
-            collective_id=2, has_side_effects=True, vmem_limit_bytes=VMEM_LIMIT
+            collective_id=1, has_side_effects=True, vmem_limit_bytes=VMEM_LIMIT
         ),
-        name="backward",
-    )(cotangent, *weights, gains, kv, prob, *[saved[name] for name in KEPT])
-    return d_hid, small, dict(zip([name for name, _, _ in GRADS], grads))
+        name="layers",
+    )(tokens, cotangent, *weights, segments, lengths, *params)
+    return act, d_hid, small, dict(zip([name for name, _, _ in SAVED + GRADS], rest))
 
 
 UNIT = 16
@@ -1186,11 +1090,10 @@
 ):
     weights = (qkv_weight, out_weight, up_weight, down_weight)
     params = (qv_bias, out_biases, norm_gains, norm_shifts, up_bias)
-    act, kv, prob, saved = forward(tokens, weights, segments, lengths, params)
-    d_hid, small, grads = backward(cotangent, weights, norm_gains, kv, prob, saved)
+    act, d_hid, small, kept = layers(tokens, cotangent, weights, segments, lengths, params)
     totals, small = reduce_gradients(
-        lax.axis_size("dp") // 4, saved["gelu"], grads["d_down"], saved["low"], grads["d_up"],
-        saved["ctx"], grads["d_attn"], saved["hid"], grads["d_qkv"], small,
+        lax.axis_size("dp") // 4, kept["gelu"], kept["d_down"], kept["low"], kept["d_up"],
+        kept["ctx"], kept["d_attn"], kept["hid"], kept["d_qkv"], small,
     )
     (
         o_act, o_hid, g_down, g_up, g_out, g_qkv, g_qv, g_bias, g_gain, g_shift, g_up_bias

time: 301 us -> 290 us (0.963)
  Pallas kernels: 299 us -> 288 us
    pallas_call x2 -> x1, Pallas kernels: 143 us -> 133 us  [layers(): pl.pallas_call(functools.partial(layers_kernel, sequences), out_shape=sha...]
where the time goes in v5:
time: 290 us
  Pallas kernels  288 us (99%)
    pallas_call x1, Pallas kernels, reduce_gradients(): pl.pallas_call(functools.partial(reduce_kernel, depth), out_shape=[pltpu....  145 us
    pallas_call x1, Pallas kernels, layers(): pl.pallas_call(functools.partial(layers_kernel, sequences), out_shape=sha...  133 us
    pallas_call x1, Pallas kernels, finish(): pl.pallas_call(finish_kernel, out_shape=shapes, in_specs=[VMEM, VMEM, ANY...  11 us

profile of v5, /device:TPU:0, one launch (start us, length us, event | category | flops | bytes accessed | tf_op | source)
XLA Modules:
  0.0 290.1 jit_solution(14257392196336515342)
XLA Ops:
  0.6 132.5 %layers.1 = (bf16[1024,768]{1,0:T(8,128)(2,1)}, bf16[1024,768]{1,0:T(8,128)(2,1)}, f32[16,768]{1,0:T(8,128)}, bf16[4,12,256,512]{3,2,1,0:T(8,128)(2,1)}, bf16[10...) custom-call(bf16[1024,768]{1,0:T(8,128)(2,1)} %refs_0_.1, ...), custom_call_target="tpu_custom_call" | custom-call | tf_op jit(solution)/shard_map/layers/pallas_call | solution.py:573
  133.2 0.0 copy-start
  133.2 0.0 copy-start.1
  133.2 144.9 %reduce_gradients.1 = (bf16[24,768,384]{2,1,0:T(8,128)(2,1)S(1)}, f32[16,768]{1,0:T(8,128)}) custom-call(bf16[1024,3072]{1,0:T(8,128)(2,1)} %get-tuple-element.35.refs_0_, bf16[1024,768]{1,0:T(8,128)(2,1)} %get-tuple-element.36.refs_1_, bf16[1024,768]{1,0:T(8,128)(2,1)} %get-tuple-element.37.refs_2_, bf16[1024,3072]{1,0:T(8,128)(2,1)} %get-tuple-element.38.refs_3_, ...), custom_call_target="tpu_custom_call" | custom-call | tf_op jit(solution)/shard_map/reduce_gradients/pallas_call | solution.py:997
  278.1 0.0 copy-done
  278.1 0.0 copy-done.1
  278.1 0.0 copy-start.2
  278.1 0.8 copy-done.2
  278.9 11.0 %finish.1 = (bf16[1,1024,768]{2,1,0:T(8,128)(2,1)}, bf16[1,1024,768]{2,1,0:T(8,128)(2,1)}, f32[1,3072,768]{2,1,0:T(8,128)}, f32[1,768,3072]{2,1,0:T(8,128)}, f32...) custom-call(bf16[24,768,384]{2,1,0:T(8,128)(2,1)S(1)} %get-tuple-ele, ...), custom_call_target="tpu_custom_call" | custom-call | tf_op jit(solution)/shard_map/finish/pallas_call | solution.py:1072
Async XLA Ops:
  133.2 144.9 %copy-start = (bf16[1024,768]{1,0:T(8,128)(2,1)S(1)}, bf16[1024,768]{1,0:T(8,128)(2,1)}, u32[]{:S(2)}) copy-start(bf16[1024,768]{1,0:T(8,128)(2,1)} %get-tuple-element.46.refs_2_) | copy-start | bytes 4718596
  133.2 144.9 %copy-start.1 = (bf16[1024,768]{1,0:T(8,128)(2,1)S(1)}, bf16[1024,768]{1,0:T(8,128)(2,1)}, u32[]{:S(2)}) copy-start(bf16[1024,768]{1,0:T(8,128)(2,1)} %get-tuple-element.47.refs_3_) | copy-start | bytes 4718596
  278.1 0.8 copy-start.2

commit v6 on v5

--- a/solution.py
+++ b/solution.py
@@ -280,17 +280,16 @@
             view = kv_v.at[step, place.theirs, pl.ds(block * D, D)]
             remote(view, view, kv_sent.at[step, block], kv_arrived.at[step, block], place.sibling).wait_recv()
 
-        when_first(step, (get_qkv[2],))
+        @pl.when(step == 0)
+        def _():
+            get_qkv[2].wait()
+            seg_copy.wait()
 
         @pl.when(step > 0)
         def _():
-            for name in buffers:
-                settle(name)
-            settle_prob()
+            settle("q")
 
         buffers["q"][...] = (dot_nn(hidden, wqkv_v[:, 0:D]) + qv_bias[0, 0:1, :]).astype(BF16)
-        save("q", step)
-        when_first(step, (seg_copy,))
 
         sequence = lax.rem(step, sequences)
         mine = jnp.where(place.is_mine(step, sequences), 1.0, 0.0)
@@ -303,6 +302,13 @@
             cols = slice(tile * 128, (tile + 1) * 128)
             visible = (key_rows[1:2, cols] > 0.5) | (key + tile * 128 == query)
             bias_v[:, cols] = jnp.where((query_seg == key_rows[0:1, cols]) & visible, 0.0, NEG_FILL)
+
+        @pl.when(step > 0)
+        def _():
+            for name in buffers:
+                if name != "q":
+                    settle(name)
+            settle_prob()
 
         await_keys_or_values(0)
         q_v, linv_v, ctx_v = buffers["q"], buffers["linv"], buffers["ctx"]
@@ -319,6 +325,7 @@
                     weights.append(weight)
                 if pair == 0:
                     await_keys_or_values(1)
+                    when_first(step, (get_wo, get_wu, get_wd))
                 v2 = kv_v[step, :, D + at : D + at + PAIR]
                 total = None
                 for head in range(2):
@@ -331,9 +338,6 @@
                 ctx_v[:, at : at + PAIR] = (total[:, 0:PAIR] * inverse).astype(BF16)
             view, target, sem = prob_part(group, step)
             pltpu.make_async_copy(view, target, sem).start()
-        save("linv", step)
-        save("ctx", step)
-        when_first(step, (get_wo,))
         resid = hidden.astype(F32) + (dot_nn(ctx_v[...], wo_v[...]) + out_biases[0, 0:1, :])
         scaled, inverse = normalize(resid)
         buffers["xh1"][...] = scaled.astype(BF16)
@@ -341,29 +345,29 @@
         normed = scaled * gains[0, 0:1, :] + shifts[0, 0:1, :]
         buffers["low"][...] = normed.astype(BF16)
         acc_v[...] = normed + out_biases[0, 1:2, :]
-        for name in ("xh1", "inv1", "low"):
-            save(name, step)
-        when_first(step, (get_wu, get_wd))
         width = 1024
-        for chunk in range(FF // width):
-            cols = slice(chunk * width, (chunk + 1) * width)
-            up = dot_nn(buffers["low"][...], wu_v[:, cols]) + up_bias[0:1, cols]
-            gelu, slope = gelu_and_slope(up)
-            gelu = gelu.astype(BF16)
-            buffers["gelu"][:, cols] = gelu
-            buffers["slope"][:, cols] = slope.astype(BF16)
-            acc_v[...] += dot_nn(gelu, wd_v[cols, :])
-        scaled, inverse = normalize(acc_v[...])
-        act_v[step] = (scaled * gains[0, 1:2, :] + shifts[0, 1:2, :]).astype(BF16)
-
-        @pl.when(section == 0)
-        def _():
-            remote(act_v.at[step], h_v.at[step], hop_sent.at[step], in_arrived.at[step], place.other_layer).start()
+        for half in range(2):
+            rows = slice(half * ROWS // 2, (half + 1) * ROWS // 2)
+            for chunk in range(FF // width):
+                cols = slice(chunk * width, (chunk + 1) * width)
+                up = dot_nn(buffers["low"][rows, :], wu_v[:, cols]) + up_bias[0:1, cols]
+                gelu, slope = gelu_and_slope(up)
+                gelu = gelu.astype(BF16)
+                buffers["gelu"][rows, cols] = gelu
+                buffers["slope"][rows, cols] = slope.astype(BF16)
+                acc_v[rows, :] += dot_nn(gelu, wd_v[cols, :])
+            scaled, inverse = normalize(acc_v[rows, :])
+            act_v[step, rows, :] = (scaled * gains[0, 1:2, :] + shifts[0, 1:2, :]).astype(BF16)
+            buffers["xh2"][rows, :] = scaled.astype(BF16)
+            buffers["inv2"][rows, :] = jnp.broadcast_to(inverse, (ROWS // 2, 128))
+
+            @pl.when(section == 0)
+            def _():
+                source, target = [array.at[step, pl.ds(half * (ROWS // 2), ROWS // 2)] for array in (act_v, h_v)]
+                remote(source, target, hop_sent.at[step], in_arrived.at[step], place.other_layer).start()
 
         outputs.collect(step)
-        buffers["xh2"][...] = scaled.astype(BF16)
-        buffers["inv2"][...] = jnp.broadcast_to(inverse, (ROWS, 128))
-        for name in ("gelu", "slope", "xh2", "inv2"):
+        for name in buffers:
             save(name, step)
         return carry
 
@@ -372,22 +376,15 @@
     def backward_step(turn, carry):
         step = steps - 1 - turn
 
-        def fetched(*wanted):
-            @pl.when(turn > 0)
-            def _():
-                for name in wanted:
-                    settle(name)
-
-        def fetch_next(*wanted):
-            @pl.when(turn == 0)
-            def _():
-                for name in wanted:
-                    settle(name)
-
-            @pl.when(turn + 1 < steps)
-            def _():
-                for name in wanted:
-                    fetch(name, step - 1)
+        early = ("xh2", "inv2", "slope", "xh1", "inv1")
+        late = ("q", "linv", "ctx")
+
+        def part_copy(group):
+            pairs = pl.ds(group * GROUP, GROUP)
+            return remote(
+                part_v.at[pairs, place.theirs], their_v.at[step, pairs], part_sent.at[group],
+                part_arrived.at[step, group], place.sibling,
+            )
 
         def keep(name):
             pltpu.make_async_copy(
@@ -395,70 +392,66 @@
             ).start()
 
         def free(name):
-            @pl.when(turn > 0)
-            def _():
-                buffer = grad_buffers[name]
-                pltpu.make_async_copy(buffer, buffer, grad_sem.at[grad_names.index(name)]).wait()
+            buffer = grad_buffers[name]
+            pltpu.make_async_copy(buffer, buffer, grad_sem.at[grad_names.index(name)]).wait()
 
         upstream.await_step(step, section == 1)
-        fetched("xh2", "inv2")
+
+        @pl.when(turn > 0)
+        def _():
+            for name in early:
+                settle(name)
+            for name in ("d_down", "d_up", "d_attn"):
+                free(name)
+
         grad = g_v[step].astype(F32)
         scaled = buffers["xh2"][...].astype(F32)
         small_out[5:6, :] += column_sum(grad * scaled)
         small_out[7:8, :] += column_sum(grad)
         d_r2 = norm_back(grad, scaled, buffers["inv2"][:, 0:1], gains[0, 1:2, :])
         d_down = d_r2.astype(BF16)
-        free("d_down")
         d_down_v, d_up_v, d_attn_v, d_qkv_v = [grad_buffers[name] for name in grad_names]
         d_down_v[...] = d_down
         small_out[3:4, :] += column_sum(d_down.astype(F32))
         acc_v[...] = d_r2
-        keep("d_down")
-        fetch_next("xh2", "inv2")
-        fetched("slope")
-        free("d_up")
         for chunk in range(FF // D):
             cols = slice(chunk * D, (chunk + 1) * D)
             d_up = (dot_nt(d_down_v[...], wd_v[cols, :]) * buffers["slope"][:, cols].astype(F32)).astype(BF16)
             d_up_v[:, cols] = d_up
             small_out[8 + chunk : 9 + chunk, :] += column_sum(d_up.astype(F32))
             acc_v[...] += dot_nt(d_up, wu_v[:, cols])
-        keep("d_up")
-        fetch_next("slope")
-        fetched("xh1", "inv1")
         d_normed = acc_v[...]
         scaled = buffers["xh1"][...].astype(F32)
         small_out[4:5, :] += column_sum(d_normed * scaled)
         small_out[6:7, :] += column_sum(d_normed)
         d_r1 = norm_back(d_normed, scaled, buffers["inv1"][:, 0:1], gains[0, 0:1, :])
         d_attn = d_r1.astype(BF16)
-        free("d_attn")
         d_attn_v[...] = d_attn
         small_out[2:3, :] += column_sum(d_attn.astype(F32))
         acc_v[...] = d_r1
-        keep("d_attn")
-        fetch_next("xh1", "inv1")
-        fetched("q", "linv", "ctx")
+
+        @pl.when(turn == 0)
+        def _():
+            for name in early:
+                settle(name)
 
         @pl.when(turn > 0)
         def _():
+            for name in late:
+                settle(name)
             settle_prob()
-
-        d_ctx_v[...] = (dot_nt(d_attn_v[...], wo_v[...]) * buffers["linv"][...]).astype(BF16)
-        free("d_qkv")
-
-        def part_copy(group):
-            pairs = pl.ds(group * GROUP, GROUP)
-            return remote(
-                part_v.at[pairs, place.theirs], their_v.at[step, pairs], part_sent.at[group],
-                part_arrived.at[step, group], place.sibling,
-            )
-
-        @pl.when(turn > 0)
-        def _():
+            free("d_qkv")
             for group in range(2):
                 part_copy(group).wait_send()
 
+        @pl.when(turn + 1 < steps)
+        def _():
+            for name in early:
+                fetch(name, step - 1)
+
+        for name in ("d_down", "d_up", "d_attn"):
+            keep(name)
+        d_ctx_v[...] = (dot_nt(d_attn_v[...], wo_v[...]) * buffers["linv"][...]).astype(BF16)
         q_v, ctx_v = buffers["q"], buffers["ctx"]
         for group in range(2):
             for pair in range(group * GROUP, (group + 1) * GROUP):
@@ -487,14 +480,16 @@
                 part_v[pair, :, PAIR : 2 * PAIR] = jnp.transpose(d_v).astype(BF16)
             part_copy(group).start()
 
-        fetch_next("q", "linv", "ctx")
-
         @pl.when(turn == 0)
         def _():
+            for name in late:
+                settle(name)
             settle_prob()
 
         @pl.when(turn + 1 < steps)
         def _():
+            for name in late:
+                fetch(name, step - 1)
             for group in range(2):
                 view, source, sem = prob_part(group, step - 1)
                 pltpu.make_async_copy(source, view, sem).start()
@@ -998,7 +993,7 @@
         functools.partial(reduce_kernel, depth),
         out_shape=[
             pltpu.VMEM((count, SLAB, columns), BF16),
-            jax.ShapeDtypeStruct((SMALL_ROWS, small.shape[-1]), F32),
+            pltpu.VMEM((SMALL_ROWS, small.shape[-1]), F32),
         ],
         in_specs=[ANY] * 8 + [VMEM],
         out_specs=[VMEM] * 2,
@@ -1081,7 +1076,7 @@
         ],
         compiler_params=pltpu.CompilerParams(vmem_limit_bytes=16 << 20),
         name="finish",
-    )(pltpu.with_memory_space_constraint(totals, pltpu.VMEM), small, act, d_hid)
+    )(*[pltpu.with_memory_space_constraint(array, pltpu.VMEM) for array in (totals, small)], act, d_hid)
 
 
 def shards(

time: 290 us -> 284 us (0.979)
  Pallas kernels: 288 us -> 283 us
    pallas_call x1, Pallas kernels: 133 us -> 127 us  [layers(): pl.pallas_call(functools.partial(layers_kernel, sequences), out_shape=sha...]
where the time goes in v6:
time: 284 us
  Pallas kernels  283 us (100%)
    pallas_call x1, Pallas kernels, reduce_gradients(): pl.pallas_call(functools.partial(reduce_kernel, depth), out_shape=[pltpu....  144 us
    pallas_call x1, Pallas kernels, layers(): pl.pallas_call(functools.partial(layers_kernel, sequences), out_shape=sha...  127 us
    pallas_call x1, Pallas kernels, finish(): pl.pallas_call(finish_kernel, out_shape=shapes, in_specs=[VMEM, VMEM, ANY...  11 us

profile of v6, /device:TPU:0, one launch (start us, length us, event | category | flops | bytes accessed | tf_op | source)
XLA Modules:
  0.0 283.6 jit_solution(17964787497303782507)
XLA Ops:
  0.6 127.4 %layers.1 = (bf16[1024,768]{1,0:T(8,128)(2,1)}, bf16[1024,768]{1,0:T(8,128)(2,1)}, f32[16,768]{1,0:T(8,128)}, bf16[4,12,256,512]{3,2,1,0:T(8,128)(2,1)}, bf16[10...) custom-call(bf16[1024,768]{1,0:T(8,128)(2,1)} %refs_0_.1, ...), custom_call_target="tpu_custom_call" | custom-call | tf_op jit(solution)/shard_map/layers/pallas_call | solution.py:568
  128.0 0.0 copy-start
  128.0 0.0 copy-start.1
  128.0 144.4 %reduce_gradients.1 = (bf16[24,768,384]{2,1,0:T(8,128)(2,1)S(1)}, f32[16,768]{1,0:T(8,128)S(1)}) custom-call(bf16[1024,3072]{1,0:T(8,128)(2,1)} %get-tuple-element.35.refs_0_, bf16[1024,768]{1,0:T(8,128)(2,1)} %get-tuple-element.36.refs_1_, bf16[1024,768]{1,0:T(8,128)(2,1)} %get-tuple-element.37.refs_2_, bf16[1024,3072]{1,0:T(8,128)(2,1)} %get-tuple-element.38.refs_3_, ...), custom_call_target="tpu_custom_call" | custom-call | tf_op jit(solution)/shard_map/reduce_gradients/pallas_call | solution.py:992
  272.4 0.0 copy-done
  272.4 0.0 copy-done.1
  272.4 11.0 %finish.1 = (bf16[1,1024,768]{2,1,0:T(8,128)(2,1)}, bf16[1,1024,768]{2,1,0:T(8,128)(2,1)}, f32[1,3072,768]{2,1,0:T(8,128)}, f32[1,768,3072]{2,1,0:T(8,128)}, f32...) custom-call(bf16[24,768,384]{2,1,0:T(8,128)(2,1)S(1)} %get-tuple-ele, ...), custom_call_target="tpu_custom_call" | custom-call | tf_op jit(solution)/shard_map/finish/pallas_call | solution.py:1067
Async XLA Ops:
  128.0 144.4 %copy-start = (bf16[1024,768]{1,0:T(8,128)(2,1)S(1)}, bf16[1024,768]{1,0:T(8,128)(2,1)}, u32[]{:S(2)}) copy-start(bf16[1024,768]{1,0:T(8,128)(2,1)} %get-tuple-element.46.refs_2_) | copy-start | bytes 4718596
  128.0 144.4 %copy-start.1 = (bf16[1024,768]{1,0:T(8,128)(2,1)S(1)}, bf16[1024,768]{1,0:T(8,128)(2,1)}, u32[]{:S(2)}) copy-start(bf16[1024,768]{1,0:T(8,128)(2,1)} %get-tuple-element.47.refs_3_) | copy-start | bytes 4718596

commit v7 on v6

--- a/solution.py
+++ b/solution.py
@@ -17,6 +17,7 @@
 PAIRS = H // 2
 PAIR = 2 * HD
 GROUP = PAIRS // 2
+BACK_GROUPS = ((0, 4), (4, 6))
 
 EPSILON = 1e-05
 SCORE_SCALE = 0.125
@@ -345,6 +346,8 @@
         normed = scaled * gains[0, 0:1, :] + shifts[0, 0:1, :]
         buffers["low"][...] = normed.astype(BF16)
         acc_v[...] = normed + out_biases[0, 1:2, :]
+        for name in ("q", "linv", "ctx", "xh1", "inv1", "low"):
+            save(name, step)
         width = 1024
         for half in range(2):
             rows = slice(half * ROWS // 2, (half + 1) * ROWS // 2)
@@ -367,7 +370,7 @@
                 remote(source, target, hop_sent.at[step], in_arrived.at[step], place.other_layer).start()
 
         outputs.collect(step)
-        for name in buffers:
+        for name in ("gelu", "slope", "xh2", "inv2"):
             save(name, step)
         return carry
 
@@ -380,7 +383,8 @@
         late = ("q", "linv", "ctx")
 
         def part_copy(group):
-            pairs = pl.ds(group * GROUP, GROUP)
+            first, last = BACK_GROUPS[group]
+            pairs = pl.ds(first, last - first)
             return remote(
                 part_v.at[pairs, place.theirs], their_v.at[step, pairs], part_sent.at[group],
                 part_arrived.at[step, group], place.sibling,
@@ -441,7 +445,7 @@
                 settle(name)
             settle_prob()
             free("d_qkv")
-            for group in range(2):
+            for group in range(len(BACK_GROUPS)):
                 part_copy(group).wait_send()
 
         @pl.when(turn + 1 < steps)
@@ -453,8 +457,8 @@
             keep(name)
         d_ctx_v[...] = (dot_nt(d_attn_v[...], wo_v[...]) * buffers["linv"][...]).astype(BF16)
         q_v, ctx_v = buffers["q"], buffers["ctx"]
-        for group in range(2):
-            for pair in range(group * GROUP, (group + 1) * GROUP):
+        for group, (first, last) in enumerate(BACK_GROUPS):
+            for pair in range(first, last):
                 at = pair * PAIR
                 q2 = q_v[:, at : at + PAIR] * SCORE_SCALE
                 k2 = kv_v[step, :, at : at + PAIR]
@@ -497,18 +501,17 @@
         d_query = d_qkv_v[:, 0:D]
         acc_v[...] += dot_nt(d_query, wqkv_v[:, 0:D])
         small_out[0:1, :] += column_sum(d_query.astype(F32))
-        for group in range(2):
-            start = group * GROUP
+        for group, (first, last) in enumerate(BACK_GROUPS):
             part_copy(group).wait_recv()
-            for pair in range(start, start + GROUP):
+            for pair in range(first, last):
                 total = part_v[pair, place.own, :].astype(F32) + their_v[step, pair].astype(F32)
                 at = pair * PAIR
                 d_qkv_v[:, D + at : D + at + PAIR] = total[:, 0:PAIR].astype(BF16)
                 d_qkv_v[:, 2 * D + at : 2 * D + at + PAIR] = total[:, PAIR : 2 * PAIR].astype(BF16)
-            keys = slice(D + start * PAIR, D + (start + GROUP) * PAIR)
-            values = slice(2 * D + start * PAIR, 2 * D + (start + GROUP) * PAIR)
+            keys = slice(D + first * PAIR, D + last * PAIR)
+            values = slice(2 * D + first * PAIR, 2 * D + last * PAIR)
             d_hid = acc_v[...] + dot_nt(d_qkv_v[:, keys], wqkv_v[:, keys]) + dot_nt(d_qkv_v[:, values], wqkv_v[:, values])
-            if group == 0:
+            if last < PAIRS:
                 acc_v[...] = d_hid
             else:
                 d_hid_v[step] = d_hid.astype(BF16)
@@ -529,8 +532,8 @@
     for name in grad_names:
         buffer = grad_buffers[name]
         pltpu.make_async_copy(buffer, buffer, grad_sem.at[grad_names.index(name)]).wait()
-    for group in range(2):
-        view = part_v.at[pl.ds(group * GROUP, GROUP), place.theirs]
+    for group, (first, last) in enumerate(BACK_GROUPS):
+        view = part_v.at[pl.ds(first, last - first), place.theirs]
         remote(view, view, part_sent.at[group], part_arrived.at[0, group], place.sibling).wait_send()
     for step in range(steps):
         pltpu.make_async_copy(h_v.at[step], h_v.at[step], hid_sem.at[step]).wait()
@@ -589,7 +592,7 @@
         + [pltpu.VMEM((ROWS, width), dtype) for name, width, dtype in SAVED + GRADS if name != "hid"]
         + [
             dma((6,)), dma((len(SAVED),)), dma((steps,)), dma((len(GRADS),)), dma((2,)), dma((2,)),
-            dma((steps, 2)), dma((steps, 2)), dma((2,)), dma((steps, 2)),
+            dma((steps, 2)), dma((steps, 2)), dma((len(BACK_GROUPS),)), dma((steps, len(BACK_GROUPS))),
         ]
         + [dma((sequences,)), dma((sequences,)), dma((steps,))]
         + [dma((sequences,)), dma((sequences,)), dma((sequences,)), dma((steps,))]
@@ -907,7 +910,6 @@
 
     load(jnp.int32(0), True)
     neighbours = 2 + (z > 0).astype(jnp.int32) + (z < depth - 1).astype(jnp.int32)
-    pl.semaphore_wait(barrier, neighbours)
 
     last = max(
         [2 + half_depth + half_depth + 2] + [2 + tree.reach + max(tree.root, depth - 1 - tree.root) + 1 for tree in line]
@@ -926,6 +928,10 @@
 
             def form():
                 p_v[slot] = dot_tn(left_v[slot], right_v[slot]).astype(BF16)
+
+                @pl.when(now == 0)
+                def _():
+                    pl.semaphore_wait(barrier, neighbours)
 
             view = p_v.at[slot, at(theirs, HALF)]
             send(CX, now, view, s_v.at[now], recv_sem.at[CX, now], sibling, form)

time: 284 us -> 279 us (0.982)
  Pallas kernels: 283 us -> 278 us
    pallas_call x1, Pallas kernels: 127 us -> 123 us  [layers(): pl.pallas_call(functools.partial(layers_kernel, sequences), out_shape=sha...]
where the time goes in v7:
time: 279 us
  Pallas kernels  278 us (100%)
    pallas_call x1, Pallas kernels, reduce_gradients(): pl.pallas_call(functools.partial(reduce_kernel, depth), out_shape=[pltpu....  144 us
    pallas_call x1, Pallas kernels, layers(): pl.pallas_call(functools.partial(layers_kernel, sequences), out_shape=sha...  123 us
    pallas_call x1, Pallas kernels, finish(): pl.pallas_call(finish_kernel, out_shape=shapes, in_specs=[VMEM, VMEM, ANY...  11 us

profile of v7, /device:TPU:0, one launch (start us, length us, event | category | flops | bytes accessed | tf_op | source)
XLA Modules:
  0.0 279.1 jit_solution(12652178350026309176)
XLA Ops:
  0.6 122.9 %layers.1 = (bf16[1024,768]{1,0:T(8,128)(2,1)}, bf16[1024,768]{1,0:T(8,128)(2,1)}, f32[16,768]{1,0:T(8,128)}, bf16[4,12,256,512]{3,2,1,0:T(8,128)(2,1)}, bf16[10...) custom-call(bf16[1024,768]{1,0:T(8,128)(2,1)} %refs_0_.1, ...), custom_call_target="tpu_custom_call" | custom-call | tf_op jit(solution)/shard_map/layers/pallas_call | solution.py:571
  123.5 0.0 copy-start
  123.5 0.0 copy-start.1
  123.5 144.4 %reduce_gradients.1 = (bf16[24,768,384]{2,1,0:T(8,128)(2,1)S(1)}, f32[16,768]{1,0:T(8,128)S(1)}) custom-call(bf16[1024,3072]{1,0:T(8,128)(2,1)} %get-tuple-element.35.refs_0_, bf16[1024,768]{1,0:T(8,128)(2,1)} %get-tuple-element.36.refs_1_, bf16[1024,768]{1,0:T(8,128)(2,1)} %get-tuple-element.37.refs_2_, bf16[1024,3072]{1,0:T(8,128)(2,1)} %get-tuple-element.38.refs_3_, ...), custom_call_target="tpu_custom_call" | custom-call | tf_op jit(solution)/shard_map/reduce_gradients/pallas_call | solution.py:998
  267.9 0.0 copy-done
  267.9 0.0 copy-done.1
  267.9 11.0 %finish.1 = (bf16[1,1024,768]{2,1,0:T(8,128)(2,1)}, bf16[1,1024,768]{2,1,0:T(8,128)(2,1)}, f32[1,3072,768]{2,1,0:T(8,128)}, f32[1,768,3072]{2,1,0:T(8,128)}, f32...) custom-call(bf16[24,768,384]{2,1,0:T(8,128)(2,1)S(1)} %get-tuple-ele, ...), custom_call_target="tpu_custom_call" | custom-call | tf_op jit(solution)/shard_map/finish/pallas_call | solution.py:1073
Async XLA Ops:
  123.5 144.4 %copy-start = (bf16[1024,768]{1,0:T(8,128)(2,1)S(1)}, bf16[1024,768]{1,0:T(8,128)(2,1)}, u32[]{:S(2)}) copy-start(bf16[1024,768]{1,0:T(8,128)(2,1)} %get-tuple-element.46.refs_2_) | copy-start | bytes 4718596
  123.5 144.4 %copy-start.1 = (bf16[1024,768]{1,0:T(8,128)(2,1)S(1)}, bf16[1024,768]{1,0:T(8,128)(2,1)}, u32[]{:S(2)}) copy-start(bf16[1024,768]{1,0:T(8,128)(2,1)} %get-tuple-element.47.refs_3_) | copy-start | bytes 4718596

commit v8 on v7

--- a/solution.py
+++ b/solution.py
@@ -313,30 +313,30 @@
 
         await_keys_or_values(0)
         q_v, linv_v, ctx_v = buffers["q"], buffers["linv"], buffers["ctx"]
+        for pair in range(PAIRS):
+            at = pair * PAIR
+            q2 = q_v[:, at : at + PAIR] * SCORE_SCALE
+            k2 = kv_v[step, :, at : at + PAIR]
+            weights = []
+            for head in range(2):
+                scores = dot_nt(q2, k2 * half_mask(head)) + bias_v[...]
+                weight = jnp.exp(scores - jnp.max(scores, axis=-1, keepdims=True)).astype(BF16)
+                p_v[pair * 2 + head] = weight
+                weights.append(weight)
+            if pair == 0:
+                await_keys_or_values(1)
+                when_first(step, (get_wo, get_wu, get_wd))
+            v2 = kv_v[step, :, D + at : D + at + PAIR]
+            total = None
+            for head in range(2):
+                mask = half_mask(head)
+                values = jnp.concatenate([v2 * mask, jnp.broadcast_to(mask, (SEQ, PAIR))], axis=1)
+                part = dot_nn(weights[head], values)
+                total = part if total is None else total + part
+            inverse = 1.0 / total[:, PAIR : 2 * PAIR]
+            linv_v[:, at : at + PAIR] = inverse
+            ctx_v[:, at : at + PAIR] = (total[:, 0:PAIR] * inverse).astype(BF16)
         for group in range(2):
-            for pair in range(group * GROUP, (group + 1) * GROUP):
-                at = pair * PAIR
-                q2 = q_v[:, at : at + PAIR] * SCORE_SCALE
-                k2 = kv_v[step, :, at : at + PAIR]
-                weights = []
-                for head in range(2):
-                    scores = dot_nt(q2, k2 * half_mask(head)) + bias_v[...]
-                    weight = jnp.exp(scores - jnp.max(scores, axis=-1, keepdims=True)).astype(BF16)
-                    p_v[pair * 2 + head] = weight
-                    weights.append(weight)
-                if pair == 0:
-                    await_keys_or_values(1)
-                    when_first(step, (get_wo, get_wu, get_wd))
-                v2 = kv_v[step, :, D + at : D + at + PAIR]
-                total = None
-                for head in range(2):
-                    mask = half_mask(head)
-                    values = jnp.concatenate([v2 * mask, jnp.broadcast_to(mask, (SEQ, PAIR))], axis=1)
-                    part = dot_nn(weights[head], values)
-                    total = part if total is None else total + part
-                inverse = 1.0 / total[:, PAIR : 2 * PAIR]
-                linv_v[:, at : at + PAIR] = inverse
-                ctx_v[:, at : at + PAIR] = (total[:, 0:PAIR] * inverse).astype(BF16)
             view, target, sem = prob_part(group, step)
             pltpu.make_async_copy(view, target, sem).start()
         resid = hidden.astype(F32) + (dot_nn(ctx_v[...], wo_v[...]) + out_biases[0, 0:1, :])
@@ -348,7 +348,7 @@
         acc_v[...] = normed + out_biases[0, 1:2, :]
         for name in ("q", "linv", "ctx", "xh1", "inv1", "low"):
             save(name, step)
-        width = 1024
+        width = 1536
         for half in range(2):
             rows = slice(half * ROWS // 2, (half + 1) * ROWS // 2)
             for chunk in range(FF // width):
@@ -945,7 +945,7 @@
             view = s_v.at[step, at(other, RAIL)]
             send(UP, step, view, y_v.at[step, pl.ds(0, RAIL)], recv_sem.at[UP, step], partner)
 
-        for tree in line:
+        for tree in line[::-1]:
             tree.towards(now)
 
         step_up = now - 2
@@ -958,7 +958,7 @@
 
         rail.towards(now)
         rail.away(now)
-        for tree in line:
+        for tree in line[::-1]:
             tree.away(now)
 
         step_down = now - 2 - half_depth - other_distance - 1

time: 279 us -> 277 us (level)
  no operation moved by 1% of the time
where the time goes in v8:
time: 277 us
  Pallas kernels  276 us (100%)
    pallas_call x1, Pallas kernels, reduce_gradients(): pl.pallas_call(functools.partial(reduce_kernel, depth), out_shape=[pltpu....  143 us
    pallas_call x1, Pallas kernels, layers(): pl.pallas_call(functools.partial(layers_kernel, sequences), out_shape=sha...  122 us
    pallas_call x1, Pallas kernels, finish(): pl.pallas_call(finish_kernel, out_shape=shapes, in_specs=[VMEM, VMEM, ANY...  11 us

profile of v8, /device:TPU:0, one launch (start us, length us, event | category | flops | bytes accessed | tf_op | source)
XLA Modules:
  0.0 276.7 jit_solution(7997425277252674513)
XLA Ops:
  0.6 122.1 %layers.1 = (bf16[1024,768]{1,0:T(8,128)(2,1)}, bf16[1024,768]{1,0:T(8,128)(2,1)}, f32[16,768]{1,0:T(8,128)}, bf16[4,12,256,512]{3,2,1,0:T(8,128)(2,1)}, bf16[10...) custom-call(bf16[1024,768]{1,0:T(8,128)(2,1)} %refs_0_.1, ...), custom_call_target="tpu_custom_call" | custom-call | tf_op jit(solution)/shard_map/layers/pallas_call | solution.py:571
  122.8 0.0 copy-start
  122.8 0.0 copy-start.1
  122.8 142.8 %reduce_gradients.1 = (bf16[24,768,384]{2,1,0:T(8,128)(2,1)S(1)}, f32[16,768]{1,0:T(8,128)S(1)}) custom-call(bf16[1024,3072]{1,0:T(8,128)(2,1)} %get-tuple-element.35.refs_0_, bf16[1024,768]{1,0:T(8,128)(2,1)} %get-tuple-element.36.refs_1_, bf16[1024,768]{1,0:T(8,128)(2,1)} %get-tuple-element.37.refs_2_, bf16[1024,3072]{1,0:T(8,128)(2,1)} %get-tuple-element.38.refs_3_, ...), custom_call_target="tpu_custom_call" | custom-call | tf_op jit(solution)/shard_map/reduce_gradients/pallas_call | solution.py:998
  265.6 0.0 copy-done
  265.6 0.0 copy-done.1
  265.6 11.0 %finish.1 = (bf16[1,1024,768]{2,1,0:T(8,128)(2,1)}, bf16[1,1024,768]{2,1,0:T(8,128)(2,1)}, f32[1,3072,768]{2,1,0:T(8,128)}, f32[1,768,3072]{2,1,0:T(8,128)}, f32...) custom-call(bf16[24,768,384]{2,1,0:T(8,128)(2,1)S(1)} %get-tuple-ele, ...), custom_call_target="tpu_custom_call" | custom-call | tf_op jit(solution)/shard_map/finish/pallas_call | solution.py:1073
Async XLA Ops:
  122.8 142.8 %copy-start = (bf16[1024,768]{1,0:T(8,128)(2,1)S(1)}, bf16[1024,768]{1,0:T(8,128)(2,1)}, u32[]{:S(2)}) copy-start(bf16[1024,768]{1,0:T(8,128)(2,1)} %get-tuple-element.46.refs_2_) | copy-start | bytes 4718596
  122.8 142.8 %copy-start.1 = (bf16[1024,768]{1,0:T(8,128)(2,1)S(1)}, bf16[1024,768]{1,0:T(8,128)(2,1)}, u32[]{:S(2)}) copy-start(bf16[1024,768]{1,0:T(8,128)(2,1)} %get-tuple-element.47.refs_3_) | copy-start | bytes 4718596

commit v9 on v8

--- a/solution.py
+++ b/solution.py
@@ -110,14 +110,19 @@
     def part(self, sequence, core):
         return self.array.at[pl.ds(pl.multiple_of(sequence * SEQ + core * ROWS, ROWS), ROWS)]
 
+    def spread_own(self):
+        place = self.place
+        for sequence in range(self.sequences):
+            target = self.steps.at[place.core * self.sequences + sequence]
+            pltpu.make_async_copy(self.part(sequence, place.core), target, self.local.at[sequence]).start()
+
     def spread(self):
         place = self.place
         for sequence in range(self.sequences):
             step = place.core * self.sequences + sequence
-            target = self.steps.at[step]
-            pltpu.make_async_copy(self.part(sequence, place.core), target, self.local.at[sequence]).start()
             remote(
-                self.part(sequence, 1 - place.core), target, self.sent.at[sequence], self.arrived.at[step], place.sibling
+                self.part(sequence, 1 - place.core), self.steps.at[step], self.sent.at[sequence],
+                self.arrived.at[step], place.sibling,
             ).start()
 
     def spread_done(self):
@@ -241,6 +246,18 @@
         begin(wqkv.at[0, :, pl.ds(block * D, D)], wqkv_v.at[:, pl.ds(block * D, D)], w_sem.at[block])
         for block in (1, 2, 0)
     ]
+
+    @pl.when(section == 0)
+    def _():
+        inputs.spread_own()
+
+    @pl.when(section == 1)
+    def _():
+        upstream.spread_own()
+
+    get_wo = begin(wo.at[0], wo_v, w_sem.at[3])
+    get_wu = begin(wu.at[0], wu_v, w_sem.at[4])
+    get_wd = begin(wd.at[0], wd_v, w_sem.at[5])
     position = lax.broadcasted_iota(jnp.int32, (1, SEQ), 1)
     for sequence in range(sequences):
         seg_own[sequence, 0:1, :] = segs[sequence : sequence + 1, :].astype(F32)
@@ -258,9 +275,6 @@
         upstream.spread()
 
     seg_copy.start()
-    get_wo = begin(wo.at[0], wo_v, w_sem.at[3])
-    get_wu = begin(wu.at[0], wu_v, w_sem.at[4])
-    get_wd = begin(wd.at[0], wd_v, w_sem.at[5])
     small_out[...] = jnp.zeros_like(small_out)
 
     def forward_step(step, carry):

time: 277 us -> 277 us (level)
  no operation moved by 1% of the time
where the time goes in v9:
time: 277 us
  Pallas kernels  276 us (100%)
    pallas_call x1, Pallas kernels, reduce_gradients(): pl.pallas_call(functools.partial(reduce_kernel, depth), out_shape=[pltpu....  143 us
    pallas_call x1, Pallas kernels, layers(): pl.pallas_call(functools.partial(layers_kernel, sequences), out_shape=sha...  122 us
    pallas_call x1, Pallas kernels, finish(): pl.pallas_call(finish_kernel, out_shape=shapes, in_specs=[VMEM, VMEM, ANY...  11 us

profile of v9, /device:TPU:0, one launch (start us, length us, event | category | flops | bytes accessed | tf_op | source)
XLA Modules:
  0.0 277.0 jit_solution(11830919468917734911)
XLA Ops:
  0.6 122.0 %layers.1 = (bf16[1024,768]{1,0:T(8,128)(2,1)}, bf16[1024,768]{1,0:T(8,128)(2,1)}, f32[16,768]{1,0:T(8,128)}, bf16[4,12,256,512]{3,2,1,0:T(8,128)(2,1)}, bf16[10...) custom-call(bf16[1024,768]{1,0:T(8,128)(2,1)} %refs_0_.1, ...), custom_call_target="tpu_custom_call" | custom-call | tf_op jit(solution)/shard_map/layers/pallas_call | solution.py:585
  122.6 0.0 copy-start
  122.6 0.0 copy-start.1
  122.6 143.2 %reduce_gradients.1 = (bf16[24,768,384]{2,1,0:T(8,128)(2,1)S(1)}, f32[16,768]{1,0:T(8,128)S(1)}) custom-call(bf16[1024,3072]{1,0:T(8,128)(2,1)} %get-tuple-element.35.refs_0_, bf16[1024,768]{1,0:T(8,128)(2,1)} %get-tuple-element.36.refs_1_, bf16[1024,768]{1,0:T(8,128)(2,1)} %get-tuple-element.37.refs_2_, bf16[1024,3072]{1,0:T(8,128)(2,1)} %get-tuple-element.38.refs_3_, ...), custom_call_target="tpu_custom_call" | custom-call | tf_op jit(solution)/shard_map/reduce_gradients/pallas_call | solution.py:1012
  265.8 0.0 copy-done
  265.8 0.0 copy-done.1
  265.8 11.0 %finish.1 = (bf16[1,1024,768]{2,1,0:T(8,128)(2,1)}, bf16[1,1024,768]{2,1,0:T(8,128)(2,1)}, f32[1,3072,768]{2,1,0:T(8,128)}, f32[1,768,3072]{2,1,0:T(8,128)}, f32...) custom-call(bf16[24,768,384]{2,1,0:T(8,128)(2,1)S(1)} %get-tuple-ele, ...), custom_call_target="tpu_custom_call" | custom-call | tf_op jit(solution)/shard_map/finish/pallas_call | solution.py:1087
Async XLA Ops:
  122.6 143.2 %copy-start = (bf16[1024,768]{1,0:T(8,128)(2,1)S(1)}, bf16[1024,768]{1,0:T(8,128)(2,1)}, u32[]{:S(2)}) copy-start(bf16[1024,768]{1,0:T(8,128)(2,1)} %get-tuple-element.46.refs_2_) | copy-start | bytes 4718596
  122.6 143.2 %copy-start.1 = (bf16[1024,768]{1,0:T(8,128)(2,1)S(1)}, bf16[1024,768]{1,0:T(8,128)(2,1)}, u32[]{:S(2)}) copy-start(bf16[1024,768]{1,0:T(8,128)(2,1)} %get-tuple-element.47.refs_3_) | copy-start | bytes 4718596
